TPU v7x, 32 devices: a whole 2x2x4 slice. The times are simulated.
32 devices in a mesh: depth: 4 (over z), height: 8 (over y, x, core).
Axes of the slice: x: 2, y: 2, z: 4, core: 2. Of those that a mesh axis runs over, the one named last changes fastest.
Arguments:
- grad_out: bfloat16 [4, 16, 64, 1024], P('depth', 'height'), may hold values from -6 to 6
- pre_act: bfloat16 [4, 16, 64, 1024], P('depth', None, None, 'height'), may hold values from -6 to 6
- w_in: bfloat16 [1024, 1024], P('depth'), may hold values from -0.1875 to 0.1875
- w_out: bfloat16 [1024, 1024], P('depth'), may hold values from -0.1875 to 0.1875
- kernel: bfloat16 [27, 32, 1024], P(None, None, 'height'), may hold values from -0.21875 to 0.21875
Outputs:
- grad_in: bfloat16 [4, 16, 64, 1024], P('depth', 'height')
- kernel_grad: float32 [27, 32, 1024], P(None, None, 'height')
All inputs are finite; a program needn't handle non-finite values.
Results may differ from a plain program's by a relative error of at most 0.014.
Values may be sent and summed in bfloat16 or wider, within the bound.
No kernel may reach another device: no remote copies, remote signals or barrier semaphores. Data moves between devices by JAX's collectives and lax.ppermute only.
A program may use at most 64 MiB of HBM per device.

v0:
```python
import jax
import jax.numpy as jnp
from jax import lax
from jax.sharding import PartitionSpec as P


def with_halo(cells, sides, width):
    for axis, dim in sides:
        count = lax.axis_size(axis)
        ends = count - 1
        head = lax.slice_in_dim(cells, 0, width, axis=dim)
        tail = lax.slice_in_dim(cells, cells.shape[dim] - width, cells.shape[dim], axis=dim)
        cells = jnp.concatenate(
            [
                lax.ppermute(tail, axis, [(i, (i + 1) % count) for i in range(ends)]),
                cells,
                lax.ppermute(head, axis, [((i + 1) % count, i) for i in range(ends)]),
            ],
            axis=dim,
        )
    return cells


def shards(grad_out, pre_act, w_in, w_out, kernel):
    product = lax.dot_general(
        grad_out,
        lax.all_gather(w_out, "depth", axis=0, tiled=True),
        (((3,), (1,)), ((), ())),
        preferred_element_type=jnp.float32,
    )
    grad_mid = product.astype(jnp.bfloat16)
    grouped = lax.all_to_all(grad_mid, "height", split_axis=3, concat_axis=1, tiled=True)
    padded = with_halo(grouped, (("depth", 0),), 1)
    padded = jnp.pad(padded, ((0, 0), (1, 1), (1, 1), (0, 0)))
    depth_len, height_len, width_len, chans = pre_act.shape
    group_width = kernel.shape[1]
    groups_here = chans // group_width
    hidden = jnp.maximum(pre_act, jnp.zeros_like(pre_act)).reshape(
        depth_len, height_len, width_len, groups_here, group_width
    )
    kern = kernel.reshape(27, group_width, groups_here, group_width)
    back = jnp.zeros((groups_here, group_width, depth_len, height_len, width_len), jnp.float32)
    grads = []
    for step_d in (-1, 0, 1):
        windows = []
        for step_h in (-1, 0, 1):
            for step_w in (-1, 0, 1):
                windows.append(
                    padded[
                        1 - step_d : 1 - step_d + depth_len,
                        1 - step_h : 1 - step_h + height_len,
                        1 - step_w : 1 - step_w + width_len,
                        :,
                    ]
                )
        stacked = jnp.concatenate(windows, axis=3)
        stacked = stacked.reshape(depth_len, height_len, width_len, 9, groups_here, group_width)
        first = 9 * (step_d + 1)
        kern_plane = kern[first : first + 9]
        back = back + jnp.einsum(
            "dhwkgj,kigj->gidhw", stacked, kern_plane, preferred_element_type=jnp.float32
        )
        grads.append(
            jnp.einsum("dhwkgj,dhwgi->kigj", stacked, hidden, preferred_element_type=jnp.float32)
        )
    back = jnp.transpose(back, (2, 3, 4, 0, 1)).reshape(depth_len, height_len, width_len, chans)
    grad_pre = jnp.where(pre_act > 0, back, jnp.zeros_like(back)).astype(jnp.bfloat16)
    partial_grad = jnp.concatenate(grads, axis=0).reshape(27, group_width, chans)
    total_cells = depth_len * lax.axis_size("depth") * height_len * width_len
    scale = jnp.float32(total_cells) ** (-0.5)
    kernel_grad = lax.psum(partial_grad.astype(jnp.bfloat16), "depth").astype(jnp.float32) * scale
    by_height = lax.all_to_all(grad_pre, "height", split_axis=1, concat_axis=3, tiled=True)
    branch = lax.dot_general(
        by_height,
        lax.all_gather(w_in, "depth", axis=0, tiled=True),
        (((3,), (1,)), ((), ())),
        preferred_element_type=jnp.float32,
    )
    grad_in = (grad_out.astype(jnp.float32) + branch).astype(jnp.bfloat16)
    return (grad_in, kernel_grad)


def solution(mesh):
    in_specs = (
        P("depth", "height", None, None),
        P("depth", None, None, "height"),
        P("depth", None),
        P("depth", None),
        P(None, None, "height"),
    )
    out_specs = (P("depth", "height", None, None), P(None, None, "height"))
    return jax.shard_map(shards, mesh=mesh, in_specs=in_specs, out_specs=out_specs, check_vma=False)
```

profile of v0, /device:TPU:0, one launch (start us, length us, event | category | flops | bytes accessed | tf_op | source)
XLA Modules:
  0.0 219.9 jit_solution(11790411011793790664)
XLA Ops:
  7.2 0.7 all-gather.3.cloned.1.call-update
  7.9 50.3 %all-gather.3.cloned.1.call-done = bf16[1024,1024]{1,0:T(8,128)(2,1)} async-done(((bf16[256,1024]{1,0:T(8,128)(2,1)}), bf16[1024,1024]{1,0:T(8,128)(2,1)}) %all-gather.3.cloned.1.call-update) | async-done | bytes 2097168 | tf_op jit(solution)/shard_map/all_gather | solution.py:27
  58.2 2.5 %fusion.76 = bf16[1,2,64,1024]{3,2,1,0:T(8,128)(2,1)S(1)} fusion(bf16[1024,1024]{1,0:T(8,128)(2,1)} %all-gather.3.cloned.1.call-done, bf16[1,2,64,1024]{3,2,1,0:T(8,128)(2,1)} %param.5), kind=kOutput, calls=%fused_computation.42 | convolution fusion | flops 268566528 | bytes 2621440 | tf_op jit(solution)/shard_map/dot_general | solution.py:25
  60.8 0.4 copy.81
  61.2 0.4 reshape.79
  61.6 10.4 %all_to_all.33 = bf16[8,2,8192]{2,1,0:T(2,128)(2,1)S(1)} all-to-all(bf16[8,2,8192]{2,1,0:T(2,128)(2,1)S(1)} %reshape.79), channel_id=1, replica_groups=mesh['depth'=4,'height'=8] {'height'}, dimensions={0} | all-to-all | bytes 524288 | tf_op jit(solution)/shard_map/all_to_all | solution.py:32
  71.9 0.3 reshape.80
  72.3 0.3 copy.117
  72.6 1.8 collective-permute-start
  74.5 1.3 collective-permute-start.1
  76.0 0.9 slice.115
  76.8 0.9 slice.125
  77.7 1.6 collective-permute-done
  79.3 4.1 %collective-permute-done.1 = bf16[1,16,64,128]{3,2,1,0:T(8,128)(2,1)S(1)} collective-permute-done((bf16[1,16,64,128]{3,2,1,0:T(8,128)(2,1)S(1)}, bf16[1,16,64,128]{3,2,1,0:T(8,128)(2,1)S(1)}, u32[]{:S(2)}, u32[]{:S(2)}) %collective-permute-start.1) | collective-permute-done | bytes 262176 | tf_op jit(solution)/shard_map/ppermute | solution.py:17
  83.5 0.3 select_maximum_fusion
  83.8 0.2 slice_dynamic-update-slice_fusion.7
  84.0 0.4 slice_dynamic-update-slice_fusion.6
  84.4 0.2 slice_dynamic-update-slice_fusion.5
  84.7 0.4 slice_dynamic-update-slice_fusion.4
  85.2 0.2 slice_dynamic-update-slice_fusion.3
  85.5 0.4 slice_dynamic-update-slice_fusion.2
  85.9 0.4 slice_dynamic-update-slice_fusion.1
  86.2 0.2 slice_dynamic-update-slice_fusion
  86.5 1.4 copy-done.2
  87.9 1.5 copy-done.3
  89.3 5.6 %copy.84 = bf16[1,16,64,1152]{2,3,1,0:T(8,128)(2,1)} copy(bf16[1,16,64,1152]{3,2,1,0:T(8,128)(2,1)} %copy-done.3) | data formatting | bytes 4718592 | tf_op jit(solution)/shard_map/concatenate | solution.py:56
  94.9 5.6 %copy.87 = bf16[1,16,64,1152]{2,3,1,0:T(8,128)(2,1)} copy(bf16[1,16,64,1152]{3,2,1,0:T(8,128)(2,1)} %copy-done.2) | data formatting | bytes 4718592 | tf_op jit(solution)/shard_map/concatenate | solution.py:56
  100.5 4.0 %copy.90 = bf16[1,16,64,1152]{2,3,1,0:T(8,128)(2,1)} copy(bf16[1,16,64,1152]{3,2,1,0:T(8,128)(2,1)S(1)} %get-tuple-element.2) | data formatting | bytes 4718592 | tf_op jit(solution)/shard_map/concatenate | solution.py:56
  104.5 3.5 %fusion.19 = f32[4,16,64,32]{2,3,1,0:T(8,128)S(1)} fusion(bf16[16,64,9,4,32]{1,4,3,2,0:T(8,128)(2,1)} %bitcast.101, bf16[9,32,4,32,1]{3,2,1,0,4:T(4,128)(2,1)S(1)} %bitcast.122), kind=kOutput, calls=%fused_computation.23 | convolution fusion | flops 75497472 | bytes 2957312 | tf_op jit(solution)/shard_map/dhwkgj,kigj->gidhw/dot_general | solution.py:60
  108.0 0.3 copy-done
  108.3 1.0 fusion.34
  109.3 1.4 copy-done.1
  110.7 1.0 fusion.31
  111.7 0.2 copy.94
  112.0 0.9 broadcast_maximum_fusion
  112.8 0.3 copy.97
  113.1 5.7 %fusion.67 = bf16[9,32,4,32]{3,1,0,2:T(8,128)(2,1)S(1)} fusion(bf16[16,64,9,4,32]{1,4,3,2,0:T(8,128)(2,1)} %bitcast.102, bf16[16,64,4,32,1]{1,3,2,0,4:T(8,128)(2,1)S(1)} %bitcast.119), kind=kOutput, calls=%fused_computation.39 | convolution fusion | flops 75534336 | bytes 2695168 | tf_op jit(solution)/shard_map/dhwkgj,dhwgi->kigj/dot_general | solution.py:64
  118.8 5.5 %fusion.70 = bf16[9,32,4,32]{3,1,0,2:T(8,128)(2,1)S(1)} fusion(bf16[16,64,9,4,32]{1,4,3,2,0:T(8,128)(2,1)} %bitcast.103, bf16[16,64,4,32,1]{1,3,2,0,4:T(8,128)(2,1)S(1)} %bitcast.120), kind=kOutput, calls=%fused_computation.40 | convolution fusion | flops 75534336 | bytes 2695168 | tf_op jit(solution)/shard_map/dhwkgj,dhwgi->kigj/dot_general | solution.py:64
  124.3 3.2 %fusion.73 = bf16[9,32,4,32]{3,1,0,2:T(8,128)(2,1)S(1)} fusion(bf16[16,64,9,4,32]{1,4,3,2,0:T(8,128)(2,1)S(1)} %bitcast.108, bf16[16,64,4,32,1]{1,3,2,0,4:T(8,128)(2,1)S(1)} %bitcast.121), kind=kOutput, calls=%fused_computation.41 | convolution fusion | flops 75534336 | bytes 2695168 | tf_op jit(solution)/shard_map/dhwkgj,dhwgi->kigj/dot_general | solution.py:64
  127.5 0.2 pad_maximum_fusion
  127.7 0.5 copy.104
  128.2 1.1 convert_element_type.29
  129.4 0.7 all-gather.5.cloned.1.call-update
  130.1 3.4 %all-to-all-start.1 = ((bf16[1,16,64,128]{3,2,0,1:T(8,128)(2,1)}), bf16[1,16,64,128]{3,2,0,1:T(8,128)(2,1)S(1)}, u32[]{:S(2)}, u32[]{:S(2)}) async-start(bf16[1,16,64,128]{3,2,0,1:T(8,128)(2,1)} %get-tuple-element.27), calls=%async_computation.1 | async-start | bytes 524288 | tf_op jit(solution)/shard_map/all_to_all | solution.py:72
  133.5 29.3 %all-reduce.3.cloned.1.call-done = bf16[27,32,128]{2,1,0:T(8,128)(2,1)} async-done(((bf16[27,32,128]{2,1,0:T(8,128)(2,1)}), bf16[27,32,128]{2,1,0:T(8,128)(2,1)}) %all-reduce.3.cloned.1.call-update) | async-done | bytes 221200 | tf_op jit(solution)/shard_map/psum | solution.py:71
  162.8 1.7 convert_multiply_fusion
  164.8 45.4 %all-gather.5.cloned.1.call-done = bf16[1024,1024]{1,0:T(8,128)(2,1)} async-done(((bf16[256,1024]{1,0:T(8,128)(2,1)}), bf16[1024,1024]{1,0:T(8,128)(2,1)}) %all-gather.5.cloned.1.call-update) | async-done | bytes 2097168 | tf_op jit(solution)/shard_map/all_gather | solution.py:75
  210.2 3.1 %fusion.64 = bf16[1,2,64,1024]{3,2,1,0:T(8,128)(2,1)} fusion(bf16[2,64,1024]{2,1,0:T(8,128)(2,1)S(1)} %reshape.63, bf16[1024,1024]{1,0:T(8,128)(2,1)} %all-gather.5.cloned.1.call-done, bf16[1,2,64,1024]{3,2,1,0:T(8,128)(2,1)S(1)} %copy-done.4), kind=kOutput, calls=%fused_computation.38 | convolution fusion | flops 268828672 | bytes 2883584 | tf_op jit(solution)/shard_map/dot_general | solution.py:73
  (32 shorter events, 1.0 us)
Async XLA Ops:
  7.2 51.1 %all-gather.3.cloned.1.call-start = ((), (), s32[]{:S(2)}) async-start(), calls=%async_computation.2 | async-start | bytes 2621440 | tf_op jit(solution)/shard_map/all_gather | solution.py:27
  7.9 154.9 %all-reduce.3.cloned.1.call-start = ((), (), s32[]{:S(2)}) async-start(), calls=%async_computation.4 | async-start | bytes 442368 | tf_op jit(solution)/shard_map/psum | solution.py:71
  60.8 15.0 %copy-start.8 = (bf16[27,32,128]{2,1,0:T(8,128)(2,1)S(1)}, bf16[27,32,128]{2,1,0:T(8,128)(2,1)}, u32[]{:S(2)}) copy-start(bf16[27,32,128]{2,1,0:T(8,128)(2,1)} %param.9) | copy-start | bytes 663556
  72.6 6.7 %collective-permute-start = (bf16[1,16,64,128]{3,2,1,0:T(8,128)(2,1)S(1)}, bf16[1,16,64,128]{3,2,1,0:T(8,128)(2,1)S(1)}, u32[]{:S(2)}, u32[]{:S(2)}) collective-permute-start(bf16[1,16,64,128]{3,2,1,0:T(8,128)(2,1)S(1)} %bitcast.109), channel_id=1, source_target_pairs={{0,8},{8,16},{16,24},{1,9},{9,17},{17,25},{2,10},{10,18},{18,26},{... | collective-permute-start | bytes 786440 | tf_op jit(solution)/shard_map/ppermute | solution.py:15
  74.5 9.0 %collective-permute-start.1 = (bf16[1,16,64,128]{3,2,1,0:T(8,128)(2,1)S(1)}, bf16[1,16,64,128]{3,2,1,0:T(8,128)(2,1)S(1)}, u32[]{:S(2)}, u32[]{:S(2)}) collective-permute-start(bf16[1,16,64,128]{3,2,1,0:T(8,128)(2,1)S(1)} %bitcast.110), channel_id=1, source_target_pairs={{8,0},{16,8},{24,16},{9,1},{17,9},{25,17},{10,2},{18,10},{26,18},{... | collective-permute-start | bytes 786440 | tf_op jit(solution)/shard_map/ppermute | solution.py:17
  86.5 1.4 copy-start.2
  87.9 1.5 copy-start.3
  104.5 3.8 %copy-start = (bf16[1,16,64,1152]{2,3,1,0:T(8,128)(2,1)S(1)}, bf16[1,16,64,1152]{2,3,1,0:T(8,128)(2,1)}, u32[]{:S(2)}) copy-start(bf16[1,16,64,1152]{2,3,1,0:T(8,128)(2,1)} %copy.87) | copy-start | bytes 7077892
  104.5 3.8 %copy-start.5 = (bf16[9,32,4,32]{3,2,1,0:T(4,128)(2,1)S(1)}, bf16[9,32,4,32]{3,2,1,0:T(4,128)(2,1)}, u32[]{:S(2)}) copy-start(bf16[9,32,4,32]{3,2,1,0:T(4,128)(2,1)} %slice.115) | copy-start | bytes 221188
  108.3 2.3 %copy-start.1 = (bf16[1,16,64,1152]{2,3,1,0:T(8,128)(2,1)S(1)}, bf16[1,16,64,1152]{2,3,1,0:T(8,128)(2,1)}, u32[]{:S(2)}) copy-start(bf16[1,16,64,1152]{2,3,1,0:T(8,128)(2,1)} %copy.90) | copy-start | bytes 7077892
  108.3 2.4 %copy-start.6 = (bf16[9,32,4,32]{3,2,1,0:T(4,128)(2,1)S(1)}, bf16[9,32,4,32]{3,2,1,0:T(4,128)(2,1)}, u32[]{:S(2)}) copy-start(bf16[9,32,4,32]{3,2,1,0:T(4,128)(2,1)} %slice.125) | copy-start | bytes 221188
  110.7 1.3 copy-start.7
  112.8 11.5 %slice-start = ((s8[4718592]{0:T(1024)(128)(4,1)}), s8[524288]{0:T(1024)(128)(4,1)S(1)}, s32[]{:S(2)}) async-start(s8[4718592]{0:T(1024)(128)(4,1)} %bitcast.106), calls=%async_computation.5 | async-start | bytes 1048576
  113.1 11.2 %slice-start.1 = ((s8[4718592]{0:T(1024)(128)(4,1)}), s8[4194304]{0:T(1024)(128)(4,1)S(1)}, s32[]{:S(2)}) async-start(s8[4718592]{0:T(1024)(128)(4,1)} %bitcast.106), calls=%async_computation.6 | async-start | bytes 8388608
  128.2 82.1 %copy-start.4 = (bf16[1,2,64,1024]{3,2,1,0:T(8,128)(2,1)S(1)}, bf16[1,2,64,1024]{3,2,1,0:T(8,128)(2,1)}, u32[]{:S(2)}) copy-start(bf16[1,2,64,1024]{3,2,1,0:T(8,128)(2,1)} %param.5) | copy-start | bytes 786436
  129.3 80.9 %all-gather.5.cloned.1.call-start = ((), (), s32[]{:S(2)}) async-start(), calls=%async_computation.3 | async-start | bytes 2621440 | tf_op jit(solution)/shard_map/all_gather | solution.py:75
  130.1 34.5 %all-to-all-start.1 = ((bf16[1,16,64,128]{3,2,0,1:T(8,128)(2,1)}), bf16[1,16,64,128]{3,2,0,1:T(8,128)(2,1)S(1)}, u32[]{:S(2)}, u32[]{:S(2)}) async-start(bf16[1,16,64,128]{3,2,0,1:T(8,128)(2,1)} %get-tuple-element.27), calls=%async_computation.1 | async-start | bytes 524288 | tf_op jit(solution)/shard_map/all_to_all | solution.py:72
Sparse Core Ops, SparseCore 0:
  9.6 48.6 all-gather.2
  129.5 33.2 all-reduce.2
  164.4 45.7 all-gather.4
where the time goes:
time: 221 us; the launch traced here: 220 us
  waiting for transfers between devices  132 us (60%)
  local copies, waits for them, and re-layouts  28.3 us (13%)
  matrix products  25.4 us (11%)
  between operations  14 us (6%)
  blocking collectives  10.4 us (5%)
  starting transfers between devices  6.66 us (3%)
  other arithmetic  3.13 us (1%)
    all_gather x1, waiting for transfers between devices, shards(): lax.all_gather(w_out, 'depth', axis=0, tiled=True)  50.3 us
    all_gather x1, waiting for transfers between devices, shards(): lax.all_gather(w_in, 'depth', axis=0, tiled=True)  45.4 us
    psum x1, waiting for transfers between devices, shards(): lax.psum(partial_grad.astype(jnp.bfloat16), 'depth').astype(jnp.float32)  29.3 us
    concatenate x4, local copies, waits for them, and re-layouts, shards(): stacked = jnp.concatenate(windows, axis=3)  15.4 us
    dot_general x3, matrix products, shards(): jnp.einsum('dhwkgj,dhwgi->kigj', stacked, hidden, preferred_element_type=...  14.3 us
    all_to_all x1, blocking collectives, shards(): lax.all_to_all(grad_mid, 'height', split_axis=3, concat_axis=1, tiled=True)  10.4 us
    unnamed x33, local copies, waits for them, and re-layouts  7.7 us
    dot_general x3, matrix products, shards(): jnp.einsum('dhwkgj,kigj->gidhw', stacked, kern_plane, preferred_element_t...  5.4 us
  transfers between devices with their start and end apart: 6, of which 5 were waited for; matrix products, arithmetic and copies ran while one was open for 2% of the time, Pallas kernels for 0%

commit v1 on v0

v1 whole, which is shorter than its diff:
```python
import functools

import jax
import jax.numpy as jnp
from jax import lax
from jax.experimental import pallas as pl
from jax.experimental.pallas import tpu as pltpu
from jax.sharding import PartitionSpec as P

F32 = jnp.float32
BF16 = jnp.bfloat16
NT = (((1,), (1,)), ((), ()))
TN = (((0,), (0,)), ((), ()))
VMEM_LIMIT = 48 * 1024 * 1024


def vmem():
    return pl.BlockSpec(memory_space=pltpu.VMEM)


def smem():
    return pl.BlockSpec(memory_space=pltpu.SMEM)


def call(body, out_shape, n_in, *, scalars=1, scratch=(), flops=0, nbytes=0):
    return pl.pallas_call(
        body,
        out_shape=out_shape,
        in_specs=[smem()] * scalars + [vmem()] * n_in,
        out_specs=jax.tree.map(lambda _: vmem(), out_shape),
        scratch_shapes=list(scratch),
        compiler_params=pltpu.CompilerParams(vmem_limit_bytes=VMEM_LIMIT),
        cost_estimate=pl.CostEstimate(flops=flops, bytes_accessed=nbytes, transcendentals=0),
    )


def swap(x, axis, mask):
    n = lax.axis_size(axis)
    return lax.ppermute(x, axis, [(i, i ^ mask) for i in range(n)])


def shift(x, axis, step):
    n = lax.axis_size(axis)
    return lax.ppermute(x, axis, [(i, i + step) for i in range(n) if 0 <= i + step < n])


def fetch_rows(w, me_core):
    planes, cols = lax.axis_size("depth"), lax.axis_size("height")
    chips = cols // 2
    part = w.shape[0] // 2
    mine = lax.dynamic_slice_in_dim(w, me_core * part, part, axis=0)
    pairs = []
    for d in range(planes):
        for h in range(cols):
            pairs.append((d * cols + h, (d ^ (h // 2)) * cols + 2 * d + h % 2))
    del chips
    return lax.ppermute(mine, ("depth", "height"), pairs)


def plane_gather(x):
    half = x.shape[0] // 2
    across_x, across_y = swap(x, "height", 2), swap(x, "height", 4)
    core = swap(x, "height", 1)
    diag_a = swap(across_x[:half], "height", 4)
    diag_b = swap(across_y[half:], "height", 2)
    return [
        (0, 0, x),
        (1, 0, core),
        (2, 0, across_x),
        (3, 0, swap(across_x, "height", 1)),
        (4, 0, across_y),
        (5, 0, swap(across_y, "height", 1)),
        (6, 0, diag_a),
        (6, half, diag_b),
        (7, 0, swap(diag_a, "height", 1)),
        (7, half, swap(diag_b, "height", 1)),
    ]


def mid_body(places, rows, h_ref, w_ref, *refs):
    blocks, out = refs[:-1], refs[-1]
    h = h_ref[0]
    w = w_ref[...]
    for (mask, first), block in zip(places, blocks):
        n = block.shape[0]
        at = pl.multiple_of((h ^ mask) * rows + first, 16)
        out[pl.ds(at, n), :] = lax.dot_general(
            block[...], w, NT, preferred_element_type=F32
        ).astype(BF16)


def kgrad_body(wid, group, mid, own, up, down, out, pad):
    cells, chans = mid.shape
    g32 = mid[...].astype(F32)
    col = lax.broadcasted_iota(jnp.int32, (cells, 1), 0) % wid
    left = jnp.where(col < wid - 1, pltpu.roll(g32, cells - 1, 0), 0.0).astype(BF16)
    right = jnp.where(col > 0, pltpu.roll(g32, 1, 0), 0.0).astype(BF16)
    rhs = jnp.concatenate([left, mid[...], right], axis=1)
    zero = jnp.zeros((wid, chans), BF16)
    lane_group = lax.broadcasted_iota(jnp.int32, (group, chans), 1) // group
    for s, plane in enumerate((down, own, up)):
        pad[0:wid, :] = zero
        pad[wid + cells : 2 * wid + cells, :] = zero
        pad[wid : wid + cells, :] = jnp.maximum(plane[...], jnp.zeros((), BF16))
        for t in range(3):
            lhs = pad[t * wid : t * wid + cells, :]
            res = lax.dot_general(lhs, rhs, TN, preferred_element_type=F32)
            for u in range(3):
                tile = res[:, u * chans : (u + 1) * chans]
                acc = jnp.zeros((group, chans), F32)
                for g in range(chans // group):
                    acc = jnp.where(lane_group == g, tile[g * group : (g + 1) * group, :], acc)
                out[9 * s + 3 * t + u] = acc.astype(BF16)


def back_body(wid, mid, lower, upper, pre, weights, out, pad):
    cells, chans = mid.shape
    zero = jnp.zeros((wid, chans), BF16)
    for s, plane in enumerate((upper, mid, lower)):
        pad[s, 0:wid, :] = zero
        pad[s, wid + cells : 2 * wid + cells, :] = zero
        pad[s, wid : wid + cells, :] = plane[...]
    col = lax.broadcasted_iota(jnp.int32, (256, 1), 0) % wid
    for c in range(cells // 256):
        lhs = jnp.concatenate(
            [pad[s, (2 - t) * wid + 256 * c : (2 - t) * wid + 256 * c + 256, :] for s in range(3) for t in range(3)],
            axis=1,
        )
        y = lax.dot_general(lhs, weights[...], NT, preferred_element_type=F32)
        total = y[:, chans : 2 * chans]
        total = total + jnp.where(col < wid - 1, pltpu.roll(y[:, :chans], 255, 0), 0.0)
        total = total + jnp.where(col > 0, pltpu.roll(y[:, 2 * chans :], 1, 0), 0.0)
        rows = slice(256 * c, 256 * c + 256)
        out[rows, :] = jnp.where(pre[rows, :].astype(F32) > 0, total, 0.0).astype(BF16)


def final_body(grad, w, skip, out):
    lhs = jnp.concatenate([grad[i] for i in range(grad.shape[0])], axis=1)
    acc = lax.dot_general(lhs, w[...], NT, preferred_element_type=F32)
    out[...] = (skip[...].astype(F32) + acc).astype(BF16)


def block_weights(kernel, chans, group):
    groups = chans // group
    row_group = jnp.arange(chans)[:, None] // group
    lane_group = jnp.arange(chans)[None, :] // group
    tiled = jnp.tile(kernel, (1, groups, 1))
    tiled = jnp.where(row_group == lane_group, tiled, jnp.zeros_like(tiled))
    tiled = tiled.reshape(9, 3, chans, chans)
    return jnp.transpose(tiled, (1, 2, 0, 3)).reshape(3 * chans, 9 * chans)


def sum_depth(part):
    n = lax.axis_size("depth")
    mask = 1
    while mask < n:
        part = part.astype(BF16)
        part = part.astype(F32) + swap(part, "depth", mask).astype(F32)
        mask *= 2
    return part


def fast(grad_out, pre_act, w_in, w_out, kernel):
    _, rows_here, wid, width = grad_out.shape
    _, height, _, chans = pre_act.shape
    group = kernel.shape[1]
    block = rows_here * wid
    cells = height * wid
    h = lax.axis_index("height")
    h_arr = h.astype(jnp.int32).reshape(1)
    skip = grad_out.reshape(block, width)
    pre = pre_act.reshape(cells, chans)

    gathered = plane_gather(skip)
    w_rows = fetch_rows(w_out, h % 2)
    w_full = lax.all_gather(w_in, "depth", axis=0, tiled=True)
    pre_lower, pre_upper = shift(pre, "depth", 1), shift(pre, "depth", -1)
    weights = block_weights(kernel, chans, group)

    places = [(mask, first) for mask, first, _ in gathered]
    mid = call(
        functools.partial(mid_body, places, block),
        jax.ShapeDtypeStruct((cells, chans), BF16),
        1 + len(places),
        flops=2 * cells * width * chans,
        nbytes=2 * cells * width,
    )(h_arr, w_rows, *[b for _, _, b in gathered])

    lower, upper = shift(mid, "depth", 1), shift(mid, "depth", -1)
    part = call(
        functools.partial(kgrad_body, wid, group),
        jax.ShapeDtypeStruct((27, group, chans), BF16),
        4,
        scalars=0,
        scratch=[pltpu.VMEM((cells + 2 * wid, chans), BF16)],
        flops=2 * 27 * chans * chans * cells,
        nbytes=10 * cells * chans,
    )(mid, pre, pre_upper, pre_lower)
    total_cells = cells * lax.axis_size("depth")
    scale = jnp.float32(total_cells) ** (-0.5)
    kernel_grad = sum_depth(part) * scale

    back = call(
        functools.partial(back_body, wid),
        jax.ShapeDtypeStruct((cells, chans), BF16),
        5,
        scalars=0,
        scratch=[pltpu.VMEM((3, cells + 2 * wid, chans), BF16)],
        flops=2 * 27 * chans * chans * cells,
        nbytes=10 * cells * chans,
    )(mid, lower, upper, pre, weights)

    parts = lax.all_to_all(back.reshape(cells // block, block, chans), "height", 0, 0)
    grad_in = call(
        final_body,
        jax.ShapeDtypeStruct((block, width), BF16),
        3,
        scalars=0,
        flops=2 * block * width * width,
        nbytes=2 * width * width,
    )(parts, w_full, skip)
    return grad_in.reshape(grad_out.shape), kernel_grad


def with_halo(cells, axis, dim, width):
    head = lax.slice_in_dim(cells, 0, width, axis=dim)
    tail = lax.slice_in_dim(cells, cells.shape[dim] - width, cells.shape[dim], axis=dim)
    return jnp.concatenate([shift(tail, axis, 1), cells, shift(head, axis, -1)], axis=dim)


def general(grad_out, pre_act, w_in, w_out, kernel):
    product = lax.dot_general(
        grad_out,
        lax.all_gather(w_out, "depth", axis=0, tiled=True),
        (((3,), (1,)), ((), ())),
        preferred_element_type=F32,
    )
    grad_mid = product.astype(BF16)
    grouped = lax.all_to_all(grad_mid, "height", split_axis=3, concat_axis=1, tiled=True)
    padded = with_halo(grouped, "depth", 0, 1)
    padded = jnp.pad(padded, ((0, 0), (1, 1), (1, 1), (0, 0)))
    depth_len, height_len, width_len, chans = pre_act.shape
    group = kernel.shape[1]
    groups = chans // group
    hidden = jnp.maximum(pre_act, jnp.zeros_like(pre_act)).reshape(
        depth_len, height_len, width_len, groups, group
    )
    kern = kernel.reshape(27, group, groups, group)
    back = jnp.zeros((groups, group, depth_len, height_len, width_len), F32)
    grads = []
    for s in range(3):
        windows = [
            padded[2 - s : 2 - s + depth_len, 2 - t : 2 - t + height_len, 2 - u : 2 - u + width_len, :]
            for t in range(3)
            for u in range(3)
        ]
        stacked = jnp.concatenate(windows, axis=3)
        stacked = stacked.reshape(depth_len, height_len, width_len, 9, groups, group)
        back = back + jnp.einsum(
            "dhwkgj,kigj->gidhw", stacked, kern[9 * s : 9 * s + 9], preferred_element_type=F32
        )
        grads.append(jnp.einsum("dhwkgj,dhwgi->kigj", stacked, hidden, preferred_element_type=F32))
    back = jnp.transpose(back, (2, 3, 4, 0, 1)).reshape(depth_len, height_len, width_len, chans)
    grad_pre = jnp.where(pre_act > 0, back, jnp.zeros_like(back)).astype(BF16)
    part = jnp.concatenate(grads, axis=0).reshape(27, group, chans)
    total_cells = depth_len * lax.axis_size("depth") * height_len * width_len
    scale = jnp.float32(total_cells) ** (-0.5)
    kernel_grad = lax.psum(part.astype(BF16), "depth").astype(F32) * scale
    by_height = lax.all_to_all(grad_pre, "height", split_axis=1, concat_axis=3, tiled=True)
    branch = lax.dot_general(
        by_height,
        lax.all_gather(w_in, "depth", axis=0, tiled=True),
        (((3,), (1,)), ((), ())),
        preferred_element_type=F32,
    )
    return (grad_out.astype(F32) + branch).astype(BF16), kernel_grad


def solution(mesh):
    planes, cols = mesh.shape["depth"], mesh.shape["height"]

    def shards(grad_out, pre_act, w_in, w_out, kernel):
        whole_lanes = pre_act.shape[3] == 128 and pre_act.shape[0] == 1 and grad_out.shape[0] == 1
        if cols == 8 and planes == 4 and whole_lanes:
            return fast(grad_out, pre_act, w_in, w_out, kernel)
        return general(grad_out, pre_act, w_in, w_out, kernel)

    in_specs = (
        P("depth", "height", None, None),
        P("depth", None, None, "height"),
        P("depth", None),
        P("depth", None),
        P(None, None, "height"),
    )
    out_specs = (P("depth", "height", None, None), P(None, None, "height"))
    return jax.shard_map(shards, mesh=mesh, in_specs=in_specs, out_specs=out_specs, check_vma=False)
```

time: 221 us -> 107 us (0.48)
  the two profiles are of different devices: /device:TPU:0 before, /device:TPU:8 now
where the time goes in v1:
time: 107 us
  starting transfers between devices  44.8 us (42%)
  waiting for transfers between devices  37.2 us (35%)
  between operations  14.2 us (13%)
  Pallas kernels  6.14 us (6%)
  local copies, waits for them, and re-layouts  3.65 us (3%)
    ppermute x4, waiting for transfers between devices, shift(): lax.ppermute(x, axis, [(i, i + step) for i in range(n) if 0 <= i + step <...  17.5 us
    ppermute x4, starting transfers between devices, shift(): lax.ppermute(x, axis, [(i, i + step) for i in range(n) if 0 <= i + step <...  15.7 us
    all_to_all x1, starting transfers between devices, fast(): lax.all_to_all(back.reshape(cells // block, block, chans), 'height', 0, 0)  15.5 us
    ppermute x11, waiting for transfers between devices, swap(): return lax.ppermute(x, axis, [(i, i ^ mask) for i in range(n)])  13 us
    ppermute x11, starting transfers between devices, swap(): return lax.ppermute(x, axis, [(i, i ^ mask) for i in range(n)])  11.1 us
    all_to_all x1, waiting for transfers between devices, fast(): lax.all_to_all(back.reshape(cells // block, block, chans), 'height', 0, 0)  6.09 us
    unnamed x13, local copies, waits for them, and re-layouts  2.82 us
    ppermute x1, starting transfers between devices, fetch_rows(): return lax.ppermute(mine, ('depth', 'height'), pairs)  2.44 us
  transfers between devices with their start and end apart: 18, of which 10 were waited for; matrix products, arithmetic and copies ran while one was open for 2% of the time, Pallas kernels for 4%

profile of v1, /device:TPU:8, one launch (start us, length us, event | category | flops | bytes accessed | tf_op | source)
XLA Modules:
  0.0 107.1 jit_solution(15934634726669791809)
XLA Ops:
  7.2 0.0 copy-start
  7.2 0.0 copy-start.4
  7.2 0.0 all-gather.2.cloned.1.call-start
  7.2 0.7 all-gather.2.cloned.1.call-update
  7.9 1.6 %collective-permute-start.2 = (bf16[128,1024]{1,0:T(8,128)(2,1)}, bf16[128,1024]{1,0:T(8,128)(2,1)S(1)}, u32[]{:S(2)}, u32[]{:S(2)}) collective-permute-start(bf16[128,1024]{1,0:T(8,128)(2,1)} %bitcast.13), channel_id=1, source_target_pairs={{0,2},{1,3},{2,0},{3,1},{4,6},{5,7},{6,4},{7,5},{8,10},{9,11},{10,... | collective-permute-start | bytes 786440 | tf_op jit(solution)/shard_map/ppermute | solution.py:39
  9.5 1.5 %collective-permute-start.4 = (bf16[128,1024]{1,0:T(8,128)(2,1)}, bf16[128,1024]{1,0:T(8,128)(2,1)S(1)}, u32[]{:S(2)}, u32[]{:S(2)}) collective-permute-start(bf16[128,1024]{1,0:T(8,128)(2,1)} %bitcast.14), channel_id=1, source_target_pairs={{0,4},{1,5},{2,6},{3,7},{4,0},{5,1},{6,2},{7,3},{8,12},{9,13},{10,... | collective-permute-start | bytes 786440 | tf_op jit(solution)/shard_map/ppermute | solution.py:39
  11.0 2.4 %collective-permute-start = (bf16[128,1024]{1,0:T(8,128)(2,1)S(1)}, bf16[128,1024]{1,0:T(8,128)(2,1)S(1)}, u32[]{:S(2)}, u32[]{:S(2)}) collective-permute-start(bf16[128,1024]{1,0:T(8,128)(2,1)S(1)} %constant_dynamic-slice_fusion), channel_id=1, source_target_pairs={{0,0},{1,1},{2,8},{3,9},{4,16},{5,17},{6,24},{7,25},{8,10},{9,11},... | collective-permute-start | bytes 786440 | tf_op jit(solution)/shard_map/ppermute | solution.py:57
  13.5 0.1 collective-permute-start.1
  13.6 8.3 %collective-permute-done.2.refs_2_ = bf16[128,1024]{1,0:T(8,128)(2,1)S(1)} collective-permute-done((bf16[128,1024]{1,0:T(8,128)(2,1)}, bf16[128,1024]{1,0:T(8,128)(2,1)S(1)}, u32[]{:S(2)}, u32[]{:S(2)}) %collective-permute-start.2) | collective-permute-done | bytes 262176 | tf_op jit(solution)/shard_map/ppermute | solution.py:39
  21.9 0.0 collective-permute-start.3
  21.9 0.7 collective-permute-start.6
  22.6 0.0 collective-permute-done.4.refs_4_
  22.6 2.4 %collective-permute-start.7 = (bf16[64,1024]{1,0:T(8,128)(2,1)S(1)}, bf16[64,1024]{1,0:T(8,128)(2,1)S(1)}, u32[]{:S(2)}, u32[]{:S(2)}) collective-permute-start(bf16[64,1024]{1,0:T(8,128)(2,1)S(1)} %slice.9), channel_id=1, source_target_pairs={{0,2},{1,3},{2,0},{3,1},{4,6},{5,7},{6,4},{7,5},{8,10},{9,11},{10,... | collective-permute-start | bytes 393224 | tf_op jit(solution)/shard_map/ppermute | solution.py:39
  25.1 1.9 %collective-permute-start.12 = (bf16[1024,128]{1,0:T(8,128)(2,1)}, bf16[1024,128]{1,0:T(8,128)(2,1)S(1)}, u32[]{:S(2)}, u32[]{:S(2)}) collective-permute-start(bf16[1024,128]{1,0:T(8,128)(2,1)} %bitcast.19), channel_id=1, source_target_pairs={{8,0},{16,8},{24,16},{9,1},{17,9},{25,17},{10,2},{18,10},{26,18},{... | collective-permute-start | bytes 786440 | tf_op jit(solution)/shard_map/ppermute | solution.py:44
  27.0 0.9 collective-permute-done.6.refs_6_
  27.9 3.1 %collective-permute-start.13 = (bf16[1024,128]{1,0:T(8,128)(2,1)}, bf16[1024,128]{1,0:T(8,128)(2,1)S(1)}, u32[]{:S(2)}, u32[]{:S(2)}) collective-permute-start(bf16[1024,128]{1,0:T(8,128)(2,1)} %bitcast.20), channel_id=1, source_target_pairs={{0,8},{8,16},{16,24},{1,9},{9,17},{17,25},{2,10},{10,18},{18,26},{... | collective-permute-start | bytes 786440 | tf_op jit(solution)/shard_map/ppermute | solution.py:44
  30.9 0.0 collective-permute-done.7.refs_7_
  30.9 0.1 collective-permute-start.8
  31.0 0.5 collective-permute-start.9
  31.5 0.0 collective-permute-done.5.refs_5_
  31.5 0.8 collective-permute-done.8.refs_8_
  32.4 0.2 collective-permute-done.9.refs_9_
  32.5 0.9 copy-done.2
  33.5 0.9 shard_map.68.mid
  34.4 0.0 copy-start.5
  34.4 12.9 %collective-permute-done.12.up = bf16[1024,128]{1,0:T(8,128)(2,1)S(1)} collective-permute-done((bf16[1024,128]{1,0:T(8,128)(2,1)}, bf16[1024,128]{1,0:T(8,128)(2,1)S(1)}, u32[]{:S(2)}, u32[]{:S(2)}) %collective-permute-start.12) | collective-permute-done | bytes 262176 | tf_op jit(solution)/shard_map/ppermute | solution.py:44
  47.3 0.4 collective-permute-done.13.down
  47.6 1.5 %shard_map.71 = bf16[27,32,128]{2,1,0:T(8,128)(2,1)S(1)} custom-call(bf16[1024,128]{1,0:T(8,128)(2,1)S(1)} %shard_map.68.mid, bf16[1024,128]{1,0:T(8,128)(2,1)S(1)} %bitcast.21, bf16[1024,128]{1,0:T(8,128)(2,1)S(1)} %collective-permute-done.12.up, bf16[1024,128]{1,0:T(8,128)(2,1)S(1)} %collective-permute-done.13.down), custom_call_target="tpu_custom_call" | custom-call | flops 905969664 | bytes 1310720 | tf_op jit(solution)/shard_map/pallas_call | solution.py:190
  49.1 0.8 collective-permute-start.14
  49.9 0.1 broadcast_compare_fusion
  50.0 8.8 %collective-permute-start.10 = (bf16[1024,128]{1,0:T(8,128)(2,1)S(1)}, bf16[1024,128]{1,0:T(8,128)(2,1)S(1)}, u32[]{:S(2)}, u32[]{:S(2)}) collective-permute-start(bf16[1024,128]{1,0:T(8,128)(2,1)S(1)} %shard_map.68.mid), channel_id=1, source_target_pairs={{0,8},{8,16},{16,24},{1,9},{9,17},{17,25},{2,10},{10,18},{18,26},{... | collective-permute-start | bytes 786440 | tf_op jit(solution)/shard_map/ppermute | solution.py:44
  58.8 1.9 %collective-permute-start.11 = (bf16[1024,128]{1,0:T(8,128)(2,1)S(1)}, bf16[1024,128]{1,0:T(8,128)(2,1)S(1)}, u32[]{:S(2)}, u32[]{:S(2)}) collective-permute-start(bf16[1024,128]{1,0:T(8,128)(2,1)S(1)} %shard_map.68.mid), channel_id=1, source_target_pairs={{8,0},{16,8},{24,16},{9,1},{17,9},{25,17},{10,2},{18,10},{26,18},{... | collective-permute-start | bytes 786440 | tf_op jit(solution)/shard_map/ppermute | solution.py:44
  60.8 2.8 %collective-permute-done.14 = bf16[27,32,128]{2,1,0:T(8,128)(2,1)S(1)} collective-permute-done((bf16[27,32,128]{2,1,0:T(8,128)(2,1)S(1)}, bf16[27,32,128]{2,1,0:T(8,128)(2,1)S(1)}, u32[]{:S(2)}, u32[]{:S(2)}) %collective-permute-start.14) | collective-permute-done | bytes 221216 | tf_op jit(solution)/shard_map/ppermute | solution.py:39
  63.5 0.1 add_convert_fusion
  63.6 3.4 %collective-permute-start.15 = (bf16[27,32,128]{2,1,0:T(8,128)(2,1)S(1)}, bf16[27,32,128]{2,1,0:T(8,128)(2,1)S(1)}, u32[]{:S(2)}, u32[]{:S(2)}) collective-permute-start(bf16[27,32,128]{2,1,0:T(8,128)(2,1)S(1)} %add_convert_fusion), channel_id=1, source_target_pairs={{0,16},{8,24},{16,0},{24,8},{1,17},{9,25},{17,1},{25,9},{2,18},{10... | collective-permute-start | bytes 663560 | tf_op jit(solution)/shard_map/ppermute | solution.py:39
  67.0 0.1 tile.4
  67.2 0.1 select_bitcast_fusion
  67.2 0.7 copy.9
  67.9 0.3 copy.13
  68.2 2.2 %collective-permute-done.10.lower = bf16[1024,128]{1,0:T(8,128)(2,1)S(1)} collective-permute-done((bf16[1024,128]{1,0:T(8,128)(2,1)S(1)}, bf16[1024,128]{1,0:T(8,128)(2,1)S(1)}, u32[]{:S(2)}, u32[]{:S(2)}) %collective-permute-start.10) | collective-permute-done | bytes 262176 | tf_op jit(solution)/shard_map/ppermute | solution.py:44
  70.3 2.1 %collective-permute-done.11.upper = bf16[1024,128]{1,0:T(8,128)(2,1)S(1)} collective-permute-done((bf16[1024,128]{1,0:T(8,128)(2,1)S(1)}, bf16[1024,128]{1,0:T(8,128)(2,1)S(1)}, u32[]{:S(2)}, u32[]{:S(2)}) %collective-permute-start.11) | collective-permute-done | bytes 262176 | tf_op jit(solution)/shard_map/ppermute | solution.py:44
  72.4 2.2 %shard_map.69 = bf16[1024,128]{1,0:T(8,128)(2,1)} custom-call(bf16[1024,128]{1,0:T(8,128)(2,1)S(1)} %shard_map.68.mid, bf16[1024,128]{1,0:T(8,128)(2,1)S(1)} %collective-permute-done.10.lower, bf16[1024,128]{1,0:T(8,128)(2,1)S(1)} %collective-permute-done.11.upper, bf16[1024,128]{1,0:T(8,128)(2,1)S(1)} %bitcast.22, bf16[384,1152]{1,0:T(8,128)(2,1)S(1)} %bitcast.18), custom_call_target="tpu_custom_call" | custom-call | flops 905969664 | bytes 1310720 | tf_op jit(solution)/shard_map/pallas_call | solution.py:203
  74.7 15.5 %all-to-all-start = ((bf16[8,128,128]{2,1,0:T(8,128)(2,1)}), bf16[8,128,128]{2,1,0:T(8,128)(2,1)S(1)}, u32[]{:S(2)}, u32[]{:S(2)}) async-start(bf16[8,128,128]{2,1,0:T(8,128)(2,1)} %bitcast.5), calls=%async_computation | async-start | bytes 524288 | tf_op jit(solution)/shard_map/all_to_all | solution.py:213
  90.2 0.0 collective-permute-done.15
  90.2 0.8 add_multiply_fusion
  91.0 6.1 %all-to-all-done.grad = bf16[8,128,128]{2,1,0:T(8,128)(2,1)S(1)} async-done(((bf16[8,128,128]{2,1,0:T(8,128)(2,1)}), bf16[8,128,128]{2,1,0:T(8,128)(2,1)S(1)}, u32[]{:S(2)}, u32[]{:S(2)}) %all-to-all-start) | async-done | bytes 262176 | tf_op jit(solution)/shard_map/all_to_all | solution.py:213
  97.1 1.6 %copy-done.1 = bf16[1024,1024]{1,0:T(8,128)(2,1)S(1)} copy-done((bf16[1024,1024]{1,0:T(8,128)(2,1)S(1)}, bf16[1024,1024]{1,0:T(8,128)(2,1)}, u32[]{:S(2)}) %copy-start.1) | copy-done | bytes 2097176
  98.7 1.5 %shard_map.70 = bf16[128,1024]{1,0:T(8,128)(2,1)} custom-call(bf16[8,128,128]{2,1,0:T(8,128)(2,1)S(1)} %all-to-all-done.grad, bf16[1024,1024]{1,0:T(8,128)(2,1)S(1)} %copy-done.1, bf16[128,1024]{1,0:T(8,128)(2,1)S(1)} %bitcast.17), custom_call_target="tpu_custom_call" | custom-call | flops 268435456 | bytes 2097152 | tf_op jit(solution)/shard_map/pallas_call | solution.py:214
  (16 shorter events, 0.1 us)
Async XLA Ops:
  7.2 3.8 %copy-start = (bf16[256,1024]{1,0:T(8,128)(2,1)S(1)}, bf16[256,1024]{1,0:T(8,128)(2,1)}, u32[]{:S(2)}) copy-start(bf16[256,1024]{1,0:T(8,128)(2,1)} %param.8) | copy-start | bytes 1572868
  7.2 40.4 %copy-start.4 = (bf16[1,16,64,128]{3,2,1,0:T(8,128)(2,1)S(1)}, bf16[1,16,64,128]{3,2,1,0:T(8,128)(2,1)}, u32[]{:S(2)}) copy-start(bf16[1,16,64,128]{3,2,1,0:T(8,128)(2,1)} %param.6) | copy-start | bytes 786436
  7.2 89.9 %all-gather.2.cloned.1.call-start = ((), (), s32[]{:S(2)}) async-start(), calls=%async_computation.1 | async-start | bytes 2621440 | tf_op jit(solution)/shard_map/all_gather | solution.py:176
  7.9 13.9 %collective-permute-start.2 = (bf16[128,1024]{1,0:T(8,128)(2,1)}, bf16[128,1024]{1,0:T(8,128)(2,1)S(1)}, u32[]{:S(2)}, u32[]{:S(2)}) collective-permute-start(bf16[128,1024]{1,0:T(8,128)(2,1)} %bitcast.13), channel_id=1, source_target_pairs={{0,2},{1,3},{2,0},{3,1},{4,6},{5,7},{6,4},{7,5},{8,10},{9,11},{10,... | collective-permute-start | bytes 786440 | tf_op jit(solution)/shard_map/ppermute | solution.py:39
  9.5 13.1 %collective-permute-start.4 = (bf16[128,1024]{1,0:T(8,128)(2,1)}, bf16[128,1024]{1,0:T(8,128)(2,1)S(1)}, u32[]{:S(2)}, u32[]{:S(2)}) collective-permute-start(bf16[128,1024]{1,0:T(8,128)(2,1)} %bitcast.14), channel_id=1, source_target_pairs={{0,4},{1,5},{2,6},{3,7},{4,0},{5,1},{6,2},{7,3},{8,12},{9,13},{10,... | collective-permute-start | bytes 786440 | tf_op jit(solution)/shard_map/ppermute | solution.py:39
  11.0 14.0 %collective-permute-start = (bf16[128,1024]{1,0:T(8,128)(2,1)S(1)}, bf16[128,1024]{1,0:T(8,128)(2,1)S(1)}, u32[]{:S(2)}, u32[]{:S(2)}) collective-permute-start(bf16[128,1024]{1,0:T(8,128)(2,1)S(1)} %constant_dynamic-slice_fusion), channel_id=1, source_target_pairs={{0,0},{1,1},{2,8},{3,9},{4,16},{5,17},{6,24},{7,25},{8,10},{9,11},... | collective-permute-start | bytes 786440 | tf_op jit(solution)/shard_map/ppermute | solution.py:57
  13.5 11.6 %collective-permute-start.1 = (bf16[128,1024]{1,0:T(8,128)(2,1)}, bf16[128,1024]{1,0:T(8,128)(2,1)S(1)}, u32[]{:S(2)}, u32[]{:S(2)}) collective-permute-start(bf16[128,1024]{1,0:T(8,128)(2,1)} %bitcast.15), channel_id=1, source_target_pairs={{0,1},{1,0},{2,3},{3,2},{4,5},{5,4},{6,7},{7,6},{8,9},{9,8},{10,11... | collective-permute-start | bytes 786440 | tf_op jit(solution)/shard_map/ppermute | solution.py:39
  21.9 9.2 %collective-permute-start.3 = (bf16[128,1024]{1,0:T(8,128)(2,1)S(1)}, bf16[128,1024]{1,0:T(8,128)(2,1)S(1)}, u32[]{:S(2)}, u32[]{:S(2)}) collective-permute-start(bf16[128,1024]{1,0:T(8,128)(2,1)S(1)} %collective-permute-done.2.refs_2_), channel_id=1, source_target_pairs={{0,1},{1,0},{2,3},{3,2},{4,5},{5,4},{6,7},{7,6},{8,9},{9,8},{10,11... | collective-permute-start | bytes 786440 | tf_op jit(solution)/shard_map/ppermute | solution.py:39
  21.9 6.0 %collective-permute-start.6 = (bf16[64,1024]{1,0:T(8,128)(2,1)S(1)}, bf16[64,1024]{1,0:T(8,128)(2,1)S(1)}, u32[]{:S(2)}, u32[]{:S(2)}) collective-permute-start(bf16[64,1024]{1,0:T(8,128)(2,1)S(1)} %slice.8), channel_id=1, source_target_pairs={{0,4},{1,5},{2,6},{3,7},{4,0},{5,1},{6,2},{7,3},{8,12},{9,13},{10,... | collective-permute-start | bytes 393224 | tf_op jit(solution)/shard_map/ppermute | solution.py:39
  22.6 8.3 %collective-permute-start.7 = (bf16[64,1024]{1,0:T(8,128)(2,1)S(1)}, bf16[64,1024]{1,0:T(8,128)(2,1)S(1)}, u32[]{:S(2)}, u32[]{:S(2)}) collective-permute-start(bf16[64,1024]{1,0:T(8,128)(2,1)S(1)} %slice.9), channel_id=1, source_target_pairs={{0,2},{1,3},{2,0},{3,1},{4,6},{5,7},{6,4},{7,5},{8,10},{9,11},{10,... | collective-permute-start | bytes 393224 | tf_op jit(solution)/shard_map/ppermute | solution.py:39
  25.0 6.5 %collective-permute-start.5 = (bf16[128,1024]{1,0:T(8,128)(2,1)S(1)}, bf16[128,1024]{1,0:T(8,128)(2,1)S(1)}, u32[]{:S(2)}, u32[]{:S(2)}) collective-permute-start(bf16[128,1024]{1,0:T(8,128)(2,1)S(1)} %collective-permute-done.4.refs_4_), channel_id=1, source_target_pairs={{0,1},{1,0},{2,3},{3,2},{4,5},{5,4},{6,7},{7,6},{8,9},{9,8},{10,11... | collective-permute-start | bytes 786440 | tf_op jit(solution)/shard_map/ppermute | solution.py:39
  25.1 22.2 %collective-permute-start.12 = (bf16[1024,128]{1,0:T(8,128)(2,1)}, bf16[1024,128]{1,0:T(8,128)(2,1)S(1)}, u32[]{:S(2)}, u32[]{:S(2)}) collective-permute-start(bf16[1024,128]{1,0:T(8,128)(2,1)} %bitcast.19), channel_id=1, source_target_pairs={{8,0},{16,8},{24,16},{9,1},{17,9},{25,17},{10,2},{18,10},{26,18},{... | collective-permute-start | bytes 786440 | tf_op jit(solution)/shard_map/ppermute | solution.py:44
  27.9 19.8 %collective-permute-start.13 = (bf16[1024,128]{1,0:T(8,128)(2,1)}, bf16[1024,128]{1,0:T(8,128)(2,1)S(1)}, u32[]{:S(2)}, u32[]{:S(2)}) collective-permute-start(bf16[1024,128]{1,0:T(8,128)(2,1)} %bitcast.20), channel_id=1, source_target_pairs={{0,8},{8,16},{16,24},{1,9},{9,17},{17,25},{2,10},{10,18},{18,26},{... | collective-permute-start | bytes 786440 | tf_op jit(solution)/shard_map/ppermute | solution.py:44
  30.9 1.4 %collective-permute-start.8 = (bf16[64,1024]{1,0:T(8,128)(2,1)S(1)}, bf16[64,1024]{1,0:T(8,128)(2,1)S(1)}, u32[]{:S(2)}, u32[]{:S(2)}) collective-permute-start(bf16[64,1024]{1,0:T(8,128)(2,1)S(1)} %collective-permute-done.6.refs_6_), channel_id=1, source_target_pairs={{0,1},{1,0},{2,3},{3,2},{4,5},{5,4},{6,7},{7,6},{8,9},{9,8},{10,11... | collective-permute-start | bytes 393224 | tf_op jit(solution)/shard_map/ppermute | solution.py:39
  31.0 1.5 %collective-permute-start.9 = (bf16[64,1024]{1,0:T(8,128)(2,1)S(1)}, bf16[64,1024]{1,0:T(8,128)(2,1)S(1)}, u32[]{:S(2)}, u32[]{:S(2)}) collective-permute-start(bf16[64,1024]{1,0:T(8,128)(2,1)S(1)} %collective-permute-done.7.refs_7_), channel_id=1, source_target_pairs={{0,1},{1,0},{2,3},{3,2},{4,5},{5,4},{6,7},{7,6},{8,9},{9,8},{10,11... | collective-permute-start | bytes 393224 | tf_op jit(solution)/shard_map/ppermute | solution.py:39
  32.5 1.0 copy-start.2
  34.4 32.6 %copy-start.5 = (bf16[27,32,128]{2,1,0:T(8,128)(2,1)S(1)}, bf16[27,32,128]{2,1,0:T(8,128)(2,1)}, u32[]{:S(2)}) copy-start(bf16[27,32,128]{2,1,0:T(8,128)(2,1)} %param.9) | copy-start | bytes 663556
  49.1 14.4 %collective-permute-start.14 = (bf16[27,32,128]{2,1,0:T(8,128)(2,1)S(1)}, bf16[27,32,128]{2,1,0:T(8,128)(2,1)S(1)}, u32[]{:S(2)}, u32[]{:S(2)}) collective-permute-start(bf16[27,32,128]{2,1,0:T(8,128)(2,1)S(1)} %shard_map.71), channel_id=1, source_target_pairs={{0,8},{8,0},{16,24},{24,16},{1,9},{9,1},{17,25},{25,17},{2,10},{10... | collective-permute-start | bytes 663560 | tf_op jit(solution)/shard_map/ppermute | solution.py:39
  50.0 20.3 %collective-permute-start.10 = (bf16[1024,128]{1,0:T(8,128)(2,1)S(1)}, bf16[1024,128]{1,0:T(8,128)(2,1)S(1)}, u32[]{:S(2)}, u32[]{:S(2)}) collective-permute-start(bf16[1024,128]{1,0:T(8,128)(2,1)S(1)} %shard_map.68.mid), channel_id=1, source_target_pairs={{0,8},{8,16},{16,24},{1,9},{9,17},{17,25},{2,10},{10,18},{18,26},{... | collective-permute-start | bytes 786440 | tf_op jit(solution)/shard_map/ppermute | solution.py:44
  58.8 13.6 %collective-permute-start.11 = (bf16[1024,128]{1,0:T(8,128)(2,1)S(1)}, bf16[1024,128]{1,0:T(8,128)(2,1)S(1)}, u32[]{:S(2)}, u32[]{:S(2)}) collective-permute-start(bf16[1024,128]{1,0:T(8,128)(2,1)S(1)} %shard_map.68.mid), channel_id=1, source_target_pairs={{8,0},{16,8},{24,16},{9,1},{17,9},{25,17},{10,2},{18,10},{26,18},{... | collective-permute-start | bytes 786440 | tf_op jit(solution)/shard_map/ppermute | solution.py:44
  63.6 26.6 %collective-permute-start.15 = (bf16[27,32,128]{2,1,0:T(8,128)(2,1)S(1)}, bf16[27,32,128]{2,1,0:T(8,128)(2,1)S(1)}, u32[]{:S(2)}, u32[]{:S(2)}) collective-permute-start(bf16[27,32,128]{2,1,0:T(8,128)(2,1)S(1)} %add_convert_fusion), channel_id=1, source_target_pairs={{0,16},{8,24},{16,0},{24,8},{1,17},{9,25},{17,1},{25,9},{2,18},{10... | collective-permute-start | bytes 663560 | tf_op jit(solution)/shard_map/ppermute | solution.py:39
  72.4 24.7 %copy-start.3 = (bf16[1,2,64,1024]{3,2,1,0:T(8,128)(2,1)S(1)}, bf16[1,2,64,1024]{3,2,1,0:T(8,128)(2,1)}, u32[]{:S(2)}) copy-start(bf16[1,2,64,1024]{3,2,1,0:T(8,128)(2,1)} %param.5) | copy-start | bytes 786436
  74.7 22.4 %all-to-all-start = ((bf16[8,128,128]{2,1,0:T(8,128)(2,1)}), bf16[8,128,128]{2,1,0:T(8,128)(2,1)S(1)}, u32[]{:S(2)}, u32[]{:S(2)}) async-start(bf16[8,128,128]{2,1,0:T(8,128)(2,1)} %bitcast.5), calls=%async_computation | async-start | bytes 524288 | tf_op jit(solution)/shard_map/all_to_all | solution.py:213
  97.1 1.6 %copy-start.1 = (bf16[1024,1024]{1,0:T(8,128)(2,1)S(1)}, bf16[1024,1024]{1,0:T(8,128)(2,1)}, u32[]{:S(2)}) copy-start(bf16[1024,1024]{1,0:T(8,128)(2,1)} %all-gather.2.cloned.1.call-done.w) | copy-start | bytes 6291460
Sparse Core Ops, SparseCore 0:
  9.6 58.0 all-gather.1

commit v2 on v1

--- a/solution.py
+++ b/solution.py
@@ -44,43 +44,60 @@
     return lax.ppermute(x, axis, [(i, i + step) for i in range(n) if 0 <= i + step < n])
 
 
-def fetch_rows(w, me_core):
+def order(x, *before):
+    return lax.optimization_barrier((x,) + before)[0]
+
+
+CARRIER = {
+    (0, 1): 0, (0, 2): 1, (0, 3): 2,
+    (1, 0): 1, (1, 2): 3, (1, 3): 0,
+    (2, 0): 0, (2, 1): 2, (2, 3): 3,
+    (3, 0): 3, (3, 1): 1, (3, 2): 2,
+}
+
+
+def fetch_rows(w, core):
+    cols = lax.axis_size("height")
+    part = w.shape[0] // 2
+    mine = lax.dynamic_slice_in_dim(w, core * part, part, axis=0)
+    pairs = [
+        (src * cols + 2 * chip + c, dst * cols + 2 * src + c)
+        for (src, dst), chip in CARRIER.items()
+        for c in range(2)
+    ]
+    return mine, lax.ppermute(mine, ("depth", "height"), pairs)
+
+
+def fetch_columns(w, core):
     planes, cols = lax.axis_size("depth"), lax.axis_size("height")
-    chips = cols // 2
-    part = w.shape[0] // 2
-    mine = lax.dynamic_slice_in_dim(w, me_core * part, part, axis=0)
-    pairs = []
-    for d in range(planes):
-        for h in range(cols):
-            pairs.append((d * cols + h, (d ^ (h // 2)) * cols + 2 * d + h % 2))
-    del chips
-    return lax.ppermute(mine, ("depth", "height"), pairs)
-
-
-def plane_gather(x):
+    rows, width = w.shape
+    lanes = width // cols
+    split = w.reshape(rows, cols // 2, 2, lanes)
+    piece = lax.dynamic_index_in_dim(split, core, 2, keepdims=False).reshape(rows, width // 2)
+    pairs = [(d * cols + h, (d ^ (h // 2)) * cols + h) for d in range(planes) for h in range(cols)]
+    return lax.ppermute(piece, ("depth", "height"), pairs)
+
+
+def chip_gather(x):
     half = x.shape[0] // 2
     across_x, across_y = swap(x, "height", 2), swap(x, "height", 4)
-    core = swap(x, "height", 1)
     diag_a = swap(across_x[:half], "height", 4)
     diag_b = swap(across_y[half:], "height", 2)
-    return [
-        (0, 0, x),
-        (1, 0, core),
-        (2, 0, across_x),
-        (3, 0, swap(across_x, "height", 1)),
-        (4, 0, across_y),
-        (5, 0, swap(across_y, "height", 1)),
-        (6, 0, diag_a),
-        (6, half, diag_b),
-        (7, 0, swap(diag_a, "height", 1)),
-        (7, half, swap(diag_b, "height", 1)),
-    ]
-
-
-def mid_body(places, rows, h_ref, w_ref, *refs):
+    return [(0, 0, x), (1, 0, across_x), (2, 0, across_y), (3, 0, diag_a), (3, half, diag_b)]
+
+
+def plane_gather(x):
+    blocks = []
+    for mask, first, block in chip_gather(x):
+        blocks.append((2 * mask, first, block))
+        blocks.append((2 * mask + 1, first, swap(block, "height", 1)))
+    return blocks
+
+
+def mid_body(places, rows, here, local, fetched, *refs):
     blocks, out = refs[:-1], refs[-1]
-    h = h_ref[0]
-    w = w_ref[...]
+    d, h = here[0], here[1]
+    w = jnp.where(d == h // 2, local[...], fetched[...])
     for (mask, first), block in zip(places, blocks):
         n = block.shape[0]
         at = pl.multiple_of((h ^ mask) * rows + first, 16)
@@ -89,7 +106,7 @@
         ).astype(BF16)
 
 
-def kgrad_body(wid, group, mid, own, up, down, out, pad):
+def kgrad_body(wid, group, here, mid, own, near, far, out, pad):
     cells, chans = mid.shape
     g32 = mid[...].astype(F32)
     col = lax.broadcasted_iota(jnp.int32, (cells, 1), 0) % wid
@@ -98,10 +115,12 @@
     rhs = jnp.concatenate([left, mid[...], right], axis=1)
     zero = jnp.zeros((wid, chans), BF16)
     lane_group = lax.broadcasted_iota(jnp.int32, (group, chans), 1) // group
-    for s, plane in enumerate((down, own, up)):
-        pad[0:wid, :] = zero
-        pad[wid + cells : 2 * wid + cells, :] = zero
-        pad[wid : wid + cells, :] = jnp.maximum(plane[...], jnp.zeros((), BF16))
+    odd = here[0] % 2 == 1
+    below, above = jnp.where(odd, near[...], far[...]), jnp.where(odd, far[...], near[...])
+    pad[0:wid, :] = zero
+    pad[wid + cells : 2 * wid + cells, :] = zero
+    for s, plane in enumerate((below, own[...], above)):
+        pad[wid : wid + cells, :] = jnp.maximum(plane, jnp.zeros((), BF16))
         for t in range(3):
             lhs = pad[t * wid : t * wid + cells, :]
             res = lax.dot_general(lhs, rhs, TN, preferred_element_type=F32)
@@ -113,31 +132,51 @@
                 out[9 * s + 3 * t + u] = acc.astype(BF16)
 
 
-def back_body(wid, mid, lower, upper, pre, weights, out, pad):
+def back_body(wid, here, mid, near, far, pre, weights, *refs):
+    outs, pad = refs[:-1], refs[-1]
+    d, h = here[0], here[1]
     cells, chans = mid.shape
+    rows = cells // len(outs)
     zero = jnp.zeros((wid, chans), BF16)
-    for s, plane in enumerate((upper, mid, lower)):
+    odd = d % 2 == 1
+    pad[1, wid : wid + cells, :] = mid[...]
+    pad[2, wid : wid + cells, :] = jnp.where(odd, near[...], far[...])
+    pad[0, wid : wid + cells, :] = jnp.where(odd, far[...], near[...])
+    for s in range(3):
         pad[s, 0:wid, :] = zero
         pad[s, wid + cells : 2 * wid + cells, :] = zero
-        pad[s, wid : wid + cells, :] = plane[...]
-    col = lax.broadcasted_iota(jnp.int32, (256, 1), 0) % wid
-    for c in range(cells // 256):
+    col = lax.broadcasted_iota(jnp.int32, (rows, 1), 0) % wid
+    for m, out in enumerate(outs):
+        first = pl.multiple_of(((h // 2) ^ m) * rows, wid)
         lhs = jnp.concatenate(
-            [pad[s, (2 - t) * wid + 256 * c : (2 - t) * wid + 256 * c + 256, :] for s in range(3) for t in range(3)],
-            axis=1,
+            [pad[s, pl.ds(first + (2 - t) * wid, rows), :] for s in range(3) for t in range(3)], axis=1
         )
         y = lax.dot_general(lhs, weights[...], NT, preferred_element_type=F32)
         total = y[:, chans : 2 * chans]
-        total = total + jnp.where(col < wid - 1, pltpu.roll(y[:, :chans], 255, 0), 0.0)
+        total = total + jnp.where(col < wid - 1, pltpu.roll(y[:, :chans], rows - 1, 0), 0.0)
         total = total + jnp.where(col > 0, pltpu.roll(y[:, 2 * chans :], 1, 0), 0.0)
-        rows = slice(256 * c, 256 * c + 256)
-        out[rows, :] = jnp.where(pre[rows, :].astype(F32) > 0, total, 0.0).astype(BF16)
-
-
-def final_body(grad, w, skip, out):
-    lhs = jnp.concatenate([grad[i] for i in range(grad.shape[0])], axis=1)
-    acc = lax.dot_general(lhs, w[...], NT, preferred_element_type=F32)
-    out[...] = (skip[...].astype(F32) + acc).astype(BF16)
+        keep = pre[pl.ds(first, rows), :].astype(F32) > 0
+        out[...] = jnp.where(keep, total, 0.0).astype(BF16)
+
+
+def partial_body(places, here, skip, *refs):
+    chips = 4
+    grads, ws, (own, other, lhs_ref) = refs[:chips], refs[chips:-3], refs[-3:]
+    d, h = here[0], here[1]
+    chip, core = h // 2, h % 2
+    rows = skip.shape[0]
+    for m, grad in enumerate(grads):
+        lhs_ref[chip ^ m] = grad[...]
+    lhs = jnp.concatenate([lhs_ref[i] for i in range(chips)], axis=1)
+    width = skip.shape[1] // chips
+    for (mask, first), w in zip(places, ws):
+        n = w.shape[0]
+        acc = lax.dot_general(lhs, w[...], NT, preferred_element_type=F32)
+        at = pl.ds(pl.multiple_of((d ^ chip ^ mask) * width + first, 128), n)
+        here_part = jnp.where(core == 0, acc[:rows], acc[rows:])
+        there_part = jnp.where(core == 0, acc[rows:], acc[:rows])
+        own[:, at] = here_part + skip[:, at].astype(F32)
+        other[:, at] = there_part.astype(BF16)
 
 
 def block_weights(kernel, chans, group):
@@ -160,65 +199,73 @@
     return part
 
 
+def z_swaps(x):
+    n = lax.axis_size("depth")
+    between = [(i, i + 1) for i in range(1, n - 1, 2)]
+    far = lax.ppermute(x, "depth", between + [(j, i) for i, j in between])
+    return swap(x, "depth", 1), far
+
+
 def fast(grad_out, pre_act, w_in, w_out, kernel):
     _, rows_here, wid, width = grad_out.shape
     _, height, _, chans = pre_act.shape
     group = kernel.shape[1]
     block = rows_here * wid
     cells = height * wid
-    h = lax.axis_index("height")
-    h_arr = h.astype(jnp.int32).reshape(1)
+    d, h = lax.axis_index("depth"), lax.axis_index("height")
+    here = jnp.stack([d, h]).astype(jnp.int32)
     skip = grad_out.reshape(block, width)
     pre = pre_act.reshape(cells, chans)
 
     gathered = plane_gather(skip)
-    w_rows = fetch_rows(w_out, h % 2)
-    w_full = lax.all_gather(w_in, "depth", axis=0, tiled=True)
-    pre_lower, pre_upper = shift(pre, "depth", 1), shift(pre, "depth", -1)
+    local_rows, w_rows = fetch_rows(w_out, h % 2)
+    pre_near, pre_far = z_swaps(pre)
+    w_cols = fetch_columns(w_in, h % 2)
     weights = block_weights(kernel, chans, group)
 
     places = [(mask, first) for mask, first, _ in gathered]
     mid = call(
         functools.partial(mid_body, places, block),
         jax.ShapeDtypeStruct((cells, chans), BF16),
-        1 + len(places),
+        2 + len(places),
         flops=2 * cells * width * chans,
         nbytes=2 * cells * width,
-    )(h_arr, w_rows, *[b for _, _, b in gathered])
-
-    lower, upper = shift(mid, "depth", 1), shift(mid, "depth", -1)
+    )(here, local_rows, w_rows, *[b for _, _, b in gathered])
+
+    near, far = z_swaps(mid)
     part = call(
         functools.partial(kgrad_body, wid, group),
         jax.ShapeDtypeStruct((27, group, chans), BF16),
         4,
-        scalars=0,
         scratch=[pltpu.VMEM((cells + 2 * wid, chans), BF16)],
         flops=2 * 27 * chans * chans * cells,
         nbytes=10 * cells * chans,
-    )(mid, pre, pre_upper, pre_lower)
+    )(here, mid, pre, pre_near, pre_far)
     total_cells = cells * lax.axis_size("depth")
     scale = jnp.float32(total_cells) ** (-0.5)
     kernel_grad = sum_depth(part) * scale
 
+    w_blocks = chip_gather(w_cols)
+    chip_cells = 2 * block
     back = call(
         functools.partial(back_body, wid),
-        jax.ShapeDtypeStruct((cells, chans), BF16),
+        [jax.ShapeDtypeStruct((chip_cells, chans), BF16)] * (cells // chip_cells),
         5,
-        scalars=0,
         scratch=[pltpu.VMEM((3, cells + 2 * wid, chans), BF16)],
         flops=2 * 27 * chans * chans * cells,
         nbytes=10 * cells * chans,
-    )(mid, lower, upper, pre, weights)
-
-    parts = lax.all_to_all(back.reshape(cells // block, block, chans), "height", 0, 0)
-    grad_in = call(
-        final_body,
-        jax.ShapeDtypeStruct((block, width), BF16),
-        3,
-        scalars=0,
+    )(here, mid, near, far, pre, weights)
+    parts = [back[0]] + [swap(b, "height", 2 * m) for m, b in enumerate(back) if m]
+
+    own, other = call(
+        functools.partial(partial_body, [(mask, first) for mask, first, _ in w_blocks]),
+        [jax.ShapeDtypeStruct((block, width), F32), jax.ShapeDtypeStruct((block, width), BF16)],
+        1 + len(parts) + len(w_blocks),
+        scratch=[pltpu.VMEM((len(parts), chip_cells, chans), BF16)],
         flops=2 * block * width * width,
-        nbytes=2 * width * width,
-    )(parts, w_full, skip)
+        nbytes=width * width,
+    )(here, skip, *parts, *[b for _, _, b in w_blocks])
+    grad_in = (own + swap(other, "height", 1).astype(F32)).astype(BF16)
     return grad_in.reshape(grad_out.shape), kernel_grad
 
 

time: 107 us -> 73 us (0.68)
  the two profiles are of different devices: /device:TPU:8 before, /device:TPU:15 now
where the time goes in v2:
time: 73 us; the launch traced here: 72.6 us
  starting transfers between devices  41.1 us (56%)
  waiting for transfers between devices  16.2 us (22%)
  Pallas kernels  7.87 us (11%)
  local copies, waits for them, and re-layouts  4.68 us (6%)
  other arithmetic  1.89 us (3%)
  between operations  0.91 us (1%)
    ppermute x21, starting transfers between devices, swap(): return lax.ppermute(x, axis, [(i, i ^ mask) for i in range(n)])  27 us
    ppermute x1, waiting for transfers between devices, fetch_columns(): return lax.ppermute(piece, ('depth', 'height'), pairs)  8.93 us
    ppermute x2, starting transfers between devices, z_swaps(): far = lax.ppermute(x, 'depth', between + [(j, i) for i, j in between])  7.13 us
    ppermute x21, waiting for transfers between devices, swap(): return lax.ppermute(x, axis, [(i, i ^ mask) for i in range(n)])  5.88 us
    ppermute x1, starting transfers between devices, fetch_rows(): return (mine, lax.ppermute(mine, ('depth', 'height'), pairs))  3.81 us
    ppermute x1, starting transfers between devices, fetch_columns(): return lax.ppermute(piece, ('depth', 'height'), pairs)  3.18 us
    pallas_call x1, Pallas kernels, fast(): call(functools.partial(kgrad_body, wid, group), jax.ShapeDtypeStruct((27,...  2.7 us
    pallas_call x1, Pallas kernels, fast(): call(functools.partial(back_body, wid), [jax.ShapeDtypeStruct((chip_cells...  2.63 us
  transfers between devices with their start and end apart: 25, of which 6 were waited for; matrix products, arithmetic and copies ran while one was open for 7% of the time, Pallas kernels for 11%

profile of v2, /device:TPU:15, one launch (start us, length us, event | category | flops | bytes accessed | tf_op | source)
XLA Modules:
  0.0 72.6 jit_solution(3959825163081625749)
XLA Ops:
  0.6 0.0 copy-start
  0.6 0.3 collective-permute-start.2
  1.0 0.2 collective-permute-start.4
  1.2 0.5 copy-done
  1.7 0.0 copy-start.1
  1.7 3.8 %collective-permute-start = (bf16[128,1024]{1,0:T(8,128)(2,1)S(1)}, bf16[128,1024]{1,0:T(8,128)(2,1)S(1)}, u32[]{:S(2)}, u32[]{:S(2)}) collective-permute-start(bf16[128,1024]{1,0:T(8,128)(2,1)S(1)} %constant_dynamic-slice_fusion.local), channel_id=1, source_target_pairs={{0,8},{1,9},{2,16},{3,17},{4,24},{5,25},{10,2},{11,3},{14,18},{15,... | collective-permute-start | bytes 786440 | tf_op jit(solution)/shard_map/ppermute | solution.py:68
  5.5 1.6 %collective-permute-start.1 = (bf16[128,1024]{1,0:T(8,128)(2,1)}, bf16[128,1024]{1,0:T(8,128)(2,1)S(1)}, u32[]{:S(2)}, u32[]{:S(2)}) collective-permute-start(bf16[128,1024]{1,0:T(8,128)(2,1)} %bitcast.19), channel_id=1, source_target_pairs={{0,1},{1,0},{2,3},{3,2},{4,5},{5,4},{6,7},{7,6},{8,9},{9,8},{10,11... | collective-permute-start | bytes 786440 | tf_op jit(solution)/shard_map/ppermute | solution.py:39
  7.1 1.4 %reshape.106 = bf16[256,4,2,128]{3,2,1,0:T(2,128)(2,1)S(1)} reshape(bf16[256,1024]{1,0:T(8,128)(2,1)} %param.7) | data formatting | bytes 1048576 | tf_op jit(solution)/shard_map/reshape | solution.py:75
  8.5 1.6 %dynamic-slice_reduce_fusion = bf16[256,4,128]{2,1,0:T(4,128)(2,1)S(1)} fusion(bf16[256,4,2,128]{3,2,1,0:T(2,128)(2,1)S(1)} %reshape.106, s32[]{:T(128)S(6)} %select_n.43), kind=kLoop, calls=%fused_computation.3 | loop fusion | bytes 524292 | tf_op jit(solution)/shard_map/jit(dynamic_index_in_dim)/dynamic_slice | solution.py:76
  10.2 3.2 %collective-permute-start.15 = (bf16[256,512]{1,0:T(8,128)(2,1)S(1)}, bf16[256,512]{1,0:T(8,128)(2,1)S(1)}, u32[]{:S(2)}, u32[]{:S(2)}) collective-permute-start(bf16[256,512]{1,0:T(8,128)(2,1)S(1)} %bitcast.26), channel_id=1, source_target_pairs={{0,0},{1,1},{2,10},{3,11},{4,20},{5,21},{6,30},{7,31},{8,8},{9,9},... | collective-permute-start | bytes 786440 | tf_op jit(solution)/shard_map/ppermute | solution.py:78
  13.4 0.4 collective-permute-start.3
  13.8 1.2 %collective-permute-start.6 = (bf16[64,1024]{1,0:T(8,128)(2,1)S(1)}, bf16[64,1024]{1,0:T(8,128)(2,1)S(1)}, u32[]{:S(2)}, u32[]{:S(2)}) collective-permute-start(bf16[64,1024]{1,0:T(8,128)(2,1)S(1)} %slice.16), channel_id=1, source_target_pairs={{0,4},{1,5},{2,6},{3,7},{4,0},{5,1},{6,2},{7,3},{8,12},{9,13},{10,... | collective-permute-start | bytes 393224 | tf_op jit(solution)/shard_map/ppermute | solution.py:39
  15.0 0.1 collective-permute-start.8
  15.1 0.6 collective-permute-start.5
  15.7 8.9 %collective-permute-done.15.refs_4_ = bf16[256,512]{1,0:T(8,128)(2,1)S(1)} collective-permute-done((bf16[256,512]{1,0:T(8,128)(2,1)S(1)}, bf16[256,512]{1,0:T(8,128)(2,1)S(1)}, u32[]{:S(2)}, u32[]{:S(2)}) %collective-permute-start.15) | collective-permute-done | bytes 262176 | tf_op jit(solution)/shard_map/ppermute | solution.py:78
  24.6 4.1 %collective-permute-start.22 = (bf16[1024,128]{1,0:T(8,128)(2,1)}, bf16[1024,128]{1,0:T(8,128)(2,1)}, u32[]{:S(2)}, u32[]{:S(2)}) collective-permute-start(bf16[1024,128]{1,0:T(8,128)(2,1)} %bitcast.3.pre.own), channel_id=1, source_target_pairs={{8,16},{16,8},{9,17},{17,9},{10,18},{18,10},{11,19},{19,11},{12,20... | collective-permute-start | bytes 786440 | tf_op jit(solution)/shard_map/ppermute | solution.py:205
  28.8 0.8 %collective-permute-start.7 = (bf16[64,1024]{1,0:T(8,128)(2,1)S(1)}, bf16[64,1024]{1,0:T(8,128)(2,1)S(1)}, u32[]{:S(2)}, u32[]{:S(2)}) collective-permute-start(bf16[64,1024]{1,0:T(8,128)(2,1)S(1)} %collective-permute-done.6.refs_6_), channel_id=1, source_target_pairs={{0,1},{1,0},{2,3},{3,2},{4,5},{5,4},{6,7},{7,6},{8,9},{9,8},{10,11... | collective-permute-start | bytes 393224 | tf_op jit(solution)/shard_map/ppermute | solution.py:39
  29.5 0.1 collective-permute-start.9
  29.6 0.1 pad_add_fusion.here
  29.7 2.8 %collective-permute-start.16 = (bf16[256,512]{1,0:T(8,128)(2,1)S(1)}, bf16[256,512]{1,0:T(8,128)(2,1)S(1)}, u32[]{:S(2)}, u32[]{:S(2)}) collective-permute-start(bf16[256,512]{1,0:T(8,128)(2,1)S(1)} %collective-permute-done.15.refs_4_), channel_id=1, source_target_pairs={{0,2},{1,3},{2,0},{3,1},{4,6},{5,7},{6,4},{7,5},{8,10},{9,11},{10,... | collective-permute-start | bytes 786440 | tf_op jit(solution)/shard_map/ppermute | solution.py:39
  32.5 1.4 %shard_map.68.mid = bf16[1024,128]{1,0:T(8,128)(2,1)S(1)} custom-call(s32[2]{0:T(128)S(1)} %pad_add_fusion.here, bf16[128,1024]{1,0:T(8,128)(2,1)S(1)} %constant_dynamic-slice_fusion.local, bf16[128,1024]{1,0:T(8,128)(2,1)S(1)} %collective-permute-done.fetched, bf16[128,1024]{1,0:T(8,128)(2,1)S(1)} %bitcast.20, ...), custom_call_target="tpu_custom_call" | custom-call | flops 268435456 | bytes 2097152 | tf_op jit(solution)/shard_map/pallas_call | solution.py:227
  34.0 1.4 %collective-permute-done.22.far = bf16[1024,128]{1,0:T(8,128)(2,1)} collective-permute-done((bf16[1024,128]{1,0:T(8,128)(2,1)}, bf16[1024,128]{1,0:T(8,128)(2,1)}, u32[]{:S(2)}, u32[]{:S(2)}) %collective-permute-start.22) | collective-permute-done | bytes 262176 | tf_op jit(solution)/shard_map/ppermute | solution.py:205
  35.3 2.7 %shard_map.71 = bf16[27,32,128]{2,1,0:T(8,128)(2,1)S(1)} custom-call(s32[2]{0:T(128)S(1)} %pad_add_fusion.here, bf16[1024,128]{1,0:T(8,128)(2,1)S(1)} %shard_map.68.mid, bf16[1024,128]{1,0:T(8,128)(2,1)} %bitcast.3.pre.own, bf16[1024,128]{1,0:T(8,128)(2,1)} %collective-permute-done.21.near, bf16[1024,128]{1,0:T(8,128)(2,1)} %collective-permute-done.22.far), custom_call_target="tpu_custom_call" | custom-call | flops 905969664 | bytes 1310720 | tf_op jit(solution)/shard_map/pallas_call | solution.py:236
  38.1 0.1 collective-permute-start.23
  38.1 0.1 broadcast_compare_fusion
  38.2 0.1 collective-permute-start.17
  38.3 1.5 %collective-permute-start.10 = (bf16[1024,128]{1,0:T(8,128)(2,1)S(1)}, bf16[1024,128]{1,0:T(8,128)(2,1)S(1)}, u32[]{:S(2)}, u32[]{:S(2)}) collective-permute-start(bf16[1024,128]{1,0:T(8,128)(2,1)S(1)} %shard_map.68.mid), channel_id=1, source_target_pairs={{0,8},{8,0},{16,24},{24,16},{1,9},{9,1},{17,25},{25,17},{2,10},{10... | collective-permute-start | bytes 786440 | tf_op jit(solution)/shard_map/ppermute | solution.py:39
  39.8 3.0 %collective-permute-start.11 = (bf16[1024,128]{1,0:T(8,128)(2,1)S(1)}, bf16[1024,128]{1,0:T(8,128)(2,1)S(1)}, u32[]{:S(2)}, u32[]{:S(2)}) collective-permute-start(bf16[1024,128]{1,0:T(8,128)(2,1)S(1)} %shard_map.68.mid), channel_id=1, source_target_pairs={{8,16},{16,8},{9,17},{17,9},{10,18},{18,10},{11,19},{19,11},{12,20... | collective-permute-start | bytes 786440 | tf_op jit(solution)/shard_map/ppermute | solution.py:205
  42.9 1.5 %collective-permute-start.18 = (bf16[128,512]{1,0:T(8,128)(2,1)S(1)}, bf16[128,512]{1,0:T(8,128)(2,1)S(1)}, u32[]{:S(2)}, u32[]{:S(2)}) collective-permute-start(bf16[128,512]{1,0:T(8,128)(2,1)S(1)} %slice.18), channel_id=1, source_target_pairs={{0,4},{1,5},{2,6},{3,7},{4,0},{5,1},{6,2},{7,3},{8,12},{9,13},{10,... | collective-permute-start | bytes 393224 | tf_op jit(solution)/shard_map/ppermute | solution.py:39
  44.3 0.1 add_convert_fusion.1
  44.4 0.6 collective-permute-start.24
  45.0 0.1 tile.4
  45.2 0.1 select_bitcast_fusion
  45.2 0.7 copy.11
  45.9 0.3 copy.18
  46.2 1.9 %collective-permute-start.19 = (bf16[128,512]{1,0:T(8,128)(2,1)S(1)}, bf16[128,512]{1,0:T(8,128)(2,1)S(1)}, u32[]{:S(2)}, u32[]{:S(2)}) collective-permute-start(bf16[128,512]{1,0:T(8,128)(2,1)S(1)} %slice.19), channel_id=1, source_target_pairs={{0,2},{1,3},{2,0},{3,1},{4,6},{5,7},{6,4},{7,5},{8,10},{9,11},{10,... | collective-permute-start | bytes 393224 | tf_op jit(solution)/shard_map/ppermute | solution.py:39
  48.1 1.6 %collective-permute-done.10.near = bf16[1024,128]{1,0:T(8,128)(2,1)S(1)} collective-permute-done((bf16[1024,128]{1,0:T(8,128)(2,1)S(1)}, bf16[1024,128]{1,0:T(8,128)(2,1)S(1)}, u32[]{:S(2)}, u32[]{:S(2)}) %collective-permute-start.10) | collective-permute-done | bytes 262176 | tf_op jit(solution)/shard_map/ppermute | solution.py:39
  49.7 2.6 %shard_map.69 = (bf16[256,128]{1,0:T(8,128)(2,1)S(1)}, bf16[256,128]{1,0:T(8,128)(2,1)S(1)}, bf16[256,128]{1,0:T(8,128)(2,1)S(1)}, bf16[256,128]{1,0:T(8,128)(2,1)S(1)}) custom-call(s32[2]{0:T(128)S(1)} %pad_add_fusion.here, bf16[1024,128]{1,0:T(8,128)(2,1)S(1)} %shard_map.68.mid, bf16[1024,128]{1,0:T(8,128)(2,1)S(1)} %collective-permute-done.10.near, ...), custom_call_target="tpu_custom_call" | custom-call | flops 905969664 | bytes 1310720 | tf_op jit(solution)/shard_map/pallas_call | solution.py:250
  52.3 1.9 %collective-permute-start.12 = (bf16[256,128]{1,0:T(8,128)(2,1)S(1)}, bf16[256,128]{1,0:T(8,128)(2,1)S(1)}, u32[]{:S(2)}, u32[]{:S(2)}) collective-permute-start(bf16[256,128]{1,0:T(8,128)(2,1)S(1)} %get-tuple-element.9), channel_id=1, source_target_pairs={{0,2},{1,3},{2,0},{3,1},{4,6},{5,7},{6,4},{7,5},{8,10},{9,11},{10,... | collective-permute-start | bytes 196616 | tf_op jit(solution)/shard_map/ppermute | solution.py:39
  54.3 3.4 %collective-permute-start.13 = (bf16[256,128]{1,0:T(8,128)(2,1)S(1)}, bf16[256,128]{1,0:T(8,128)(2,1)S(1)}, u32[]{:S(2)}, u32[]{:S(2)}) collective-permute-start(bf16[256,128]{1,0:T(8,128)(2,1)S(1)} %get-tuple-element.10), channel_id=1, source_target_pairs={{0,4},{1,5},{2,6},{3,7},{4,0},{5,1},{6,2},{7,3},{8,12},{9,13},{10,... | collective-permute-start | bytes 196616 | tf_op jit(solution)/shard_map/ppermute | solution.py:39
  57.6 0.1 collective-permute-start.14
  57.7 1.6 %collective-permute-done.13.refs_2_ = bf16[256,128]{1,0:T(8,128)(2,1)S(1)} collective-permute-done((bf16[256,128]{1,0:T(8,128)(2,1)S(1)}, bf16[256,128]{1,0:T(8,128)(2,1)S(1)}, u32[]{:S(2)}, u32[]{:S(2)}) %collective-permute-start.13) | collective-permute-done | bytes 65568 | tf_op jit(solution)/shard_map/ppermute | solution.py:39
  59.3 2.4 %collective-permute-done.14.refs_3_ = bf16[256,128]{1,0:T(8,128)(2,1)S(1)} collective-permute-done((bf16[256,128]{1,0:T(8,128)(2,1)S(1)}, bf16[256,128]{1,0:T(8,128)(2,1)S(1)}, u32[]{:S(2)}, u32[]{:S(2)}) %collective-permute-start.14) | collective-permute-done | bytes 65568 | tf_op jit(solution)/shard_map/ppermute | solution.py:39
  61.7 1.1 %shard_map.70 = (f32[128,1024]{1,0:T(8,128)S(1)}, bf16[128,1024]{1,0:T(8,128)(2,1)S(1)}) custom-call(s32[2]{0:T(128)S(1)} %pad_add_fusion.here, bf16[128,1024]{1,0:T(8,128)(2,1)S(1)} %bitcast.21, bf16[256,128]{1,0:T(8,128)(2,1)S(1)} %get-tuple-element.8.refs_0_, bf16[256,128]{1,0:T(8,128)(2,1)S(1)} %collective-permute-done.12.refs_1_, ...), custom_call_target="tpu_custom_call" | custom-call | flops 268435456 | bytes 1048576 | tf_op jit(solution)/shard_map/pallas_call | solution.py:260
  62.8 7.9 %collective-permute-start.20 = (bf16[128,1024]{1,0:T(8,128)(2,1)S(1)}, bf16[128,1024]{1,0:T(8,128)(2,1)S(1)}, u32[]{:S(2)}, u32[]{:S(2)}) collective-permute-start(bf16[128,1024]{1,0:T(8,128)(2,1)S(1)} %get-tuple-element.13), channel_id=1, source_target_pairs={{0,1},{1,0},{2,3},{3,2},{4,5},{5,4},{6,7},{7,6},{8,9},{9,8},{10,11... | collective-permute-start | bytes 786440 | tf_op jit(solution)/shard_map/ppermute | solution.py:39
  70.7 0.8 %add_multiply_fusion = f32[27,32,128]{2,1,0:T(8,128)} fusion(bf16[27,32,128]{2,1,0:T(8,128)(2,1)S(1)} %collective-permute-done.24, bf16[27,32,128]{2,1,0:T(8,128)(2,1)S(1)} %add_convert_fusion.1), kind=kLoop, calls=%fused_computation.4 | loop fusion | flops 442368 | bytes 884736 | tf_op jit(solution)/shard_map/mul | solution.py:246
  71.5 0.3 collective-permute-done.20
  71.9 0.8 %add_convert_fusion = bf16[128,1024]{1,0:T(8,128)(2,1)} fusion(f32[128,1024]{1,0:T(8,128)S(1)} %get-tuple-element.12, bf16[128,1024]{1,0:T(8,128)(2,1)S(1)} %collective-permute-done.20), kind=kLoop, calls=%fused_computation.2 | loop fusion | flops 393216 | bytes 1048576 | tf_op jit(solution)/shard_map/convert_element_type | solution.py:268
  (30 shorter events, 0.2 us)
Async XLA Ops:
  0.6 1.0 %copy-start = (bf16[256,1024]{1,0:T(8,128)(2,1)S(1)}, bf16[256,1024]{1,0:T(8,128)(2,1)}, u32[]{:S(2)}) copy-start(bf16[256,1024]{1,0:T(8,128)(2,1)} %param.8) | copy-start | bytes 1572868
  0.6 12.7 %collective-permute-start.2 = (bf16[128,1024]{1,0:T(8,128)(2,1)}, bf16[128,1024]{1,0:T(8,128)(2,1)S(1)}, u32[]{:S(2)}, u32[]{:S(2)}) collective-permute-start(bf16[128,1024]{1,0:T(8,128)(2,1)} %bitcast.17), channel_id=1, source_target_pairs={{0,2},{1,3},{2,0},{3,1},{4,6},{5,7},{6,4},{7,5},{8,10},{9,11},{10,... | collective-permute-start | bytes 786440 | tf_op jit(solution)/shard_map/ppermute | solution.py:39
  1.0 12.8 %collective-permute-start.4 = (bf16[128,1024]{1,0:T(8,128)(2,1)}, bf16[128,1024]{1,0:T(8,128)(2,1)S(1)}, u32[]{:S(2)}, u32[]{:S(2)}) collective-permute-start(bf16[128,1024]{1,0:T(8,128)(2,1)} %bitcast.18), channel_id=1, source_target_pairs={{0,4},{1,5},{2,6},{3,7},{4,0},{5,1},{6,2},{7,3},{8,12},{9,13},{10,... | collective-permute-start | bytes 786440 | tf_op jit(solution)/shard_map/ppermute | solution.py:39
  1.7 30.8 %copy-start.1 = (bf16[1,2,64,1024]{3,2,1,0:T(8,128)(2,1)S(1)}, bf16[1,2,64,1024]{3,2,1,0:T(8,128)(2,1)}, u32[]{:S(2)}) copy-start(bf16[1,2,64,1024]{3,2,1,0:T(8,128)(2,1)} %param.5) | copy-start | bytes 786436
  1.7 13.3 %collective-permute-start = (bf16[128,1024]{1,0:T(8,128)(2,1)S(1)}, bf16[128,1024]{1,0:T(8,128)(2,1)S(1)}, u32[]{:S(2)}, u32[]{:S(2)}) collective-permute-start(bf16[128,1024]{1,0:T(8,128)(2,1)S(1)} %constant_dynamic-slice_fusion.local), channel_id=1, source_target_pairs={{0,8},{1,9},{2,16},{3,17},{4,24},{5,25},{10,2},{11,3},{14,18},{15,... | collective-permute-start | bytes 786440 | tf_op jit(solution)/shard_map/ppermute | solution.py:68
  5.5 9.6 %collective-permute-start.1 = (bf16[128,1024]{1,0:T(8,128)(2,1)}, bf16[128,1024]{1,0:T(8,128)(2,1)S(1)}, u32[]{:S(2)}, u32[]{:S(2)}) collective-permute-start(bf16[128,1024]{1,0:T(8,128)(2,1)} %bitcast.19), channel_id=1, source_target_pairs={{0,1},{1,0},{2,3},{3,2},{4,5},{5,4},{6,7},{7,6},{8,9},{9,8},{10,11... | collective-permute-start | bytes 786440 | tf_op jit(solution)/shard_map/ppermute | solution.py:39
  10.2 14.4 %collective-permute-start.15 = (bf16[256,512]{1,0:T(8,128)(2,1)S(1)}, bf16[256,512]{1,0:T(8,128)(2,1)S(1)}, u32[]{:S(2)}, u32[]{:S(2)}) collective-permute-start(bf16[256,512]{1,0:T(8,128)(2,1)S(1)} %bitcast.26), channel_id=1, source_target_pairs={{0,0},{1,1},{2,10},{3,11},{4,20},{5,21},{6,30},{7,31},{8,8},{9,9},... | collective-permute-start | bytes 786440 | tf_op jit(solution)/shard_map/ppermute | solution.py:78
  13.4 16.1 %collective-permute-start.3 = (bf16[128,1024]{1,0:T(8,128)(2,1)S(1)}, bf16[128,1024]{1,0:T(8,128)(2,1)S(1)}, u32[]{:S(2)}, u32[]{:S(2)}) collective-permute-start(bf16[128,1024]{1,0:T(8,128)(2,1)S(1)} %collective-permute-done.2.refs_2_), channel_id=1, source_target_pairs={{0,1},{1,0},{2,3},{3,2},{4,5},{5,4},{6,7},{7,6},{8,9},{9,8},{10,11... | collective-permute-start | bytes 786440 | tf_op jit(solution)/shard_map/ppermute | solution.py:39
  13.8 10.8 %collective-permute-start.6 = (bf16[64,1024]{1,0:T(8,128)(2,1)S(1)}, bf16[64,1024]{1,0:T(8,128)(2,1)S(1)}, u32[]{:S(2)}, u32[]{:S(2)}) collective-permute-start(bf16[64,1024]{1,0:T(8,128)(2,1)S(1)} %slice.16), channel_id=1, source_target_pairs={{0,4},{1,5},{2,6},{3,7},{4,0},{5,1},{6,2},{7,3},{8,12},{9,13},{10,... | collective-permute-start | bytes 393224 | tf_op jit(solution)/shard_map/ppermute | solution.py:39
  15.0 13.7 %collective-permute-start.8 = (bf16[64,1024]{1,0:T(8,128)(2,1)S(1)}, bf16[64,1024]{1,0:T(8,128)(2,1)S(1)}, u32[]{:S(2)}, u32[]{:S(2)}) collective-permute-start(bf16[64,1024]{1,0:T(8,128)(2,1)S(1)} %slice.17), channel_id=1, source_target_pairs={{0,2},{1,3},{2,0},{3,1},{4,6},{5,7},{6,4},{7,5},{8,10},{9,11},{10,... | collective-permute-start | bytes 393224 | tf_op jit(solution)/shard_map/ppermute | solution.py:39
  15.1 14.6 %collective-permute-start.5 = (bf16[128,1024]{1,0:T(8,128)(2,1)S(1)}, bf16[128,1024]{1,0:T(8,128)(2,1)S(1)}, u32[]{:S(2)}, u32[]{:S(2)}) collective-permute-start(bf16[128,1024]{1,0:T(8,128)(2,1)S(1)} %collective-permute-done.4.refs_4_), channel_id=1, source_target_pairs={{0,1},{1,0},{2,3},{3,2},{4,5},{5,4},{6,7},{7,6},{8,9},{9,8},{10,11... | collective-permute-start | bytes 786440 | tf_op jit(solution)/shard_map/ppermute | solution.py:39
  24.6 9.3 %collective-permute-start.21 = (bf16[1024,128]{1,0:T(8,128)(2,1)}, bf16[1024,128]{1,0:T(8,128)(2,1)}, u32[]{:S(2)}, u32[]{:S(2)}) collective-permute-start(bf16[1024,128]{1,0:T(8,128)(2,1)} %bitcast.3.pre.own), channel_id=1, source_target_pairs={{0,8},{8,0},{16,24},{24,16},{1,9},{9,1},{17,25},{25,17},{2,10},{10... | collective-permute-start | bytes 786440 | tf_op jit(solution)/shard_map/ppermute | solution.py:39
  24.6 10.7 %collective-permute-start.22 = (bf16[1024,128]{1,0:T(8,128)(2,1)}, bf16[1024,128]{1,0:T(8,128)(2,1)}, u32[]{:S(2)}, u32[]{:S(2)}) collective-permute-start(bf16[1024,128]{1,0:T(8,128)(2,1)} %bitcast.3.pre.own), channel_id=1, source_target_pairs={{8,16},{16,8},{9,17},{17,9},{10,18},{18,10},{11,19},{19,11},{12,20... | collective-permute-start | bytes 786440 | tf_op jit(solution)/shard_map/ppermute | solution.py:205
  28.8 3.7 %collective-permute-start.7 = (bf16[64,1024]{1,0:T(8,128)(2,1)S(1)}, bf16[64,1024]{1,0:T(8,128)(2,1)S(1)}, u32[]{:S(2)}, u32[]{:S(2)}) collective-permute-start(bf16[64,1024]{1,0:T(8,128)(2,1)S(1)} %collective-permute-done.6.refs_6_), channel_id=1, source_target_pairs={{0,1},{1,0},{2,3},{3,2},{4,5},{5,4},{6,7},{7,6},{8,9},{9,8},{10,11... | collective-permute-start | bytes 393224 | tf_op jit(solution)/shard_map/ppermute | solution.py:39
  29.5 3.0 %collective-permute-start.9 = (bf16[64,1024]{1,0:T(8,128)(2,1)S(1)}, bf16[64,1024]{1,0:T(8,128)(2,1)S(1)}, u32[]{:S(2)}, u32[]{:S(2)}) collective-permute-start(bf16[64,1024]{1,0:T(8,128)(2,1)S(1)} %collective-permute-done.8.refs_8_), channel_id=1, source_target_pairs={{0,1},{1,0},{2,3},{3,2},{4,5},{5,4},{6,7},{7,6},{8,9},{9,8},{10,11... | collective-permute-start | bytes 393224 | tf_op jit(solution)/shard_map/ppermute | solution.py:39
  29.7 13.1 %collective-permute-start.16 = (bf16[256,512]{1,0:T(8,128)(2,1)S(1)}, bf16[256,512]{1,0:T(8,128)(2,1)S(1)}, u32[]{:S(2)}, u32[]{:S(2)}) collective-permute-start(bf16[256,512]{1,0:T(8,128)(2,1)S(1)} %collective-permute-done.15.refs_4_), channel_id=1, source_target_pairs={{0,2},{1,3},{2,0},{3,1},{4,6},{5,7},{6,4},{7,5},{8,10},{9,11},{10,... | collective-permute-start | bytes 786440 | tf_op jit(solution)/shard_map/ppermute | solution.py:39
  34.0 11.1 %copy-start.2 = (bf16[27,32,128]{2,1,0:T(8,128)(2,1)S(1)}, bf16[27,32,128]{2,1,0:T(8,128)(2,1)}, u32[]{:S(2)}) copy-start(bf16[27,32,128]{2,1,0:T(8,128)(2,1)} %param.9) | copy-start | bytes 663556
  38.1 6.3 %collective-permute-start.23 = (bf16[27,32,128]{2,1,0:T(8,128)(2,1)S(1)}, bf16[27,32,128]{2,1,0:T(8,128)(2,1)S(1)}, u32[]{:S(2)}, u32[]{:S(2)}) collective-permute-start(bf16[27,32,128]{2,1,0:T(8,128)(2,1)S(1)} %shard_map.71), channel_id=1, source_target_pairs={{0,8},{8,0},{16,24},{24,16},{1,9},{9,1},{17,25},{25,17},{2,10},{10... | collective-permute-start | bytes 663560 | tf_op jit(solution)/shard_map/ppermute | solution.py:39
  38.2 8.0 %collective-permute-start.17 = (bf16[256,512]{1,0:T(8,128)(2,1)S(1)}, bf16[256,512]{1,0:T(8,128)(2,1)S(1)}, u32[]{:S(2)}, u32[]{:S(2)}) collective-permute-start(bf16[256,512]{1,0:T(8,128)(2,1)S(1)} %collective-permute-done.15.refs_4_), channel_id=1, source_target_pairs={{0,4},{1,5},{2,6},{3,7},{4,0},{5,1},{6,2},{7,3},{8,12},{9,13},{10,... | collective-permute-start | bytes 786440 | tf_op jit(solution)/shard_map/ppermute | solution.py:39
  38.3 11.4 %collective-permute-start.10 = (bf16[1024,128]{1,0:T(8,128)(2,1)S(1)}, bf16[1024,128]{1,0:T(8,128)(2,1)S(1)}, u32[]{:S(2)}, u32[]{:S(2)}) collective-permute-start(bf16[1024,128]{1,0:T(8,128)(2,1)S(1)} %shard_map.68.mid), channel_id=1, source_target_pairs={{0,8},{8,0},{16,24},{24,16},{1,9},{9,1},{17,25},{25,17},{2,10},{10... | collective-permute-start | bytes 786440 | tf_op jit(solution)/shard_map/ppermute | solution.py:39
  39.8 9.9 %collective-permute-start.11 = (bf16[1024,128]{1,0:T(8,128)(2,1)S(1)}, bf16[1024,128]{1,0:T(8,128)(2,1)S(1)}, u32[]{:S(2)}, u32[]{:S(2)}) collective-permute-start(bf16[1024,128]{1,0:T(8,128)(2,1)S(1)} %shard_map.68.mid), channel_id=1, source_target_pairs={{8,16},{16,8},{9,17},{17,9},{10,18},{18,10},{11,19},{19,11},{12,20... | collective-permute-start | bytes 786440 | tf_op jit(solution)/shard_map/ppermute | solution.py:205
  42.9 14.8 %collective-permute-start.18 = (bf16[128,512]{1,0:T(8,128)(2,1)S(1)}, bf16[128,512]{1,0:T(8,128)(2,1)S(1)}, u32[]{:S(2)}, u32[]{:S(2)}) collective-permute-start(bf16[128,512]{1,0:T(8,128)(2,1)S(1)} %slice.18), channel_id=1, source_target_pairs={{0,4},{1,5},{2,6},{3,7},{4,0},{5,1},{6,2},{7,3},{8,12},{9,13},{10,... | collective-permute-start | bytes 393224 | tf_op jit(solution)/shard_map/ppermute | solution.py:39
  44.4 26.3 %collective-permute-start.24 = (bf16[27,32,128]{2,1,0:T(8,128)(2,1)S(1)}, bf16[27,32,128]{2,1,0:T(8,128)(2,1)S(1)}, u32[]{:S(2)}, u32[]{:S(2)}) collective-permute-start(bf16[27,32,128]{2,1,0:T(8,128)(2,1)S(1)} %add_convert_fusion.1), channel_id=1, source_target_pairs={{0,16},{8,24},{16,0},{24,8},{1,17},{9,25},{17,1},{25,9},{2,18},{10... | collective-permute-start | bytes 663560 | tf_op jit(solution)/shard_map/ppermute | solution.py:39
  46.2 11.5 %collective-permute-start.19 = (bf16[128,512]{1,0:T(8,128)(2,1)S(1)}, bf16[128,512]{1,0:T(8,128)(2,1)S(1)}, u32[]{:S(2)}, u32[]{:S(2)}) collective-permute-start(bf16[128,512]{1,0:T(8,128)(2,1)S(1)} %slice.19), channel_id=1, source_target_pairs={{0,2},{1,3},{2,0},{3,1},{4,6},{5,7},{6,4},{7,5},{8,10},{9,11},{10,... | collective-permute-start | bytes 393224 | tf_op jit(solution)/shard_map/ppermute | solution.py:39
  52.3 5.4 %collective-permute-start.12 = (bf16[256,128]{1,0:T(8,128)(2,1)S(1)}, bf16[256,128]{1,0:T(8,128)(2,1)S(1)}, u32[]{:S(2)}, u32[]{:S(2)}) collective-permute-start(bf16[256,128]{1,0:T(8,128)(2,1)S(1)} %get-tuple-element.9), channel_id=1, source_target_pairs={{0,2},{1,3},{2,0},{3,1},{4,6},{5,7},{6,4},{7,5},{8,10},{9,11},{10,... | collective-permute-start | bytes 196616 | tf_op jit(solution)/shard_map/ppermute | solution.py:39
  54.3 5.0 %collective-permute-start.13 = (bf16[256,128]{1,0:T(8,128)(2,1)S(1)}, bf16[256,128]{1,0:T(8,128)(2,1)S(1)}, u32[]{:S(2)}, u32[]{:S(2)}) collective-permute-start(bf16[256,128]{1,0:T(8,128)(2,1)S(1)} %get-tuple-element.10), channel_id=1, source_target_pairs={{0,4},{1,5},{2,6},{3,7},{4,0},{5,1},{6,2},{7,3},{8,12},{9,13},{10,... | collective-permute-start | bytes 196616 | tf_op jit(solution)/shard_map/ppermute | solution.py:39
  57.6 4.0 %collective-permute-start.14 = (bf16[256,128]{1,0:T(8,128)(2,1)S(1)}, bf16[256,128]{1,0:T(8,128)(2,1)S(1)}, u32[]{:S(2)}, u32[]{:S(2)}) collective-permute-start(bf16[256,128]{1,0:T(8,128)(2,1)S(1)} %get-tuple-element.11), channel_id=1, source_target_pairs={{0,6},{1,7},{2,4},{3,5},{4,2},{5,3},{6,0},{7,1},{8,14},{9,15},{10,... | collective-permute-start | bytes 196616 | tf_op jit(solution)/shard_map/ppermute | solution.py:39
  62.8 9.1 %collective-permute-start.20 = (bf16[128,1024]{1,0:T(8,128)(2,1)S(1)}, bf16[128,1024]{1,0:T(8,128)(2,1)S(1)}, u32[]{:S(2)}, u32[]{:S(2)}) collective-permute-start(bf16[128,1024]{1,0:T(8,128)(2,1)S(1)} %get-tuple-element.13), channel_id=1, source_target_pairs={{0,1},{1,0},{2,3},{3,2},{4,5},{5,4},{6,7},{7,6},{8,9},{9,8},{10,11... | collective-permute-start | bytes 786440 | tf_op jit(solution)/shard_map/ppermute | solution.py:39

commit v3 on v2

--- a/solution.py
+++ b/solution.py
@@ -12,6 +12,7 @@
 NT = (((1,), (1,)), ((), ()))
 TN = (((0,), (0,)), ((), ()))
 VMEM_LIMIT = 48 * 1024 * 1024
+SPAN = 1 << 35
 
 
 def vmem():
@@ -48,34 +49,44 @@
     return lax.optimization_barrier((x,) + before)[0]
 
 
-CARRIER = {
-    (0, 1): 0, (0, 2): 1, (0, 3): 2,
-    (1, 0): 1, (1, 2): 3, (1, 3): 0,
-    (2, 0): 0, (2, 1): 2, (2, 3): 3,
-    (3, 0): 3, (3, 1): 1, (3, 2): 2,
-}
-
-
-def fetch_rows(w, core):
+CARRIERS = (
+    {
+        (0, 1): 0, (0, 2): 1, (0, 3): 2,
+        (1, 0): 1, (1, 2): 3, (1, 3): 0,
+        (2, 0): 0, (2, 1): 2, (2, 3): 3,
+        (3, 0): 3, (3, 1): 1, (3, 2): 2,
+    },
+    {
+        (0, 1): 1, (0, 2): 2, (0, 3): 0,
+        (1, 0): 0, (1, 2): 1, (1, 3): 3,
+        (2, 0): 3, (2, 1): 0, (2, 3): 2,
+        (3, 0): 1, (3, 1): 2, (3, 2): 3,
+    },
+)
+
+
+def pack_body(here, w_out, w_in, out):
+    core = here[1] % 2
+    part, width = w_out.shape[0] // 2, w_out.shape[1]
+    out[0] = w_out[pl.ds(pl.multiple_of(core * part, part), part), :]
+    lanes = width // 8
+    for i in range(4):
+        even = w_in[:, 2 * i * lanes : (2 * i + 1) * lanes]
+        odd = w_in[:, (2 * i + 1) * lanes : (2 * i + 2) * lanes]
+        block = jnp.where(core == 0, even, odd)
+        for half in range(2):
+            first = half * width // 2 + i * lanes
+            out[1, :, first : first + lanes] = block[half * part : (half + 1) * part]
+
+
+def fetch(mine):
     cols = lax.axis_size("height")
-    part = w.shape[0] // 2
-    mine = lax.dynamic_slice_in_dim(w, core * part, part, axis=0)
     pairs = [
         (src * cols + 2 * chip + c, dst * cols + 2 * src + c)
-        for (src, dst), chip in CARRIER.items()
-        for c in range(2)
+        for c, carrier in enumerate(CARRIERS)
+        for (src, dst), chip in carrier.items()
     ]
-    return mine, lax.ppermute(mine, ("depth", "height"), pairs)
-
-
-def fetch_columns(w, core):
-    planes, cols = lax.axis_size("depth"), lax.axis_size("height")
-    rows, width = w.shape
-    lanes = width // cols
-    split = w.reshape(rows, cols // 2, 2, lanes)
-    piece = lax.dynamic_index_in_dim(split, core, 2, keepdims=False).reshape(rows, width // 2)
-    pairs = [(d * cols + h, (d ^ (h // 2)) * cols + h) for d in range(planes) for h in range(cols)]
-    return lax.ppermute(piece, ("depth", "height"), pairs)
+    return lax.ppermute(mine, ("depth", "height"), pairs)
 
 
 def chip_gather(x):
@@ -86,50 +97,67 @@
     return [(0, 0, x), (1, 0, across_x), (2, 0, across_y), (3, 0, diag_a), (3, half, diag_b)]
 
 
-def plane_gather(x):
+def plane_gather(chip_blocks):
     blocks = []
-    for mask, first, block in chip_gather(x):
+    for mask, first, block in chip_blocks:
         blocks.append((2 * mask, first, block))
         blocks.append((2 * mask + 1, first, swap(block, "height", 1)))
     return blocks
 
 
 def mid_body(places, rows, here, local, fetched, *refs):
-    blocks, out = refs[:-1], refs[-1]
+    blocks, (out, w_in) = refs[:-2], refs[-2:]
     d, h = here[0], here[1]
-    w = jnp.where(d == h // 2, local[...], fetched[...])
+    own = d == h // 2
+    w = jnp.where(own, local[0], fetched[0])
     for (mask, first), block in zip(places, blocks):
         n = block.shape[0]
         at = pl.multiple_of((h ^ mask) * rows + first, 16)
         out[pl.ds(at, n), :] = lax.dot_general(
             block[...], w, NT, preferred_element_type=F32
         ).astype(BF16)
-
-
-def kgrad_body(wid, group, here, mid, own, near, far, out, pad):
-    cells, chans = mid.shape
-    g32 = mid[...].astype(F32)
+    w_in[...] = jnp.where(own, local[1], fetched[1])
+
+
+def kgrad_body(wid, group, planes, *refs):
+    mids, (pre, out, pad) = refs[:planes], refs[planes:]
+    cells, chans = pre.shape
     col = lax.broadcasted_iota(jnp.int32, (cells, 1), 0) % wid
-    left = jnp.where(col < wid - 1, pltpu.roll(g32, cells - 1, 0), 0.0).astype(BF16)
-    right = jnp.where(col > 0, pltpu.roll(g32, 1, 0), 0.0).astype(BF16)
-    rhs = jnp.concatenate([left, mid[...], right], axis=1)
+    rhs = []
+    for mid in mids:
+        p32 = mid[...].astype(F32)
+        left = jnp.where(col < wid - 1, pltpu.roll(p32, cells - 1, 0), 0.0).astype(BF16)
+        right = jnp.where(col > 0, pltpu.roll(p32, 1, 0), 0.0).astype(BF16)
+        rhs += [left, mid[...], right]
+    rhs = jnp.concatenate(rhs, axis=1)
+    lane_group = lax.broadcasted_iota(jnp.int32, (group, chans), 1) // group
     zero = jnp.zeros((wid, chans), BF16)
-    lane_group = lax.broadcasted_iota(jnp.int32, (group, chans), 1) // group
-    odd = here[0] % 2 == 1
-    below, above = jnp.where(odd, near[...], far[...]), jnp.where(odd, far[...], near[...])
     pad[0:wid, :] = zero
     pad[wid + cells : 2 * wid + cells, :] = zero
-    for s, plane in enumerate((below, own[...], above)):
-        pad[wid : wid + cells, :] = jnp.maximum(plane, jnp.zeros((), BF16))
-        for t in range(3):
-            lhs = pad[t * wid : t * wid + cells, :]
-            res = lax.dot_general(lhs, rhs, TN, preferred_element_type=F32)
+    pad[wid : wid + cells, :] = jnp.maximum(pre[...], jnp.zeros((), BF16))
+    for t in range(3):
+        lhs = pad[t * wid : t * wid + cells, :]
+        res = lax.dot_general(lhs, rhs, TN, preferred_element_type=F32)
+        for p in range(planes):
             for u in range(3):
-                tile = res[:, u * chans : (u + 1) * chans]
+                first = (3 * p + u) * chans
+                tile = res[:, first : first + chans]
                 acc = jnp.zeros((group, chans), F32)
                 for g in range(chans // group):
                     acc = jnp.where(lane_group == g, tile[g * group : (g + 1) * group, :], acc)
-                out[9 * s + 3 * t + u] = acc.astype(BF16)
+                out[p, 3 * t + u] = acc.astype(BF16)
+
+
+def pair_body(here, early, late, other_early, other_late, out):
+    odd = here[0] % 2
+    out[1] = (early[0].astype(F32) + other_early[0].astype(F32)).astype(BF16)
+    out[2 * odd] = (early[1].astype(F32) + other_late[0].astype(F32)).astype(BF16)
+    out[2 - 2 * odd] = (late[0].astype(F32) + other_early[1].astype(F32)).astype(BF16)
+
+
+def total_body(scale, own, other, out):
+    for s in range(3):
+        out[9 * s : 9 * s + 9] = (own[s].astype(F32) + other[s].astype(F32)) * scale
 
 
 def back_body(wid, here, mid, near, far, pre, weights, *refs):
@@ -159,51 +187,46 @@
         out[...] = jnp.where(keep, total, 0.0).astype(BF16)
 
 
-def partial_body(places, here, skip, *refs):
+def partial_body(here, skip, *refs):
     chips = 4
     grads, ws, (own, other, lhs_ref) = refs[:chips], refs[chips:-3], refs[-3:]
-    d, h = here[0], here[1]
-    chip, core = h // 2, h % 2
+    chip, core = here[1] // 2, here[1] % 2
     rows = skip.shape[0]
     for m, grad in enumerate(grads):
         lhs_ref[chip ^ m] = grad[...]
     lhs = jnp.concatenate([lhs_ref[i] for i in range(chips)], axis=1)
-    width = skip.shape[1] // chips
-    for (mask, first), w in zip(places, ws):
-        n = w.shape[0]
-        acc = lax.dot_general(lhs, w[...], NT, preferred_element_type=F32)
-        at = pl.ds(pl.multiple_of((d ^ chip ^ mask) * width + first, 128), n)
-        here_part = jnp.where(core == 0, acc[:rows], acc[rows:])
-        there_part = jnp.where(core == 0, acc[rows:], acc[:rows])
-        own[:, at] = here_part + skip[:, at].astype(F32)
-        other[:, at] = there_part.astype(BF16)
-
-
-def block_weights(kernel, chans, group):
-    groups = chans // group
-    row_group = jnp.arange(chans)[:, None] // group
-    lane_group = jnp.arange(chans)[None, :] // group
-    tiled = jnp.tile(kernel, (1, groups, 1))
-    tiled = jnp.where(row_group == lane_group, tiled, jnp.zeros_like(tiled))
-    tiled = tiled.reshape(9, 3, chans, chans)
-    return jnp.transpose(tiled, (1, 2, 0, 3)).reshape(3 * chans, 9 * chans)
-
-
-def sum_depth(part):
-    n = lax.axis_size("depth")
-    mask = 1
-    while mask < n:
-        part = part.astype(BF16)
-        part = part.astype(F32) + swap(part, "depth", mask).astype(F32)
-        mask *= 2
-    return part
+    part, depth = ws[0].shape[0], lhs.shape[1]
+    for m, w in enumerate(ws):
+        for half in range(2):
+            acc = lax.dot_general(
+                lhs, w[:, half * depth : (half + 1) * depth], NT, preferred_element_type=F32
+            )
+            at = pl.ds(pl.multiple_of((chip ^ m) * 2 * part + half * part, part), part)
+            here_part = jnp.where(core == 0, acc[:rows], acc[rows:])
+            there_part = jnp.where(core == 0, acc[rows:], acc[:rows])
+            own[:, at] = here_part + skip[:, at].astype(F32)
+            other[:, at] = there_part.astype(BF16)
+
+
+def weights_body(group, kernel, out):
+    chans = kernel.shape[2]
+    row_group = lax.broadcasted_iota(jnp.int32, (chans, chans), 0) // group
+    lane_group = lax.broadcasted_iota(jnp.int32, (chans, chans), 1) // group
+    zero = jnp.zeros((chans, chans), BF16)
+    for o in range(27):
+        st, u = o // 3, o % 3
+        tiled = jnp.concatenate([kernel[o]] * (chans // group), axis=0)
+        out[u * chans : (u + 1) * chans, st * chans : (st + 1) * chans] = jnp.where(
+            row_group == lane_group, tiled, zero
+        )
 
 
 def z_swaps(x):
     n = lax.axis_size("depth")
     between = [(i, i + 1) for i in range(1, n - 1, 2)]
     far = lax.ppermute(x, "depth", between + [(j, i) for i, j in between])
-    return swap(x, "depth", 1), far
+    near = swap(x, "depth", 1)
+    return near, far
 
 
 def fast(grad_out, pre_act, w_in, w_out, kernel):
@@ -217,35 +240,60 @@
     skip = grad_out.reshape(block, width)
     pre = pre_act.reshape(cells, chans)
 
-    gathered = plane_gather(skip)
-    local_rows, w_rows = fetch_rows(w_out, h % 2)
-    pre_near, pre_far = z_swaps(pre)
-    w_cols = fetch_columns(w_in, h % 2)
-    weights = block_weights(kernel, chans, group)
+    blocks = chip_gather(skip)
+    gathered = plane_gather(blocks)
+    mine = call(
+        pack_body, jax.ShapeDtypeStruct((2, w_out.shape[0] // 2, width), BF16), 2, nbytes=6 * w_out.size
+    )(here, w_out, w_in)
+    fetched = fetch(mine)
+    weights = call(
+        functools.partial(weights_body, group),
+        jax.ShapeDtypeStruct((3 * chans, 9 * chans), BF16),
+        1,
+        scalars=0,
+        nbytes=54 * chans * chans,
+    )(order(kernel, fetched))
 
     places = [(mask, first) for mask, first, _ in gathered]
-    mid = call(
+    mid, w_cols = call(
         functools.partial(mid_body, places, block),
-        jax.ShapeDtypeStruct((cells, chans), BF16),
+        [jax.ShapeDtypeStruct((cells, chans), BF16), jax.ShapeDtypeStruct(mine.shape[1:], BF16)],
         2 + len(places),
         flops=2 * cells * width * chans,
         nbytes=2 * cells * width,
-    )(here, local_rows, w_rows, *[b for _, _, b in gathered])
+    )(here, mine, fetched, *[b for _, _, b in gathered])
 
     near, far = z_swaps(mid)
-    part = call(
-        functools.partial(kgrad_body, wid, group),
-        jax.ShapeDtypeStruct((27, group, chans), BF16),
+    kernel_flops = 2 * 9 * chans * chans * cells
+    early, late = (
+        call(
+            functools.partial(kgrad_body, wid, group, len(planes)),
+            jax.ShapeDtypeStruct((len(planes), 9, group, chans), BF16),
+            len(planes) + 1,
+            scalars=0,
+            scratch=[pltpu.VMEM((cells + 2 * wid, chans), BF16)],
+            flops=kernel_flops * len(planes),
+            nbytes=6 * cells * chans,
+        )(*planes, pre)
+        for planes in ((mid, near), (far,))
+    )
+    pair = call(
+        pair_body,
+        jax.ShapeDtypeStruct((3, 9, group, chans), BF16),
         4,
-        scratch=[pltpu.VMEM((cells + 2 * wid, chans), BF16)],
-        flops=2 * 27 * chans * chans * cells,
-        nbytes=10 * cells * chans,
-    )(here, mid, pre, pre_near, pre_far)
+        nbytes=100 * 9 * group * chans,
+    )(here, early, late, swap(early, "depth", 1), swap(late, "depth", 1))
     total_cells = cells * lax.axis_size("depth")
-    scale = jnp.float32(total_cells) ** (-0.5)
-    kernel_grad = sum_depth(part) * scale
-
-    w_blocks = chip_gather(w_cols)
+    kernel_grad = call(
+        functools.partial(total_body, float(total_cells) ** -0.5),
+        jax.ShapeDtypeStruct((27, group, chans), F32),
+        2,
+        scalars=0,
+        flops=SPAN,
+        nbytes=24 * 9 * group * chans,
+    )(pair, swap(pair, "depth", 2))
+
+    w_blocks = [w_cols] + [swap(w_cols, "height", 2 * m) for m in (1, 2, 3)]
     chip_cells = 2 * block
     back = call(
         functools.partial(back_body, wid),
@@ -254,18 +302,19 @@
         scratch=[pltpu.VMEM((3, cells + 2 * wid, chans), BF16)],
         flops=2 * 27 * chans * chans * cells,
         nbytes=10 * cells * chans,
-    )(here, mid, near, far, pre, weights)
+    )(here, mid, near, far, pre, order(weights, early, late))
     parts = [back[0]] + [swap(b, "height", 2 * m) for m, b in enumerate(back) if m]
 
     own, other = call(
-        functools.partial(partial_body, [(mask, first) for mask, first, _ in w_blocks]),
+        partial_body,
         [jax.ShapeDtypeStruct((block, width), F32), jax.ShapeDtypeStruct((block, width), BF16)],
         1 + len(parts) + len(w_blocks),
         scratch=[pltpu.VMEM((len(parts), chip_cells, chans), BF16)],
-        flops=2 * block * width * width,
+        flops=SPAN,
         nbytes=width * width,
-    )(here, skip, *parts, *[b for _, _, b in w_blocks])
-    grad_in = (own + swap(other, "height", 1).astype(F32)).astype(BF16)
+    )(here, order(skip, pair), *parts, *w_blocks)
+    theirs = order(swap(other, "height", 1), kernel_grad)
+    grad_in = (own + theirs.astype(F32)).astype(BF16)
     return grad_in.reshape(grad_out.shape), kernel_grad
 
 

time: 73 us -> 58.5 us (0.80)
  the two profiles are of different devices: /device:TPU:15 before, /device:TPU:0 now
where the time goes in v3:
time: 58.5 us; the launch traced here: 58.2 us
  starting transfers between devices  29.1 us (50%)
  waiting for transfers between devices  16.6 us (28%)
  Pallas kernels  8.75 us (15%)
  local copies, waits for them, and re-layouts  2.11 us (4%)
  other arithmetic  0.84 us (1%)
  between operations  0.8 us (1%)
    ppermute x20, starting transfers between devices, swap(): return lax.ppermute(x, axis, [(i, i ^ mask) for i in range(n)])  24.9 us
    ppermute x20, waiting for transfers between devices, swap(): return lax.ppermute(x, axis, [(i, i ^ mask) for i in range(n)])  14.9 us
    ppermute x1, starting transfers between devices, fetch(): return lax.ppermute(mine, ('depth', 'height'), pairs)  3.51 us
    pallas_call x1, Pallas kernels, fast(): call(functools.partial(back_body, wid), [jax.ShapeDtypeStruct((chip_cells...  2.21 us
    unnamed x10, local copies, waits for them, and re-layouts  2.1 us
    ppermute x1, waiting for transfers between devices, fetch(): return lax.ppermute(mine, ('depth', 'height'), pairs)  1.71 us
    pallas_call x2, Pallas kernels, fast(): call(functools.partial(kgrad_body, wid, group, len(planes)), jax.ShapeDty...  1.64 us
    pallas_call x1, Pallas kernels, fast(): call(functools.partial(mid_body, places, block), [jax.ShapeDtypeStruct((c...  1.44 us
  transfers between devices with their start and end apart: 22, of which 6 were waited for; matrix products, arithmetic and copies ran while one was open for 0% of the time, Pallas kernels for 13%

profile of v3, /device:TPU:0, one launch (start us, length us, event | category | flops | bytes accessed | tf_op | source)
XLA Modules:
  0.0 58.2 jit_solution(8413283508498067881)
XLA Ops:
  0.6 3.0 %collective-permute-start.2 = (bf16[128,1024]{1,0:T(8,128)(2,1)}, bf16[128,1024]{1,0:T(8,128)(2,1)S(1)}, u32[]{:S(2)}, u32[]{:S(2)}) collective-permute-start(bf16[128,1024]{1,0:T(8,128)(2,1)} %bitcast.5), channel_id=1, source_target_pairs={{0,2},{1,3},{2,0},{3,1},{4,6},{5,7},{6,4},{7,5},{8,10},{9,11},{10,... | collective-permute-start | bytes 786440 | tf_op jit(solution)/shard_map/ppermute | solution.py:40
  3.6 1.5 %collective-permute-start.4 = (bf16[128,1024]{1,0:T(8,128)(2,1)}, bf16[128,1024]{1,0:T(8,128)(2,1)S(1)}, u32[]{:S(2)}, u32[]{:S(2)}) collective-permute-start(bf16[128,1024]{1,0:T(8,128)(2,1)} %bitcast.6), channel_id=1, source_target_pairs={{0,4},{1,5},{2,6},{3,7},{4,0},{5,1},{6,2},{7,3},{8,12},{9,13},{10,... | collective-permute-start | bytes 786440 | tf_op jit(solution)/shard_map/ppermute | solution.py:40
  5.2 0.1 pad_add_fusion.here
  5.2 1.0 %copy-done = bf16[256,1024]{1,0:T(8,128)(2,1)S(1)} copy-done((bf16[256,1024]{1,0:T(8,128)(2,1)S(1)}, bf16[256,1024]{1,0:T(8,128)(2,1)}, u32[]{:S(2)}) %copy-start) | copy-done | bytes 524312
  6.3 1.0 %copy-done.1 = bf16[256,1024]{1,0:T(8,128)(2,1)S(1)} copy-done((bf16[256,1024]{1,0:T(8,128)(2,1)S(1)}, bf16[256,1024]{1,0:T(8,128)(2,1)}, u32[]{:S(2)}) %copy-start.1) | copy-done | bytes 524312
  7.3 0.6 %shard_map.68.local = bf16[2,128,1024]{2,1,0:T(8,128)(2,1)S(1)} custom-call(s32[2]{0:T(128)S(1)} %pad_add_fusion.here, bf16[256,1024]{1,0:T(8,128)(2,1)S(1)} %copy-done, bf16[256,1024]{1,0:T(8,128)(2,1)S(1)} %copy-done.1), custom_call_target="tpu_custom_call" | custom-call | bytes 1572864 | tf_op jit(solution)/shard_map/pallas_call | solution.py:245
  7.9 3.5 %collective-permute-start = (bf16[2,128,1024]{2,1,0:T(8,128)(2,1)S(1)}, bf16[2,128,1024]{2,1,0:T(8,128)(2,1)S(1)}, u32[]{:S(2)}, u32[]{:S(2)}) collective-permute-start(bf16[2,128,1024]{2,1,0:T(8,128)(2,1)S(1)} %shard_map.68.local), channel_id=1, source_target_pairs={{0,8},{2,16},{4,24},{10,2},{14,18},{8,26},{16,4},{20,12},{22,28},{... | collective-permute-start | bytes 1572872 | tf_op jit(solution)/shard_map/ppermute | solution.py:89
  11.5 1.1 %collective-permute-start.1 = (bf16[128,1024]{1,0:T(8,128)(2,1)S(1)}, bf16[128,1024]{1,0:T(8,128)(2,1)S(1)}, u32[]{:S(2)}, u32[]{:S(2)}) collective-permute-start(bf16[128,1024]{1,0:T(8,128)(2,1)S(1)} %bitcast.7), channel_id=1, source_target_pairs={{0,1},{1,0},{2,3},{3,2},{4,5},{5,4},{6,7},{7,6},{8,9},{9,8},{10,11... | collective-permute-start | bytes 786440 | tf_op jit(solution)/shard_map/ppermute | solution.py:40
  12.6 0.0 collective-permute-done.2.refs_2_
  12.6 2.5 %collective-permute-start.6 = (bf16[64,1024]{1,0:T(8,128)(2,1)S(1)}, bf16[64,1024]{1,0:T(8,128)(2,1)S(1)}, u32[]{:S(2)}, u32[]{:S(2)}) collective-permute-start(bf16[64,1024]{1,0:T(8,128)(2,1)S(1)} %slice.8), channel_id=1, source_target_pairs={{0,4},{1,5},{2,6},{3,7},{4,0},{5,1},{6,2},{7,3},{8,12},{9,13},{10,... | collective-permute-start | bytes 393224 | tf_op jit(solution)/shard_map/ppermute | solution.py:40
  15.1 0.0 copy-start.4
  15.1 0.1 collective-permute-start.8
  15.2 0.3 collective-permute-start.3
  15.5 0.3 collective-permute-start.5
  15.8 5.4 %collective-permute-done.6.refs_6_ = bf16[64,1024]{1,0:T(8,128)(2,1)S(1)} collective-permute-done((bf16[64,1024]{1,0:T(8,128)(2,1)S(1)}, bf16[64,1024]{1,0:T(8,128)(2,1)S(1)}, u32[]{:S(2)}, u32[]{:S(2)}) %collective-permute-start.6) | collective-permute-done | bytes 131104 | tf_op jit(solution)/shard_map/ppermute | solution.py:40
  21.2 0.5 collective-permute-start.9
  21.7 1.7 %collective-permute-done.fetched = bf16[2,128,1024]{2,1,0:T(8,128)(2,1)S(1)} collective-permute-done((bf16[2,128,1024]{2,1,0:T(8,128)(2,1)S(1)}, bf16[2,128,1024]{2,1,0:T(8,128)(2,1)S(1)}, u32[]{:S(2)}, u32[]{:S(2)}) %collective-permute-start) | collective-permute-done | bytes 524320 | tf_op jit(solution)/shard_map/ppermute | solution.py:89
  23.4 0.0 collective-permute-done.7.refs_7_
  23.4 0.0 collective-permute-done.9.refs_9_
  23.4 0.0 collective-permute-done.3.refs_3_
  23.4 1.4 %shard_map.69 = (bf16[1024,128]{1,0:T(8,128)(2,1)S(1)}, bf16[128,1024]{1,0:T(8,128)(2,1)S(1)}) custom-call(s32[2]{0:T(128)S(1)} %pad_add_fusion.here, bf16[2,128,1024]{2,1,0:T(8,128)(2,1)S(1)} %shard_map.68.local, bf16[2,128,1024]{2,1,0:T(8,128)(2,1)S(1)} %collective-permute-done.fetched, bf16[128,1024]{1,0:T(8,128)(2,1)S(1)} %bitcast.8, ...), custom_call_target="tpu_custom_call" | custom-call | flops 268435456 | bytes 2097152 | tf_op jit(solution)/shard_map/pallas_call | solution.py:258
  24.9 2.6 %collective-permute-start.10 = (bf16[1024,128]{1,0:T(8,128)(2,1)S(1)}, bf16[1024,128]{1,0:T(8,128)(2,1)S(1)}, u32[]{:S(2)}, u32[]{:S(2)}) collective-permute-start(bf16[1024,128]{1,0:T(8,128)(2,1)S(1)} %get-tuple-element.14.refs_0_.mid), channel_id=1, source_target_pairs={{0,8},{8,0},{16,24},{24,16},{1,9},{9,1},{17,25},{25,17},{2,10},{10... | collective-permute-start | bytes 786440 | tf_op jit(solution)/shard_map/ppermute | solution.py:40
  27.5 0.7 %collective-permute-start.11 = (bf16[1024,128]{1,0:T(8,128)(2,1)S(1)}, bf16[1024,128]{1,0:T(8,128)(2,1)S(1)}, u32[]{:S(2)}, u32[]{:S(2)}) collective-permute-start(bf16[1024,128]{1,0:T(8,128)(2,1)S(1)} %get-tuple-element.14.refs_0_.mid), channel_id=1, source_target_pairs={{8,16},{16,8},{9,17},{17,9},{10,18},{18,10},{11,19},{19,11},{12,20... | collective-permute-start | bytes 786440 | tf_op jit(solution)/shard_map/ppermute | solution.py:227
  28.2 0.1 collective-permute-start.17
  28.2 1.5 %collective-permute-start.18 = (bf16[128,1024]{1,0:T(8,128)(2,1)S(1)}, bf16[128,1024]{1,0:T(8,128)(2,1)S(1)}, u32[]{:S(2)}, u32[]{:S(2)}) collective-permute-start(bf16[128,1024]{1,0:T(8,128)(2,1)S(1)} %get-tuple-element.22.refs_4_), channel_id=1, source_target_pairs={{0,4},{1,5},{2,6},{3,7},{4,0},{5,1},{6,2},{7,3},{8,12},{9,13},{10,... | collective-permute-start | bytes 786440 | tf_op jit(solution)/shard_map/ppermute | solution.py:40
  29.7 2.0 %collective-permute-start.19 = (bf16[128,1024]{1,0:T(8,128)(2,1)S(1)}, bf16[128,1024]{1,0:T(8,128)(2,1)S(1)}, u32[]{:S(2)}, u32[]{:S(2)}) collective-permute-start(bf16[128,1024]{1,0:T(8,128)(2,1)S(1)} %get-tuple-element.22.refs_4_), channel_id=1, source_target_pairs={{0,6},{1,7},{2,4},{3,5},{4,2},{5,3},{6,0},{7,1},{8,14},{9,15},{10,... | collective-permute-start | bytes 786440 | tf_op jit(solution)/shard_map/ppermute | solution.py:40
  31.7 1.9 %collective-permute-done.10.refs_1_.near = bf16[1024,128]{1,0:T(8,128)(2,1)S(1)} collective-permute-done((bf16[1024,128]{1,0:T(8,128)(2,1)S(1)}, bf16[1024,128]{1,0:T(8,128)(2,1)S(1)}, u32[]{:S(2)}, u32[]{:S(2)}) %collective-permute-start.10) | collective-permute-done | bytes 262176 | tf_op jit(solution)/shard_map/ppermute | solution.py:40
  33.6 1.0 %shard_map.70.early = bf16[2,9,32,128]{3,2,1,0:T(8,128)(2,1)S(1)} custom-call(bf16[1024,128]{1,0:T(8,128)(2,1)S(1)} %get-tuple-element.14.refs_0_.mid, bf16[1024,128]{1,0:T(8,128)(2,1)S(1)} %collective-permute-done.10.refs_1_.near, bf16[1024,128]{1,0:T(8,128)(2,1)S(1)} %bitcast.10), custom_call_target="tpu_custom_call" | custom-call | flops 603979776 | bytes 786432 | tf_op jit(solution)/shard_map/pallas_call | solution.py:269
  34.6 2.9 %collective-permute-start.12 = (bf16[2,9,32,128]{3,2,1,0:T(8,128)(2,1)S(1)}, bf16[2,9,32,128]{3,2,1,0:T(8,128)(2,1)S(1)}, u32[]{:S(2)}, u32[]{:S(2)}) collective-permute-start(bf16[2,9,32,128]{3,2,1,0:T(8,128)(2,1)S(1)} %shard_map.70.early), channel_id=1, source_target_pairs={{0,8},{8,0},{16,24},{24,16},{1,9},{9,1},{17,25},{25,17},{2,10},{10... | collective-permute-start | bytes 442376 | tf_op jit(solution)/shard_map/ppermute | solution.py:40
  37.5 0.1 shard_map.73.weights
  37.6 0.0 collective-permute-done.11.refs_0_.far
  37.6 0.7 %shard_map.71.late = bf16[1,9,32,128]{3,2,1,0:T(8,128)(2,1)S(1)} custom-call(bf16[1024,128]{1,0:T(8,128)(2,1)S(1)} %collective-permute-done.11.refs_0_.far, bf16[1024,128]{1,0:T(8,128)(2,1)S(1)} %bitcast.11), custom_call_target="tpu_custom_call" | custom-call | flops 301989888 | bytes 786432 | tf_op jit(solution)/shard_map/pallas_call | solution.py:269
  38.3 1.3 %collective-permute-start.13 = (bf16[1,9,32,128]{3,2,1,0:T(8,128)(2,1)S(1)}, bf16[1,9,32,128]{3,2,1,0:T(8,128)(2,1)S(1)}, u32[]{:S(2)}, u32[]{:S(2)}) collective-permute-start(bf16[1,9,32,128]{3,2,1,0:T(8,128)(2,1)S(1)} %shard_map.71.late), channel_id=1, source_target_pairs={{0,8},{8,0},{16,24},{24,16},{1,9},{9,1},{17,25},{25,17},{2,10},{10... | collective-permute-start | bytes 221192 | tf_op jit(solution)/shard_map/ppermute | solution.py:40
  39.6 2.2 %shard_map.74 = (bf16[256,128]{1,0:T(8,128)(2,1)S(1)}, bf16[256,128]{1,0:T(8,128)(2,1)S(1)}, bf16[256,128]{1,0:T(8,128)(2,1)S(1)}, bf16[256,128]{1,0:T(8,128)(2,1)S(1)}) custom-call(s32[2]{0:T(128)S(1)} %pad_add_fusion.here, bf16[1024,128]{1,0:T(8,128)(2,1)S(1)} %get-tuple-element.14.refs_0_.mid, bf16[1024,128]{1,0:T(8,128)(2,1)S(1)} %collective-permute-done.10.refs_1_.near, ...), custom_call_target="tpu_custom_call" | custom-call | flops 905969664 | bytes 1310720 | tf_op jit(solution)/shard_map/pallas_call | solution.py:298
  41.8 0.0 collective-permute-done.17.refs_5_
  41.8 0.7 %collective-permute-start.14 = (bf16[256,128]{1,0:T(8,128)(2,1)S(1)}, bf16[256,128]{1,0:T(8,128)(2,1)S(1)}, u32[]{:S(2)}, u32[]{:S(2)}) collective-permute-start(bf16[256,128]{1,0:T(8,128)(2,1)S(1)} %get-tuple-element.19), channel_id=1, source_target_pairs={{0,2},{1,3},{2,0},{3,1},{4,6},{5,7},{6,4},{7,5},{8,10},{9,11},{10,... | collective-permute-start | bytes 196616 | tf_op jit(solution)/shard_map/ppermute | solution.py:40
  42.6 0.1 collective-permute-done.13.other_late
  42.7 0.7 %collective-permute-start.15 = (bf16[256,128]{1,0:T(8,128)(2,1)S(1)}, bf16[256,128]{1,0:T(8,128)(2,1)S(1)}, u32[]{:S(2)}, u32[]{:S(2)}) collective-permute-start(bf16[256,128]{1,0:T(8,128)(2,1)S(1)} %get-tuple-element.20), channel_id=1, source_target_pairs={{0,4},{1,5},{2,6},{3,7},{4,0},{5,1},{6,2},{7,3},{8,12},{9,13},{10,... | collective-permute-start | bytes 196616 | tf_op jit(solution)/shard_map/ppermute | solution.py:40
  43.4 0.0 collective-permute-done.12.other_early
  43.4 2.7 %collective-permute-start.16 = (bf16[256,128]{1,0:T(8,128)(2,1)S(1)}, bf16[256,128]{1,0:T(8,128)(2,1)S(1)}, u32[]{:S(2)}, u32[]{:S(2)}) collective-permute-start(bf16[256,128]{1,0:T(8,128)(2,1)S(1)} %get-tuple-element.21), channel_id=1, source_target_pairs={{0,6},{1,7},{2,4},{3,5},{4,2},{5,3},{6,0},{7,1},{8,14},{9,15},{10,... | collective-permute-start | bytes 196616 | tf_op jit(solution)/shard_map/ppermute | solution.py:40
  46.1 0.6 %shard_map.72.own = bf16[3,9,32,128]{3,2,1,0:T(8,128)(2,1)S(1)} custom-call(s32[2]{0:T(128)S(1)} %pad_add_fusion.here, bf16[2,9,32,128]{3,2,1,0:T(8,128)(2,1)S(1)} %shard_map.70.early, bf16[1,9,32,128]{3,2,1,0:T(8,128)(2,1)S(1)} %shard_map.71.late, bf16[2,9,32,128]{3,2,1,0:T(8,128)(2,1)S(1)} %collective-permute-done.12.other_early, ...), custom_call_target="tpu_custom_call" | custom-call | bytes 3686400 | tf_op jit(solution)/shard_map/pallas_call | solution.py:280
  46.7 1.1 %collective-permute-start.21 = (bf16[3,9,32,128]{3,2,1,0:T(8,128)(2,1)S(1)}, bf16[3,9,32,128]{3,2,1,0:T(8,128)(2,1)S(1)}, u32[]{:S(2)}, u32[]{:S(2)}) collective-permute-start(bf16[3,9,32,128]{3,2,1,0:T(8,128)(2,1)S(1)} %shard_map.72.own), channel_id=1, source_target_pairs={{0,16},{8,24},{16,0},{24,8},{1,17},{9,25},{17,1},{25,9},{2,18},{10... | collective-permute-start | bytes 663560 | tf_op jit(solution)/shard_map/ppermute | solution.py:40
  47.8 0.7 %collective-permute-done.16.refs_3_ = bf16[256,128]{1,0:T(8,128)(2,1)S(1)} collective-permute-done((bf16[256,128]{1,0:T(8,128)(2,1)S(1)}, bf16[256,128]{1,0:T(8,128)(2,1)S(1)}, u32[]{:S(2)}, u32[]{:S(2)}) %collective-permute-start.16) | collective-permute-done | bytes 65568 | tf_op jit(solution)/shard_map/ppermute | solution.py:40
  48.5 1.3 %shard_map.75 = (f32[128,1024]{1,0:T(8,128)S(1)}, bf16[128,1024]{1,0:T(8,128)(2,1)S(1)}) custom-call(s32[2]{0:T(128)S(1)} %pad_add_fusion.here, bf16[128,1024]{1,0:T(8,128)(2,1)S(1)} %bitcast.9, bf16[256,128]{1,0:T(8,128)(2,1)S(1)} %get-tuple-element.18.refs_0_, bf16[256,128]{1,0:T(8,128)(2,1)S(1)} %collective-permute-done.14.refs_1_, ...), custom_call_target="tpu_custom_call" | custom-call | flops 34359738368 | bytes 1048576 | tf_op jit(solution)/shard_map/pallas_call | solution.py:308
  49.8 0.1 collective-permute-start.20
  49.9 6.7 %collective-permute-done.21.other = bf16[3,9,32,128]{3,2,1,0:T(8,128)(2,1)S(1)} collective-permute-done((bf16[3,9,32,128]{3,2,1,0:T(8,128)(2,1)S(1)}, bf16[3,9,32,128]{3,2,1,0:T(8,128)(2,1)S(1)}, u32[]{:S(2)}, u32[]{:S(2)}) %collective-permute-start.21) | collective-permute-done | bytes 221216 | tf_op jit(solution)/shard_map/ppermute | solution.py:40
  56.6 0.8 %shard_map.76 = f32[27,32,128]{2,1,0:T(8,128)} custom-call(bf16[3,9,32,128]{3,2,1,0:T(8,128)(2,1)S(1)} %shard_map.72.own, bf16[3,9,32,128]{3,2,1,0:T(8,128)(2,1)S(1)} %collective-permute-done.21.other), custom_call_target="tpu_custom_call" | custom-call | flops 34359738368 | bytes 884736 | tf_op jit(solution)/shard_map/pallas_call | solution.py:287
  57.5 0.8 %add_convert_fusion = bf16[128,1024]{1,0:T(8,128)(2,1)} fusion(f32[128,1024]{1,0:T(8,128)S(1)} %get-tuple-element.23, bf16[128,1024]{1,0:T(8,128)(2,1)S(1)} %collective-permute-done.20), kind=kLoop, calls=%fused_computation | loop fusion | flops 393216 | bytes 1048576 | tf_op jit(solution)/shard_map/convert_element_type | solution.py:317
  (19 shorter events, 0.1 us)
Async XLA Ops:
  0.6 11.9 %collective-permute-start.2 = (bf16[128,1024]{1,0:T(8,128)(2,1)}, bf16[128,1024]{1,0:T(8,128)(2,1)S(1)}, u32[]{:S(2)}, u32[]{:S(2)}) collective-permute-start(bf16[128,1024]{1,0:T(8,128)(2,1)} %bitcast.5), channel_id=1, source_target_pairs={{0,2},{1,3},{2,0},{3,1},{4,6},{5,7},{6,4},{7,5},{8,10},{9,11},{10,... | collective-permute-start | bytes 786440 | tf_op jit(solution)/shard_map/ppermute | solution.py:40
  3.6 11.5 %collective-permute-start.4 = (bf16[128,1024]{1,0:T(8,128)(2,1)}, bf16[128,1024]{1,0:T(8,128)(2,1)S(1)}, u32[]{:S(2)}, u32[]{:S(2)}) collective-permute-start(bf16[128,1024]{1,0:T(8,128)(2,1)} %bitcast.6), channel_id=1, source_target_pairs={{0,4},{1,5},{2,6},{3,7},{4,0},{5,1},{6,2},{7,3},{8,12},{9,13},{10,... | collective-permute-start | bytes 786440 | tf_op jit(solution)/shard_map/ppermute | solution.py:40
  5.2 1.0 %copy-start = (bf16[256,1024]{1,0:T(8,128)(2,1)S(1)}, bf16[256,1024]{1,0:T(8,128)(2,1)}, u32[]{:S(2)}) copy-start(bf16[256,1024]{1,0:T(8,128)(2,1)} %w_out.1) | copy-start | bytes 1572868
  6.3 1.0 %copy-start.1 = (bf16[256,1024]{1,0:T(8,128)(2,1)S(1)}, bf16[256,1024]{1,0:T(8,128)(2,1)}, u32[]{:S(2)}) copy-start(bf16[256,1024]{1,0:T(8,128)(2,1)} %w_in.1) | copy-start | bytes 1572868
  7.3 4.2 %copy-start.2 = (bf16[1,2,64,1024]{3,2,1,0:T(8,128)(2,1)S(1)}, bf16[1,2,64,1024]{3,2,1,0:T(8,128)(2,1)}, u32[]{:S(2)}) copy-start(bf16[1,2,64,1024]{3,2,1,0:T(8,128)(2,1)} %param.5) | copy-start | bytes 786436
  7.9 15.5 %collective-permute-start = (bf16[2,128,1024]{2,1,0:T(8,128)(2,1)S(1)}, bf16[2,128,1024]{2,1,0:T(8,128)(2,1)S(1)}, u32[]{:S(2)}, u32[]{:S(2)}) collective-permute-start(bf16[2,128,1024]{2,1,0:T(8,128)(2,1)S(1)} %shard_map.68.local), channel_id=1, source_target_pairs={{0,8},{2,16},{4,24},{10,2},{14,18},{8,26},{16,4},{20,12},{22,28},{... | collective-permute-start | bytes 1572872 | tf_op jit(solution)/shard_map/ppermute | solution.py:89
  11.5 4.0 %collective-permute-start.1 = (bf16[128,1024]{1,0:T(8,128)(2,1)S(1)}, bf16[128,1024]{1,0:T(8,128)(2,1)S(1)}, u32[]{:S(2)}, u32[]{:S(2)}) collective-permute-start(bf16[128,1024]{1,0:T(8,128)(2,1)S(1)} %bitcast.7), channel_id=1, source_target_pairs={{0,1},{1,0},{2,3},{3,2},{4,5},{5,4},{6,7},{7,6},{8,9},{9,8},{10,11... | collective-permute-start | bytes 786440 | tf_op jit(solution)/shard_map/ppermute | solution.py:40
  12.6 8.6 %collective-permute-start.6 = (bf16[64,1024]{1,0:T(8,128)(2,1)S(1)}, bf16[64,1024]{1,0:T(8,128)(2,1)S(1)}, u32[]{:S(2)}, u32[]{:S(2)}) collective-permute-start(bf16[64,1024]{1,0:T(8,128)(2,1)S(1)} %slice.8), channel_id=1, source_target_pairs={{0,4},{1,5},{2,6},{3,7},{4,0},{5,1},{6,2},{7,3},{8,12},{9,13},{10,... | collective-permute-start | bytes 393224 | tf_op jit(solution)/shard_map/ppermute | solution.py:40
  15.1 18.5 %copy-start.4 = (bf16[1,16,64,128]{3,2,1,0:T(8,128)(2,1)S(1)}, bf16[1,16,64,128]{3,2,1,0:T(8,128)(2,1)}, u32[]{:S(2)}) copy-start(bf16[1,16,64,128]{3,2,1,0:T(8,128)(2,1)} %param.6) | copy-start | bytes 786436
  15.1 6.0 %collective-permute-start.8 = (bf16[64,1024]{1,0:T(8,128)(2,1)S(1)}, bf16[64,1024]{1,0:T(8,128)(2,1)S(1)}, u32[]{:S(2)}, u32[]{:S(2)}) collective-permute-start(bf16[64,1024]{1,0:T(8,128)(2,1)S(1)} %slice.9), channel_id=1, source_target_pairs={{0,2},{1,3},{2,0},{3,1},{4,6},{5,7},{6,4},{7,5},{8,10},{9,11},{10,... | collective-permute-start | bytes 393224 | tf_op jit(solution)/shard_map/ppermute | solution.py:40
  15.2 8.2 %collective-permute-start.3 = (bf16[128,1024]{1,0:T(8,128)(2,1)S(1)}, bf16[128,1024]{1,0:T(8,128)(2,1)S(1)}, u32[]{:S(2)}, u32[]{:S(2)}) collective-permute-start(bf16[128,1024]{1,0:T(8,128)(2,1)S(1)} %collective-permute-done.2.refs_2_), channel_id=1, source_target_pairs={{0,1},{1,0},{2,3},{3,2},{4,5},{5,4},{6,7},{7,6},{8,9},{9,8},{10,11... | collective-permute-start | bytes 786440 | tf_op jit(solution)/shard_map/ppermute | solution.py:40
  15.5 7.9 %collective-permute-start.5 = (bf16[128,1024]{1,0:T(8,128)(2,1)S(1)}, bf16[128,1024]{1,0:T(8,128)(2,1)S(1)}, u32[]{:S(2)}, u32[]{:S(2)}) collective-permute-start(bf16[128,1024]{1,0:T(8,128)(2,1)S(1)} %collective-permute-done.4.refs_4_), channel_id=1, source_target_pairs={{0,1},{1,0},{2,3},{3,2},{4,5},{5,4},{6,7},{7,6},{8,9},{9,8},{10,11... | collective-permute-start | bytes 786440 | tf_op jit(solution)/shard_map/ppermute | solution.py:40
  21.2 2.2 %collective-permute-start.7 = (bf16[64,1024]{1,0:T(8,128)(2,1)S(1)}, bf16[64,1024]{1,0:T(8,128)(2,1)S(1)}, u32[]{:S(2)}, u32[]{:S(2)}) collective-permute-start(bf16[64,1024]{1,0:T(8,128)(2,1)S(1)} %collective-permute-done.6.refs_6_), channel_id=1, source_target_pairs={{0,1},{1,0},{2,3},{3,2},{4,5},{5,4},{6,7},{7,6},{8,9},{9,8},{10,11... | collective-permute-start | bytes 393224 | tf_op jit(solution)/shard_map/ppermute | solution.py:40
  21.2 2.2 %collective-permute-start.9 = (bf16[64,1024]{1,0:T(8,128)(2,1)S(1)}, bf16[64,1024]{1,0:T(8,128)(2,1)S(1)}, u32[]{:S(2)}, u32[]{:S(2)}) collective-permute-start(bf16[64,1024]{1,0:T(8,128)(2,1)S(1)} %collective-permute-done.8.refs_8_), channel_id=1, source_target_pairs={{0,1},{1,0},{2,3},{3,2},{4,5},{5,4},{6,7},{7,6},{8,9},{9,8},{10,11... | collective-permute-start | bytes 393224 | tf_op jit(solution)/shard_map/ppermute | solution.py:40
  24.9 8.7 %collective-permute-start.10 = (bf16[1024,128]{1,0:T(8,128)(2,1)S(1)}, bf16[1024,128]{1,0:T(8,128)(2,1)S(1)}, u32[]{:S(2)}, u32[]{:S(2)}) collective-permute-start(bf16[1024,128]{1,0:T(8,128)(2,1)S(1)} %get-tuple-element.14.refs_0_.mid), channel_id=1, source_target_pairs={{0,8},{8,0},{16,24},{24,16},{1,9},{9,1},{17,25},{25,17},{2,10},{10... | collective-permute-start | bytes 786440 | tf_op jit(solution)/shard_map/ppermute | solution.py:40
  27.5 10.1 %collective-permute-start.11 = (bf16[1024,128]{1,0:T(8,128)(2,1)S(1)}, bf16[1024,128]{1,0:T(8,128)(2,1)S(1)}, u32[]{:S(2)}, u32[]{:S(2)}) collective-permute-start(bf16[1024,128]{1,0:T(8,128)(2,1)S(1)} %get-tuple-element.14.refs_0_.mid), channel_id=1, source_target_pairs={{8,16},{16,8},{9,17},{17,9},{10,18},{18,10},{11,19},{19,11},{12,20... | collective-permute-start | bytes 786440 | tf_op jit(solution)/shard_map/ppermute | solution.py:227
  28.2 13.7 %collective-permute-start.17 = (bf16[128,1024]{1,0:T(8,128)(2,1)S(1)}, bf16[128,1024]{1,0:T(8,128)(2,1)S(1)}, u32[]{:S(2)}, u32[]{:S(2)}) collective-permute-start(bf16[128,1024]{1,0:T(8,128)(2,1)S(1)} %get-tuple-element.22.refs_4_), channel_id=1, source_target_pairs={{0,2},{1,3},{2,0},{3,1},{4,6},{5,7},{6,4},{7,5},{8,10},{9,11},{10,... | collective-permute-start | bytes 786440 | tf_op jit(solution)/shard_map/ppermute | solution.py:40
  28.2 18.4 %collective-permute-start.18 = (bf16[128,1024]{1,0:T(8,128)(2,1)S(1)}, bf16[128,1024]{1,0:T(8,128)(2,1)S(1)}, u32[]{:S(2)}, u32[]{:S(2)}) collective-permute-start(bf16[128,1024]{1,0:T(8,128)(2,1)S(1)} %get-tuple-element.22.refs_4_), channel_id=1, source_target_pairs={{0,4},{1,5},{2,6},{3,7},{4,0},{5,1},{6,2},{7,3},{8,12},{9,13},{10,... | collective-permute-start | bytes 786440 | tf_op jit(solution)/shard_map/ppermute | solution.py:40
  29.7 18.1 %collective-permute-start.19 = (bf16[128,1024]{1,0:T(8,128)(2,1)S(1)}, bf16[128,1024]{1,0:T(8,128)(2,1)S(1)}, u32[]{:S(2)}, u32[]{:S(2)}) collective-permute-start(bf16[128,1024]{1,0:T(8,128)(2,1)S(1)} %get-tuple-element.22.refs_4_), channel_id=1, source_target_pairs={{0,6},{1,7},{2,4},{3,5},{4,2},{5,3},{6,0},{7,1},{8,14},{9,15},{10,... | collective-permute-start | bytes 786440 | tf_op jit(solution)/shard_map/ppermute | solution.py:40
  33.6 3.9 %copy-start.3 = (bf16[27,32,128]{2,1,0:T(8,128)(2,1)S(1)}, bf16[27,32,128]{2,1,0:T(8,128)(2,1)}, u32[]{:S(2)}) copy-start(bf16[27,32,128]{2,1,0:T(8,128)(2,1)} %kernel) | copy-start | bytes 663556
  34.6 8.8 %collective-permute-start.12 = (bf16[2,9,32,128]{3,2,1,0:T(8,128)(2,1)S(1)}, bf16[2,9,32,128]{3,2,1,0:T(8,128)(2,1)S(1)}, u32[]{:S(2)}, u32[]{:S(2)}) collective-permute-start(bf16[2,9,32,128]{3,2,1,0:T(8,128)(2,1)S(1)} %shard_map.70.early), channel_id=1, source_target_pairs={{0,8},{8,0},{16,24},{24,16},{1,9},{9,1},{17,25},{25,17},{2,10},{10... | collective-permute-start | bytes 442376 | tf_op jit(solution)/shard_map/ppermute | solution.py:40
  38.3 4.4 %collective-permute-start.13 = (bf16[1,9,32,128]{3,2,1,0:T(8,128)(2,1)S(1)}, bf16[1,9,32,128]{3,2,1,0:T(8,128)(2,1)S(1)}, u32[]{:S(2)}, u32[]{:S(2)}) collective-permute-start(bf16[1,9,32,128]{3,2,1,0:T(8,128)(2,1)S(1)} %shard_map.71.late), channel_id=1, source_target_pairs={{0,8},{8,0},{16,24},{24,16},{1,9},{9,1},{17,25},{25,17},{2,10},{10... | collective-permute-start | bytes 221192 | tf_op jit(solution)/shard_map/ppermute | solution.py:40
  41.8 5.9 %collective-permute-start.14 = (bf16[256,128]{1,0:T(8,128)(2,1)S(1)}, bf16[256,128]{1,0:T(8,128)(2,1)S(1)}, u32[]{:S(2)}, u32[]{:S(2)}) collective-permute-start(bf16[256,128]{1,0:T(8,128)(2,1)S(1)} %get-tuple-element.19), channel_id=1, source_target_pairs={{0,2},{1,3},{2,0},{3,1},{4,6},{5,7},{6,4},{7,5},{8,10},{9,11},{10,... | collective-permute-start | bytes 196616 | tf_op jit(solution)/shard_map/ppermute | solution.py:40
  42.7 5.1 %collective-permute-start.15 = (bf16[256,128]{1,0:T(8,128)(2,1)S(1)}, bf16[256,128]{1,0:T(8,128)(2,1)S(1)}, u32[]{:S(2)}, u32[]{:S(2)}) collective-permute-start(bf16[256,128]{1,0:T(8,128)(2,1)S(1)} %get-tuple-element.20), channel_id=1, source_target_pairs={{0,4},{1,5},{2,6},{3,7},{4,0},{5,1},{6,2},{7,3},{8,12},{9,13},{10,... | collective-permute-start | bytes 196616 | tf_op jit(solution)/shard_map/ppermute | solution.py:40
  43.4 5.2 %collective-permute-start.16 = (bf16[256,128]{1,0:T(8,128)(2,1)S(1)}, bf16[256,128]{1,0:T(8,128)(2,1)S(1)}, u32[]{:S(2)}, u32[]{:S(2)}) collective-permute-start(bf16[256,128]{1,0:T(8,128)(2,1)S(1)} %get-tuple-element.21), channel_id=1, source_target_pairs={{0,6},{1,7},{2,4},{3,5},{4,2},{5,3},{6,0},{7,1},{8,14},{9,15},{10,... | collective-permute-start | bytes 196616 | tf_op jit(solution)/shard_map/ppermute | solution.py:40
  46.7 10.0 %collective-permute-start.21 = (bf16[3,9,32,128]{3,2,1,0:T(8,128)(2,1)S(1)}, bf16[3,9,32,128]{3,2,1,0:T(8,128)(2,1)S(1)}, u32[]{:S(2)}, u32[]{:S(2)}) collective-permute-start(bf16[3,9,32,128]{3,2,1,0:T(8,128)(2,1)S(1)} %shard_map.72.own), channel_id=1, source_target_pairs={{0,16},{8,24},{16,0},{24,8},{1,17},{9,25},{17,1},{25,9},{2,18},{10... | collective-permute-start | bytes 663560 | tf_op jit(solution)/shard_map/ppermute | solution.py:40
  49.8 7.6 %collective-permute-start.20 = (bf16[128,1024]{1,0:T(8,128)(2,1)S(1)}, bf16[128,1024]{1,0:T(8,128)(2,1)S(1)}, u32[]{:S(2)}, u32[]{:S(2)}) collective-permute-start(bf16[128,1024]{1,0:T(8,128)(2,1)S(1)} %get-tuple-element.24), channel_id=1, source_target_pairs={{0,1},{1,0},{2,3},{3,2},{4,5},{5,4},{6,7},{7,6},{8,9},{9,8},{10,11... | collective-permute-start | bytes 786440 | tf_op jit(solution)/shard_map/ppermute | solution.py:40

commit v4 on v3

--- a/solution.py
+++ b/solution.py
@@ -277,12 +277,13 @@
         )(*planes, pre)
         for planes in ((mid, near), (far,))
     )
+    w_blocks = [w_cols] + [swap(w_cols, "height", 2 * m) for m in (1, 2, 3)]
     pair = call(
         pair_body,
         jax.ShapeDtypeStruct((3, 9, group, chans), BF16),
         4,
         nbytes=100 * 9 * group * chans,
-    )(here, early, late, swap(early, "depth", 1), swap(late, "depth", 1))
+    )(here, order(early, *w_blocks), late, swap(early, "depth", 1), swap(late, "depth", 1))
     total_cells = cells * lax.axis_size("depth")
     kernel_grad = call(
         functools.partial(total_body, float(total_cells) ** -0.5),
@@ -293,7 +294,6 @@
         nbytes=24 * 9 * group * chans,
     )(pair, swap(pair, "depth", 2))
 
-    w_blocks = [w_cols] + [swap(w_cols, "height", 2 * m) for m in (1, 2, 3)]
     chip_cells = 2 * block
     back = call(
         functools.partial(back_body, wid),

time: 58.5 us -> 57 us (0.974); the launches traced: 58.2 us -> 55.9 us
  waiting for transfers between devices: 16.6 us -> 11.6 us
  starting transfers between devices: 29.1 us -> 31.8 us
    ppermute x20, waiting for transfers between devices: 14.9 us -> 9.89 us  [swap(): return lax.ppermute(x, axis, [(i, i ^ mask) for i in range(n)])]
    ppermute x20, starting transfers between devices: 24.9 us -> 27.6 us  [swap(): return lax.ppermute(x, axis, [(i, i ^ mask) for i in range(n)])]
  transfers between devices with their start and end apart: 22 -> 22, of which waited for: 6 -> 5; matrix products, arithmetic and copies ran while one was open for 0% -> 0% of each run, Pallas kernels for 13% -> 13%
where the time goes in v4:
time: 57 us; the launch traced here: 55.9 us
  starting transfers between devices  31.8 us (56%)
  waiting for transfers between devices  11.6 us (20%)
  Pallas kernels  8.75 us (15%)
  local copies, waits for them, and re-layouts  2.12 us (4%)
  other arithmetic  0.84 us (1%)
  between operations  0.8 us (1%)
    ppermute x20, starting transfers between devices, swap(): return lax.ppermute(x, axis, [(i, i ^ mask) for i in range(n)])  27.6 us
    ppermute x20, waiting for transfers between devices, swap(): return lax.ppermute(x, axis, [(i, i ^ mask) for i in range(n)])  9.89 us
    ppermute x1, starting transfers between devices, fetch(): return lax.ppermute(mine, ('depth', 'height'), pairs)  3.51 us
    pallas_call x1, Pallas kernels, fast(): call(functools.partial(back_body, wid), [jax.ShapeDtypeStruct((chip_cells...  2.21 us
    unnamed x10, local copies, waits for them, and re-layouts  2.1 us
    ppermute x1, waiting for transfers between devices, fetch(): return lax.ppermute(mine, ('depth', 'height'), pairs)  1.71 us
    pallas_call x2, Pallas kernels, fast(): call(functools.partial(kgrad_body, wid, group, len(planes)), jax.ShapeDty...  1.64 us
    pallas_call x1, Pallas kernels, fast(): call(functools.partial(mid_body, places, block), [jax.ShapeDtypeStruct((c...  1.44 us
  transfers between devices with their start and end apart: 22, of which 5 were waited for; matrix products, arithmetic and copies ran while one was open for 0% of the time, Pallas kernels for 13%

profile of v4, /device:TPU:0, one launch (start us, length us, event | category | flops | bytes accessed | tf_op | source)
XLA Modules:
  0.0 55.9 jit_solution(5175523417174927143)
XLA Ops:
  0.6 3.0 %collective-permute-start.2 = (bf16[128,1024]{1,0:T(8,128)(2,1)}, bf16[128,1024]{1,0:T(8,128)(2,1)S(1)}, u32[]{:S(2)}, u32[]{:S(2)}) collective-permute-start(bf16[128,1024]{1,0:T(8,128)(2,1)} %bitcast.5), channel_id=1, source_target_pairs={{0,2},{1,3},{2,0},{3,1},{4,6},{5,7},{6,4},{7,5},{8,10},{9,11},{10,... | collective-permute-start | bytes 786440 | tf_op jit(solution)/shard_map/ppermute | solution.py:40
  3.6 1.5 %collective-permute-start.4 = (bf16[128,1024]{1,0:T(8,128)(2,1)}, bf16[128,1024]{1,0:T(8,128)(2,1)S(1)}, u32[]{:S(2)}, u32[]{:S(2)}) collective-permute-start(bf16[128,1024]{1,0:T(8,128)(2,1)} %bitcast.6), channel_id=1, source_target_pairs={{0,4},{1,5},{2,6},{3,7},{4,0},{5,1},{6,2},{7,3},{8,12},{9,13},{10,... | collective-permute-start | bytes 786440 | tf_op jit(solution)/shard_map/ppermute | solution.py:40
  5.2 0.1 pad_add_fusion.here
  5.2 1.0 %copy-done = bf16[256,1024]{1,0:T(8,128)(2,1)S(1)} copy-done((bf16[256,1024]{1,0:T(8,128)(2,1)S(1)}, bf16[256,1024]{1,0:T(8,128)(2,1)}, u32[]{:S(2)}) %copy-start) | copy-done | bytes 524312
  6.3 1.0 %copy-done.1 = bf16[256,1024]{1,0:T(8,128)(2,1)S(1)} copy-done((bf16[256,1024]{1,0:T(8,128)(2,1)S(1)}, bf16[256,1024]{1,0:T(8,128)(2,1)}, u32[]{:S(2)}) %copy-start.1) | copy-done | bytes 524312
  7.3 0.6 %shard_map.68.local = bf16[2,128,1024]{2,1,0:T(8,128)(2,1)S(1)} custom-call(s32[2]{0:T(128)S(1)} %pad_add_fusion.here, bf16[256,1024]{1,0:T(8,128)(2,1)S(1)} %copy-done, bf16[256,1024]{1,0:T(8,128)(2,1)S(1)} %copy-done.1), custom_call_target="tpu_custom_call" | custom-call | bytes 1572864 | tf_op jit(solution)/shard_map/pallas_call | solution.py:245
  7.9 3.5 %collective-permute-start = (bf16[2,128,1024]{2,1,0:T(8,128)(2,1)S(1)}, bf16[2,128,1024]{2,1,0:T(8,128)(2,1)S(1)}, u32[]{:S(2)}, u32[]{:S(2)}) collective-permute-start(bf16[2,128,1024]{2,1,0:T(8,128)(2,1)S(1)} %shard_map.68.local), channel_id=1, source_target_pairs={{0,8},{2,16},{4,24},{10,2},{14,18},{8,26},{16,4},{20,12},{22,28},{... | collective-permute-start | bytes 1572872 | tf_op jit(solution)/shard_map/ppermute | solution.py:89
  11.5 1.1 %collective-permute-start.1 = (bf16[128,1024]{1,0:T(8,128)(2,1)S(1)}, bf16[128,1024]{1,0:T(8,128)(2,1)S(1)}, u32[]{:S(2)}, u32[]{:S(2)}) collective-permute-start(bf16[128,1024]{1,0:T(8,128)(2,1)S(1)} %bitcast.7), channel_id=1, source_target_pairs={{0,1},{1,0},{2,3},{3,2},{4,5},{5,4},{6,7},{7,6},{8,9},{9,8},{10,11... | collective-permute-start | bytes 786440 | tf_op jit(solution)/shard_map/ppermute | solution.py:40
  12.6 0.0 collective-permute-done.2.refs_2_
  12.6 2.5 %collective-permute-start.6 = (bf16[64,1024]{1,0:T(8,128)(2,1)S(1)}, bf16[64,1024]{1,0:T(8,128)(2,1)S(1)}, u32[]{:S(2)}, u32[]{:S(2)}) collective-permute-start(bf16[64,1024]{1,0:T(8,128)(2,1)S(1)} %slice.8), channel_id=1, source_target_pairs={{0,4},{1,5},{2,6},{3,7},{4,0},{5,1},{6,2},{7,3},{8,12},{9,13},{10,... | collective-permute-start | bytes 393224 | tf_op jit(solution)/shard_map/ppermute | solution.py:40
  15.1 0.2 collective-permute-start.3
  15.3 0.3 collective-permute-start.5
  15.6 0.0 copy-start.3
  15.7 0.0 collective-permute-done.1.refs_1_
  15.7 0.1 collective-permute-start.8
  15.7 5.4 %collective-permute-done.6.refs_6_ = bf16[64,1024]{1,0:T(8,128)(2,1)S(1)} collective-permute-done((bf16[64,1024]{1,0:T(8,128)(2,1)S(1)}, bf16[64,1024]{1,0:T(8,128)(2,1)S(1)}, u32[]{:S(2)}, u32[]{:S(2)}) %collective-permute-start.6) | collective-permute-done | bytes 131104 | tf_op jit(solution)/shard_map/ppermute | solution.py:40
  21.2 0.2 collective-permute-done.8.refs_8_
  21.3 0.4 collective-permute-start.9
  21.7 1.7 %collective-permute-done.fetched = bf16[2,128,1024]{2,1,0:T(8,128)(2,1)S(1)} collective-permute-done((bf16[2,128,1024]{2,1,0:T(8,128)(2,1)S(1)}, bf16[2,128,1024]{2,1,0:T(8,128)(2,1)S(1)}, u32[]{:S(2)}, u32[]{:S(2)}) %collective-permute-start) | collective-permute-done | bytes 524320 | tf_op jit(solution)/shard_map/ppermute | solution.py:89
  23.4 0.0 collective-permute-done.3.refs_3_
  23.4 0.0 collective-permute-done.5.refs_5_
  23.4 0.0 collective-permute-done.7.refs_7_
  23.4 0.0 collective-permute-done.9.refs_9_
  23.4 1.4 %shard_map.69 = (bf16[1024,128]{1,0:T(8,128)(2,1)S(1)}, bf16[128,1024]{1,0:T(8,128)(2,1)S(1)}) custom-call(s32[2]{0:T(128)S(1)} %pad_add_fusion.here, bf16[2,128,1024]{2,1,0:T(8,128)(2,1)S(1)} %shard_map.68.local, bf16[2,128,1024]{2,1,0:T(8,128)(2,1)S(1)} %collective-permute-done.fetched, bf16[128,1024]{1,0:T(8,128)(2,1)S(1)} %bitcast.8, ...), custom_call_target="tpu_custom_call" | custom-call | flops 268435456 | bytes 2097152 | tf_op jit(solution)/shard_map/pallas_call | solution.py:258
  24.9 2.6 %collective-permute-start.10 = (bf16[1024,128]{1,0:T(8,128)(2,1)S(1)}, bf16[1024,128]{1,0:T(8,128)(2,1)S(1)}, u32[]{:S(2)}, u32[]{:S(2)}) collective-permute-start(bf16[1024,128]{1,0:T(8,128)(2,1)S(1)} %get-tuple-element.15.refs_0_.mid), channel_id=1, source_target_pairs={{0,8},{8,0},{16,24},{24,16},{1,9},{9,1},{17,25},{25,17},{2,10},{10... | collective-permute-start | bytes 786440 | tf_op jit(solution)/shard_map/ppermute | solution.py:40
  27.5 0.7 %collective-permute-start.14 = (bf16[1024,128]{1,0:T(8,128)(2,1)S(1)}, bf16[1024,128]{1,0:T(8,128)(2,1)S(1)}, u32[]{:S(2)}, u32[]{:S(2)}) collective-permute-start(bf16[1024,128]{1,0:T(8,128)(2,1)S(1)} %get-tuple-element.15.refs_0_.mid), channel_id=1, source_target_pairs={{8,16},{16,8},{9,17},{17,9},{10,18},{18,10},{11,19},{19,11},{12,20... | collective-permute-start | bytes 786440 | tf_op jit(solution)/shard_map/ppermute | solution.py:227
  28.2 0.0 copy-start.4
  28.2 0.1 collective-permute-start.11
  28.3 1.5 %collective-permute-start.12 = (bf16[128,1024]{1,0:T(8,128)(2,1)S(1)}, bf16[128,1024]{1,0:T(8,128)(2,1)S(1)}, u32[]{:S(2)}, u32[]{:S(2)}) collective-permute-start(bf16[128,1024]{1,0:T(8,128)(2,1)S(1)} %get-tuple-element.16.refs_4_), channel_id=1, source_target_pairs={{0,4},{1,5},{2,6},{3,7},{4,0},{5,1},{6,2},{7,3},{8,12},{9,13},{10,... | collective-permute-start | bytes 786440 | tf_op jit(solution)/shard_map/ppermute | solution.py:40
  29.7 2.0 %collective-permute-start.13 = (bf16[128,1024]{1,0:T(8,128)(2,1)S(1)}, bf16[128,1024]{1,0:T(8,128)(2,1)S(1)}, u32[]{:S(2)}, u32[]{:S(2)}) collective-permute-start(bf16[128,1024]{1,0:T(8,128)(2,1)S(1)} %get-tuple-element.16.refs_4_), channel_id=1, source_target_pairs={{0,6},{1,7},{2,4},{3,5},{4,2},{5,3},{6,0},{7,1},{8,14},{9,15},{10,... | collective-permute-start | bytes 786440 | tf_op jit(solution)/shard_map/ppermute | solution.py:40
  31.7 0.1 shard_map.73.weights
  31.9 1.7 %collective-permute-done.10.refs_1_.near = bf16[1024,128]{1,0:T(8,128)(2,1)S(1)} collective-permute-done((bf16[1024,128]{1,0:T(8,128)(2,1)S(1)}, bf16[1024,128]{1,0:T(8,128)(2,1)S(1)}, u32[]{:S(2)}, u32[]{:S(2)}) %collective-permute-start.10) | collective-permute-done | bytes 262176 | tf_op jit(solution)/shard_map/ppermute | solution.py:40
  33.6 1.0 %shard_map.70.early = bf16[2,9,32,128]{3,2,1,0:T(8,128)(2,1)S(1)} custom-call(bf16[1024,128]{1,0:T(8,128)(2,1)S(1)} %get-tuple-element.15.refs_0_.mid, bf16[1024,128]{1,0:T(8,128)(2,1)S(1)} %collective-permute-done.10.refs_1_.near, bf16[1024,128]{1,0:T(8,128)(2,1)S(1)} %bitcast.10), custom_call_target="tpu_custom_call" | custom-call | flops 603979776 | bytes 786432 | tf_op jit(solution)/shard_map/pallas_call | solution.py:269
  34.6 3.0 %collective-permute-start.15 = (bf16[2,9,32,128]{3,2,1,0:T(8,128)(2,1)S(1)}, bf16[2,9,32,128]{3,2,1,0:T(8,128)(2,1)S(1)}, u32[]{:S(2)}, u32[]{:S(2)}) collective-permute-start(bf16[2,9,32,128]{3,2,1,0:T(8,128)(2,1)S(1)} %shard_map.70.early), channel_id=1, source_target_pairs={{0,8},{8,0},{16,24},{24,16},{1,9},{9,1},{17,25},{25,17},{2,10},{10... | collective-permute-start | bytes 442376 | tf_op jit(solution)/shard_map/ppermute | solution.py:40
  37.6 0.7 %shard_map.71.late = bf16[1,9,32,128]{3,2,1,0:T(8,128)(2,1)S(1)} custom-call(bf16[1024,128]{1,0:T(8,128)(2,1)S(1)} %collective-permute-done.14.refs_0_.far, bf16[1024,128]{1,0:T(8,128)(2,1)S(1)} %bitcast.11), custom_call_target="tpu_custom_call" | custom-call | flops 301989888 | bytes 786432 | tf_op jit(solution)/shard_map/pallas_call | solution.py:269
  38.3 1.3 %collective-permute-start.16 = (bf16[1,9,32,128]{3,2,1,0:T(8,128)(2,1)S(1)}, bf16[1,9,32,128]{3,2,1,0:T(8,128)(2,1)S(1)}, u32[]{:S(2)}, u32[]{:S(2)}) collective-permute-start(bf16[1,9,32,128]{3,2,1,0:T(8,128)(2,1)S(1)} %shard_map.71.late), channel_id=1, source_target_pairs={{0,8},{8,0},{16,24},{24,16},{1,9},{9,1},{17,25},{25,17},{2,10},{10... | collective-permute-start | bytes 221192 | tf_op jit(solution)/shard_map/ppermute | solution.py:40
  39.6 2.2 %shard_map.74 = (bf16[256,128]{1,0:T(8,128)(2,1)S(1)}, bf16[256,128]{1,0:T(8,128)(2,1)S(1)}, bf16[256,128]{1,0:T(8,128)(2,1)S(1)}, bf16[256,128]{1,0:T(8,128)(2,1)S(1)}) custom-call(s32[2]{0:T(128)S(1)} %pad_add_fusion.here, bf16[1024,128]{1,0:T(8,128)(2,1)S(1)} %get-tuple-element.15.refs_0_.mid, bf16[1024,128]{1,0:T(8,128)(2,1)S(1)} %collective-permute-done.10.refs_1_.near, ...), custom_call_target="tpu_custom_call" | custom-call | flops 905969664 | bytes 1310720 | tf_op jit(solution)/shard_map/pallas_call | solution.py:298
  41.8 0.0 collective-permute-done.11.refs_5_
  41.8 0.8 %collective-permute-start.17 = (bf16[256,128]{1,0:T(8,128)(2,1)S(1)}, bf16[256,128]{1,0:T(8,128)(2,1)S(1)}, u32[]{:S(2)}, u32[]{:S(2)}) collective-permute-start(bf16[256,128]{1,0:T(8,128)(2,1)S(1)} %get-tuple-element.22), channel_id=1, source_target_pairs={{0,2},{1,3},{2,0},{3,1},{4,6},{5,7},{6,4},{7,5},{8,10},{9,11},{10,... | collective-permute-start | bytes 196616 | tf_op jit(solution)/shard_map/ppermute | solution.py:40
  42.6 0.0 collective-permute-start.18
  42.6 2.8 %collective-permute-start.19 = (bf16[256,128]{1,0:T(8,128)(2,1)S(1)}, bf16[256,128]{1,0:T(8,128)(2,1)S(1)}, u32[]{:S(2)}, u32[]{:S(2)}) collective-permute-start(bf16[256,128]{1,0:T(8,128)(2,1)S(1)} %get-tuple-element.24), channel_id=1, source_target_pairs={{0,6},{1,7},{2,4},{3,5},{4,2},{5,3},{6,0},{7,1},{8,14},{9,15},{10,... | collective-permute-start | bytes 196616 | tf_op jit(solution)/shard_map/ppermute | solution.py:40
  45.4 0.6 %shard_map.72.own = bf16[3,9,32,128]{3,2,1,0:T(8,128)(2,1)S(1)} custom-call(s32[2]{0:T(128)S(1)} %pad_add_fusion.here, bf16[2,9,32,128]{3,2,1,0:T(8,128)(2,1)S(1)} %shard_map.70.early, bf16[1,9,32,128]{3,2,1,0:T(8,128)(2,1)S(1)} %shard_map.71.late, bf16[2,9,32,128]{3,2,1,0:T(8,128)(2,1)S(1)} %collective-permute-done.15.other_early, ...), custom_call_target="tpu_custom_call" | custom-call | bytes 3686400 | tf_op jit(solution)/shard_map/pallas_call | solution.py:281
  46.0 4.4 %collective-permute-start.21 = (bf16[3,9,32,128]{3,2,1,0:T(8,128)(2,1)S(1)}, bf16[3,9,32,128]{3,2,1,0:T(8,128)(2,1)S(1)}, u32[]{:S(2)}, u32[]{:S(2)}) collective-permute-start(bf16[3,9,32,128]{3,2,1,0:T(8,128)(2,1)S(1)} %shard_map.72.own), channel_id=1, source_target_pairs={{0,16},{8,24},{16,0},{24,8},{1,17},{9,25},{17,1},{25,9},{2,18},{10... | collective-permute-start | bytes 663560 | tf_op jit(solution)/shard_map/ppermute | solution.py:40
  50.4 1.3 %shard_map.75 = (f32[128,1024]{1,0:T(8,128)S(1)}, bf16[128,1024]{1,0:T(8,128)(2,1)S(1)}) custom-call(s32[2]{0:T(128)S(1)} %pad_add_fusion.here, bf16[128,1024]{1,0:T(8,128)(2,1)S(1)} %bitcast.9, bf16[256,128]{1,0:T(8,128)(2,1)S(1)} %get-tuple-element.21.refs_0_, bf16[256,128]{1,0:T(8,128)(2,1)S(1)} %collective-permute-done.17.refs_1_, ...), custom_call_target="tpu_custom_call" | custom-call | flops 34359738368 | bytes 1048576 | tf_op jit(solution)/shard_map/pallas_call | solution.py:308
  51.7 0.1 collective-permute-start.20
  51.8 2.5 %collective-permute-done.21.other = bf16[3,9,32,128]{3,2,1,0:T(8,128)(2,1)S(1)} collective-permute-done((bf16[3,9,32,128]{3,2,1,0:T(8,128)(2,1)S(1)}, bf16[3,9,32,128]{3,2,1,0:T(8,128)(2,1)S(1)}, u32[]{:S(2)}, u32[]{:S(2)}) %collective-permute-start.21) | collective-permute-done | bytes 221216 | tf_op jit(solution)/shard_map/ppermute | solution.py:40
  54.3 0.8 %shard_map.76 = f32[27,32,128]{2,1,0:T(8,128)} custom-call(bf16[3,9,32,128]{3,2,1,0:T(8,128)(2,1)S(1)} %shard_map.72.own, bf16[3,9,32,128]{3,2,1,0:T(8,128)(2,1)S(1)} %collective-permute-done.21.other), custom_call_target="tpu_custom_call" | custom-call | flops 34359738368 | bytes 884736 | tf_op jit(solution)/shard_map/pallas_call | solution.py:288
  55.1 0.8 %add_convert_fusion = bf16[128,1024]{1,0:T(8,128)(2,1)} fusion(f32[128,1024]{1,0:T(8,128)S(1)} %get-tuple-element.25, bf16[128,1024]{1,0:T(8,128)(2,1)S(1)} %collective-permute-done.20), kind=kLoop, calls=%fused_computation | loop fusion | flops 393216 | bytes 1048576 | tf_op jit(solution)/shard_map/convert_element_type | solution.py:317
  (19 shorter events, 0.1 us)
Async XLA Ops:
  0.6 11.9 %collective-permute-start.2 = (bf16[128,1024]{1,0:T(8,128)(2,1)}, bf16[128,1024]{1,0:T(8,128)(2,1)S(1)}, u32[]{:S(2)}, u32[]{:S(2)}) collective-permute-start(bf16[128,1024]{1,0:T(8,128)(2,1)} %bitcast.5), channel_id=1, source_target_pairs={{0,2},{1,3},{2,0},{3,1},{4,6},{5,7},{6,4},{7,5},{8,10},{9,11},{10,... | collective-permute-start | bytes 786440 | tf_op jit(solution)/shard_map/ppermute | solution.py:40
  3.6 11.7 %collective-permute-start.4 = (bf16[128,1024]{1,0:T(8,128)(2,1)}, bf16[128,1024]{1,0:T(8,128)(2,1)S(1)}, u32[]{:S(2)}, u32[]{:S(2)}) collective-permute-start(bf16[128,1024]{1,0:T(8,128)(2,1)} %bitcast.6), channel_id=1, source_target_pairs={{0,4},{1,5},{2,6},{3,7},{4,0},{5,1},{6,2},{7,3},{8,12},{9,13},{10,... | collective-permute-start | bytes 786440 | tf_op jit(solution)/shard_map/ppermute | solution.py:40
  5.2 1.0 %copy-start = (bf16[256,1024]{1,0:T(8,128)(2,1)S(1)}, bf16[256,1024]{1,0:T(8,128)(2,1)}, u32[]{:S(2)}) copy-start(bf16[256,1024]{1,0:T(8,128)(2,1)} %w_out.1) | copy-start | bytes 1572868
  6.3 1.0 %copy-start.1 = (bf16[256,1024]{1,0:T(8,128)(2,1)S(1)}, bf16[256,1024]{1,0:T(8,128)(2,1)}, u32[]{:S(2)}) copy-start(bf16[256,1024]{1,0:T(8,128)(2,1)} %w_in.1) | copy-start | bytes 1572868
  7.3 4.2 %copy-start.2 = (bf16[1,2,64,1024]{3,2,1,0:T(8,128)(2,1)S(1)}, bf16[1,2,64,1024]{3,2,1,0:T(8,128)(2,1)}, u32[]{:S(2)}) copy-start(bf16[1,2,64,1024]{3,2,1,0:T(8,128)(2,1)} %param.5) | copy-start | bytes 786436
  7.9 15.5 %collective-permute-start = (bf16[2,128,1024]{2,1,0:T(8,128)(2,1)S(1)}, bf16[2,128,1024]{2,1,0:T(8,128)(2,1)S(1)}, u32[]{:S(2)}, u32[]{:S(2)}) collective-permute-start(bf16[2,128,1024]{2,1,0:T(8,128)(2,1)S(1)} %shard_map.68.local), channel_id=1, source_target_pairs={{0,8},{2,16},{4,24},{10,2},{14,18},{8,26},{16,4},{20,12},{22,28},{... | collective-permute-start | bytes 1572872 | tf_op jit(solution)/shard_map/ppermute | solution.py:89
  11.5 4.2 %collective-permute-start.1 = (bf16[128,1024]{1,0:T(8,128)(2,1)S(1)}, bf16[128,1024]{1,0:T(8,128)(2,1)S(1)}, u32[]{:S(2)}, u32[]{:S(2)}) collective-permute-start(bf16[128,1024]{1,0:T(8,128)(2,1)S(1)} %bitcast.7), channel_id=1, source_target_pairs={{0,1},{1,0},{2,3},{3,2},{4,5},{5,4},{6,7},{7,6},{8,9},{9,8},{10,11... | collective-permute-start | bytes 786440 | tf_op jit(solution)/shard_map/ppermute | solution.py:40
  12.6 8.6 %collective-permute-start.6 = (bf16[64,1024]{1,0:T(8,128)(2,1)S(1)}, bf16[64,1024]{1,0:T(8,128)(2,1)S(1)}, u32[]{:S(2)}, u32[]{:S(2)}) collective-permute-start(bf16[64,1024]{1,0:T(8,128)(2,1)S(1)} %slice.8), channel_id=1, source_target_pairs={{0,4},{1,5},{2,6},{3,7},{4,0},{5,1},{6,2},{7,3},{8,12},{9,13},{10,... | collective-permute-start | bytes 393224 | tf_op jit(solution)/shard_map/ppermute | solution.py:40
  15.1 8.3 %collective-permute-start.3 = (bf16[128,1024]{1,0:T(8,128)(2,1)S(1)}, bf16[128,1024]{1,0:T(8,128)(2,1)S(1)}, u32[]{:S(2)}, u32[]{:S(2)}) collective-permute-start(bf16[128,1024]{1,0:T(8,128)(2,1)S(1)} %collective-permute-done.2.refs_2_), channel_id=1, source_target_pairs={{0,1},{1,0},{2,3},{3,2},{4,5},{5,4},{6,7},{7,6},{8,9},{9,8},{10,11... | collective-permute-start | bytes 786440 | tf_op jit(solution)/shard_map/ppermute | solution.py:40
  15.3 8.1 %collective-permute-start.5 = (bf16[128,1024]{1,0:T(8,128)(2,1)S(1)}, bf16[128,1024]{1,0:T(8,128)(2,1)S(1)}, u32[]{:S(2)}, u32[]{:S(2)}) collective-permute-start(bf16[128,1024]{1,0:T(8,128)(2,1)S(1)} %collective-permute-done.4.refs_4_), channel_id=1, source_target_pairs={{0,1},{1,0},{2,3},{3,2},{4,5},{5,4},{6,7},{7,6},{8,9},{9,8},{10,11... | collective-permute-start | bytes 786440 | tf_op jit(solution)/shard_map/ppermute | solution.py:40
  15.6 16.1 %copy-start.3 = (bf16[27,32,128]{2,1,0:T(8,128)(2,1)S(1)}, bf16[27,32,128]{2,1,0:T(8,128)(2,1)}, u32[]{:S(2)}) copy-start(bf16[27,32,128]{2,1,0:T(8,128)(2,1)} %kernel) | copy-start | bytes 663556
  15.7 5.7 %collective-permute-start.8 = (bf16[64,1024]{1,0:T(8,128)(2,1)S(1)}, bf16[64,1024]{1,0:T(8,128)(2,1)S(1)}, u32[]{:S(2)}, u32[]{:S(2)}) collective-permute-start(bf16[64,1024]{1,0:T(8,128)(2,1)S(1)} %slice.9), channel_id=1, source_target_pairs={{0,2},{1,3},{2,0},{3,1},{4,6},{5,7},{6,4},{7,5},{8,10},{9,11},{10,... | collective-permute-start | bytes 393224 | tf_op jit(solution)/shard_map/ppermute | solution.py:40
  21.2 2.2 %collective-permute-start.7 = (bf16[64,1024]{1,0:T(8,128)(2,1)S(1)}, bf16[64,1024]{1,0:T(8,128)(2,1)S(1)}, u32[]{:S(2)}, u32[]{:S(2)}) collective-permute-start(bf16[64,1024]{1,0:T(8,128)(2,1)S(1)} %collective-permute-done.6.refs_6_), channel_id=1, source_target_pairs={{0,1},{1,0},{2,3},{3,2},{4,5},{5,4},{6,7},{7,6},{8,9},{9,8},{10,11... | collective-permute-start | bytes 393224 | tf_op jit(solution)/shard_map/ppermute | solution.py:40
  21.3 2.1 %collective-permute-start.9 = (bf16[64,1024]{1,0:T(8,128)(2,1)S(1)}, bf16[64,1024]{1,0:T(8,128)(2,1)S(1)}, u32[]{:S(2)}, u32[]{:S(2)}) collective-permute-start(bf16[64,1024]{1,0:T(8,128)(2,1)S(1)} %collective-permute-done.8.refs_8_), channel_id=1, source_target_pairs={{0,1},{1,0},{2,3},{3,2},{4,5},{5,4},{6,7},{7,6},{8,9},{9,8},{10,11... | collective-permute-start | bytes 393224 | tf_op jit(solution)/shard_map/ppermute | solution.py:40
  24.9 8.7 %collective-permute-start.10 = (bf16[1024,128]{1,0:T(8,128)(2,1)S(1)}, bf16[1024,128]{1,0:T(8,128)(2,1)S(1)}, u32[]{:S(2)}, u32[]{:S(2)}) collective-permute-start(bf16[1024,128]{1,0:T(8,128)(2,1)S(1)} %get-tuple-element.15.refs_0_.mid), channel_id=1, source_target_pairs={{0,8},{8,0},{16,24},{24,16},{1,9},{9,1},{17,25},{25,17},{2,10},{10... | collective-permute-start | bytes 786440 | tf_op jit(solution)/shard_map/ppermute | solution.py:40
  27.5 10.1 %collective-permute-start.14 = (bf16[1024,128]{1,0:T(8,128)(2,1)S(1)}, bf16[1024,128]{1,0:T(8,128)(2,1)S(1)}, u32[]{:S(2)}, u32[]{:S(2)}) collective-permute-start(bf16[1024,128]{1,0:T(8,128)(2,1)S(1)} %get-tuple-element.15.refs_0_.mid), channel_id=1, source_target_pairs={{8,16},{16,8},{9,17},{17,9},{10,18},{18,10},{11,19},{19,11},{12,20... | collective-permute-start | bytes 786440 | tf_op jit(solution)/shard_map/ppermute | solution.py:227
  28.2 5.4 %copy-start.4 = (bf16[1,16,64,128]{3,2,1,0:T(8,128)(2,1)S(1)}, bf16[1,16,64,128]{3,2,1,0:T(8,128)(2,1)}, u32[]{:S(2)}) copy-start(bf16[1,16,64,128]{3,2,1,0:T(8,128)(2,1)} %param.6) | copy-start | bytes 786436
  28.2 13.7 %collective-permute-start.11 = (bf16[128,1024]{1,0:T(8,128)(2,1)S(1)}, bf16[128,1024]{1,0:T(8,128)(2,1)S(1)}, u32[]{:S(2)}, u32[]{:S(2)}) collective-permute-start(bf16[128,1024]{1,0:T(8,128)(2,1)S(1)} %get-tuple-element.16.refs_4_), channel_id=1, source_target_pairs={{0,2},{1,3},{2,0},{3,1},{4,6},{5,7},{6,4},{7,5},{8,10},{9,11},{10,... | collective-permute-start | bytes 786440 | tf_op jit(solution)/shard_map/ppermute | solution.py:40
  28.3 14.3 %collective-permute-start.12 = (bf16[128,1024]{1,0:T(8,128)(2,1)S(1)}, bf16[128,1024]{1,0:T(8,128)(2,1)S(1)}, u32[]{:S(2)}, u32[]{:S(2)}) collective-permute-start(bf16[128,1024]{1,0:T(8,128)(2,1)S(1)} %get-tuple-element.16.refs_4_), channel_id=1, source_target_pairs={{0,4},{1,5},{2,6},{3,7},{4,0},{5,1},{6,2},{7,3},{8,12},{9,13},{10,... | collective-permute-start | bytes 786440 | tf_op jit(solution)/shard_map/ppermute | solution.py:40
  29.7 12.9 %collective-permute-start.13 = (bf16[128,1024]{1,0:T(8,128)(2,1)S(1)}, bf16[128,1024]{1,0:T(8,128)(2,1)S(1)}, u32[]{:S(2)}, u32[]{:S(2)}) collective-permute-start(bf16[128,1024]{1,0:T(8,128)(2,1)S(1)} %get-tuple-element.16.refs_4_), channel_id=1, source_target_pairs={{0,6},{1,7},{2,4},{3,5},{4,2},{5,3},{6,0},{7,1},{8,14},{9,15},{10,... | collective-permute-start | bytes 786440 | tf_op jit(solution)/shard_map/ppermute | solution.py:40
  34.6 10.8 %collective-permute-start.15 = (bf16[2,9,32,128]{3,2,1,0:T(8,128)(2,1)S(1)}, bf16[2,9,32,128]{3,2,1,0:T(8,128)(2,1)S(1)}, u32[]{:S(2)}, u32[]{:S(2)}) collective-permute-start(bf16[2,9,32,128]{3,2,1,0:T(8,128)(2,1)S(1)} %shard_map.70.early), channel_id=1, source_target_pairs={{0,8},{8,0},{16,24},{24,16},{1,9},{9,1},{17,25},{25,17},{2,10},{10... | collective-permute-start | bytes 442376 | tf_op jit(solution)/shard_map/ppermute | solution.py:40
  38.3 7.1 %collective-permute-start.16 = (bf16[1,9,32,128]{3,2,1,0:T(8,128)(2,1)S(1)}, bf16[1,9,32,128]{3,2,1,0:T(8,128)(2,1)S(1)}, u32[]{:S(2)}, u32[]{:S(2)}) collective-permute-start(bf16[1,9,32,128]{3,2,1,0:T(8,128)(2,1)S(1)} %shard_map.71.late), channel_id=1, source_target_pairs={{0,8},{8,0},{16,24},{24,16},{1,9},{9,1},{17,25},{25,17},{2,10},{10... | collective-permute-start | bytes 221192 | tf_op jit(solution)/shard_map/ppermute | solution.py:40
  41.8 8.5 %collective-permute-start.17 = (bf16[256,128]{1,0:T(8,128)(2,1)S(1)}, bf16[256,128]{1,0:T(8,128)(2,1)S(1)}, u32[]{:S(2)}, u32[]{:S(2)}) collective-permute-start(bf16[256,128]{1,0:T(8,128)(2,1)S(1)} %get-tuple-element.22), channel_id=1, source_target_pairs={{0,2},{1,3},{2,0},{3,1},{4,6},{5,7},{6,4},{7,5},{8,10},{9,11},{10,... | collective-permute-start | bytes 196616 | tf_op jit(solution)/shard_map/ppermute | solution.py:40
  42.6 7.8 %collective-permute-start.18 = (bf16[256,128]{1,0:T(8,128)(2,1)S(1)}, bf16[256,128]{1,0:T(8,128)(2,1)S(1)}, u32[]{:S(2)}, u32[]{:S(2)}) collective-permute-start(bf16[256,128]{1,0:T(8,128)(2,1)S(1)} %get-tuple-element.23), channel_id=1, source_target_pairs={{0,4},{1,5},{2,6},{3,7},{4,0},{5,1},{6,2},{7,3},{8,12},{9,13},{10,... | collective-permute-start | bytes 196616 | tf_op jit(solution)/shard_map/ppermute | solution.py:40
  42.6 7.8 %collective-permute-start.19 = (bf16[256,128]{1,0:T(8,128)(2,1)S(1)}, bf16[256,128]{1,0:T(8,128)(2,1)S(1)}, u32[]{:S(2)}, u32[]{:S(2)}) collective-permute-start(bf16[256,128]{1,0:T(8,128)(2,1)S(1)} %get-tuple-element.24), channel_id=1, source_target_pairs={{0,6},{1,7},{2,4},{3,5},{4,2},{5,3},{6,0},{7,1},{8,14},{9,15},{10,... | collective-permute-start | bytes 196616 | tf_op jit(solution)/shard_map/ppermute | solution.py:40
  46.0 8.3 %collective-permute-start.21 = (bf16[3,9,32,128]{3,2,1,0:T(8,128)(2,1)S(1)}, bf16[3,9,32,128]{3,2,1,0:T(8,128)(2,1)S(1)}, u32[]{:S(2)}, u32[]{:S(2)}) collective-permute-start(bf16[3,9,32,128]{3,2,1,0:T(8,128)(2,1)S(1)} %shard_map.72.own), channel_id=1, source_target_pairs={{0,16},{8,24},{16,0},{24,8},{1,17},{9,25},{17,1},{25,9},{2,18},{10... | collective-permute-start | bytes 663560 | tf_op jit(solution)/shard_map/ppermute | solution.py:40
  51.7 3.4 %collective-permute-start.20 = (bf16[128,1024]{1,0:T(8,128)(2,1)S(1)}, bf16[128,1024]{1,0:T(8,128)(2,1)S(1)}, u32[]{:S(2)}, u32[]{:S(2)}) collective-permute-start(bf16[128,1024]{1,0:T(8,128)(2,1)S(1)} %get-tuple-element.26), channel_id=1, source_target_pairs={{0,1},{1,0},{2,3},{3,2},{4,5},{5,4},{6,7},{7,6},{8,9},{9,8},{10,11... | collective-permute-start | bytes 786440 | tf_op jit(solution)/shard_map/ppermute | solution.py:40

commit v5 on v4

--- a/solution.py
+++ b/solution.py
@@ -65,10 +65,10 @@
 )
 
 
-def pack_body(here, w_out, w_in, out):
+def pack_body(here, rows, w_in, out):
     core = here[1] % 2
-    part, width = w_out.shape[0] // 2, w_out.shape[1]
-    out[0] = w_out[pl.ds(pl.multiple_of(core * part, part), part), :]
+    part, width = rows.shape
+    out[0] = rows[...]
     lanes = width // 8
     for i in range(4):
         even = w_in[:, 2 * i * lanes : (2 * i + 1) * lanes]
@@ -242,9 +242,11 @@
 
     blocks = chip_gather(skip)
     gathered = plane_gather(blocks)
+    part = w_out.shape[0] // 2
+    rows = lax.dynamic_slice_in_dim(w_out, h % 2 * part, part, axis=0)
     mine = call(
-        pack_body, jax.ShapeDtypeStruct((2, w_out.shape[0] // 2, width), BF16), 2, nbytes=6 * w_out.size
-    )(here, w_out, w_in)
+        pack_body, jax.ShapeDtypeStruct((2, part, width), BF16), 2, nbytes=6 * w_out.size
+    )(here, rows, w_in)
     fetched = fetch(mine)
     weights = call(
         functools.partial(weights_body, group),
@@ -277,23 +279,8 @@
         )(*planes, pre)
         for planes in ((mid, near), (far,))
     )
-    w_blocks = [w_cols] + [swap(w_cols, "height", 2 * m) for m in (1, 2, 3)]
-    pair = call(
-        pair_body,
-        jax.ShapeDtypeStruct((3, 9, group, chans), BF16),
-        4,
-        nbytes=100 * 9 * group * chans,
-    )(here, order(early, *w_blocks), late, swap(early, "depth", 1), swap(late, "depth", 1))
-    total_cells = cells * lax.axis_size("depth")
-    kernel_grad = call(
-        functools.partial(total_body, float(total_cells) ** -0.5),
-        jax.ShapeDtypeStruct((27, group, chans), F32),
-        2,
-        scalars=0,
-        flops=SPAN,
-        nbytes=24 * 9 * group * chans,
-    )(pair, swap(pair, "depth", 2))
-
+    w_blocks = [w_cols] + [swap(w_cols, "height", 2 * m) for m in (1, 2)]
+    w_blocks.append(swap(order(w_cols, late), "height", 6))
     chip_cells = 2 * block
     back = call(
         functools.partial(back_body, wid),
@@ -303,6 +290,23 @@
         flops=2 * 27 * chans * chans * cells,
         nbytes=10 * cells * chans,
     )(here, mid, near, far, pre, order(weights, early, late))
+    pair = call(
+        pair_body,
+        jax.ShapeDtypeStruct((3, 9, group, chans), BF16),
+        4,
+        nbytes=100 * 9 * group * chans,
+    )(here, order(early, back[0], w_blocks[1], w_blocks[2]), late, swap(early, "depth", 1), swap(late, "depth", 1))
+    total_cells = cells * lax.axis_size("depth")
+    other_pair = swap(pair, "depth", 2)
+    kernel_grad = call(
+        functools.partial(total_body, float(total_cells) ** -0.5),
+        jax.ShapeDtypeStruct((27, group, chans), F32),
+        2,
+        scalars=0,
+        flops=SPAN,
+        nbytes=24 * 9 * group * chans,
+    )(pair, other_pair)
+
     parts = [back[0]] + [swap(b, "height", 2 * m) for m, b in enumerate(back) if m]
 
     own, other = call(
@@ -310,10 +314,11 @@
         [jax.ShapeDtypeStruct((block, width), F32), jax.ShapeDtypeStruct((block, width), BF16)],
         1 + len(parts) + len(w_blocks),
         scratch=[pltpu.VMEM((len(parts), chip_cells, chans), BF16)],
-        flops=SPAN,
+        flops=2 * block * width * width,
         nbytes=width * width,
     )(here, order(skip, pair), *parts, *w_blocks)
-    theirs = order(swap(other, "height", 1), kernel_grad)
+    theirs = swap(other, "height", 1)
+    theirs = order(theirs, kernel_grad)
     grad_in = (own + theirs.astype(F32)).astype(BF16)
     return grad_in.reshape(grad_out.shape), kernel_grad
 

time: 57 us -> 55.9 us (0.981); the launches traced: 55.9 us -> 55.8 us
  waiting for transfers between devices: 11.6 us -> 14.4 us
  local copies, waits for them, and re-layouts: 2.12 us -> 0.06 us
  starting transfers between devices: 31.8 us -> 30.8 us
    ppermute x20, waiting for transfers between devices: 9.89 us -> 12.7 us  [swap(): return lax.ppermute(x, axis, [(i, i ^ mask) for i in range(n)])]
    unnamed x10, local copies, waits for them, and re-layouts: 2.1 us -> 0.03 us
    ppermute x20, starting transfers between devices: 27.6 us -> 26.7 us  [swap(): return lax.ppermute(x, axis, [(i, i ^ mask) for i in range(n)])]
  transfers between devices with their start and end apart: 22 -> 22, of which waited for: 5 -> 9; matrix products, arithmetic and copies ran while one was open for 0% -> 0% of each run, Pallas kernels for 13% -> 13%
where the time goes in v5:
time: 55.9 us; the launch traced here: 55.8 us
  starting transfers between devices  30.8 us (55%)
  waiting for transfers between devices  14.4 us (26%)
  Pallas kernels  8.74 us (16%)
  other arithmetic  0.85 us (2%)
  between operations  0.83 us (1%)
    ppermute x20, starting transfers between devices, swap(): return lax.ppermute(x, axis, [(i, i ^ mask) for i in range(n)])  26.7 us
    ppermute x20, waiting for transfers between devices, swap(): return lax.ppermute(x, axis, [(i, i ^ mask) for i in range(n)])  12.7 us
    ppermute x1, starting transfers between devices, fetch(): return lax.ppermute(mine, ('depth', 'height'), pairs)  3.51 us
    pallas_call x1, Pallas kernels, fast(): call(functools.partial(back_body, wid), [jax.ShapeDtypeStruct((chip_cells...  2.21 us
    ppermute x1, waiting for transfers between devices, fetch(): return lax.ppermute(mine, ('depth', 'height'), pairs)  1.71 us
    pallas_call x2, Pallas kernels, fast(): call(functools.partial(kgrad_body, wid, group, len(planes)), jax.ShapeDty...  1.63 us
    pallas_call x1, Pallas kernels, fast(): call(functools.partial(mid_body, places, block), [jax.ShapeDtypeStruct((c...  1.44 us
    pallas_call x1, Pallas kernels, fast(): call(partial_body, [jax.ShapeDtypeStruct((block, width), F32), jax.ShapeD...  1.29 us
  transfers between devices with their start and end apart: 22, of which 9 were waited for; matrix products, arithmetic and copies ran while one was open for 0% of the time, Pallas kernels for 13%

profile of v5, /device:TPU:0, one launch (start us, length us, event | category | flops | bytes accessed | tf_op | source)
XLA Modules:
  0.0 55.8 jit_solution(11122715675210153119)
XLA Ops:
  0.6 0.0 copy-start
  0.7 3.0 %collective-permute-start.2 = (bf16[128,1024]{1,0:T(8,128)(2,1)}, bf16[128,1024]{1,0:T(8,128)(2,1)S(1)}, u32[]{:S(2)}, u32[]{:S(2)}) collective-permute-start(bf16[128,1024]{1,0:T(8,128)(2,1)} %bitcast.5), channel_id=1, source_target_pairs={{0,2},{1,3},{2,0},{3,1},{4,6},{5,7},{6,4},{7,5},{8,10},{9,11},{10,... | collective-permute-start | bytes 786440 | tf_op jit(solution)/shard_map/ppermute | solution.py:40
  3.7 1.5 %collective-permute-start.4 = (bf16[128,1024]{1,0:T(8,128)(2,1)}, bf16[128,1024]{1,0:T(8,128)(2,1)S(1)}, u32[]{:S(2)}, u32[]{:S(2)}) collective-permute-start(bf16[128,1024]{1,0:T(8,128)(2,1)} %bitcast.6), channel_id=1, source_target_pairs={{0,4},{1,5},{2,6},{3,7},{4,0},{5,1},{6,2},{7,3},{8,12},{9,13},{10,... | collective-permute-start | bytes 786440 | tf_op jit(solution)/shard_map/ppermute | solution.py:40
  5.2 0.1 pad_add_fusion.here
  5.3 0.6 %shard_map.68.local = bf16[2,128,1024]{2,1,0:T(8,128)(2,1)S(1)} custom-call(s32[2]{0:T(128)S(1)} %pad_add_fusion.here, bf16[128,1024]{1,0:T(8,128)(2,1)S(1)} %constant_dynamic-slice_fusion.rows, bf16[256,1024]{1,0:T(8,128)(2,1)S(1)} %copy-done.2), custom_call_target="tpu_custom_call" | custom-call | bytes 1572864 | tf_op jit(solution)/shard_map/pallas_call | solution.py:247
  5.9 3.5 %collective-permute-start = (bf16[2,128,1024]{2,1,0:T(8,128)(2,1)S(1)}, bf16[2,128,1024]{2,1,0:T(8,128)(2,1)S(1)}, u32[]{:S(2)}, u32[]{:S(2)}) collective-permute-start(bf16[2,128,1024]{2,1,0:T(8,128)(2,1)S(1)} %shard_map.68.local), channel_id=1, source_target_pairs={{0,8},{2,16},{4,24},{10,2},{14,18},{8,26},{16,4},{20,12},{22,28},{... | collective-permute-start | bytes 1572872 | tf_op jit(solution)/shard_map/ppermute | solution.py:89
  9.5 1.1 %collective-permute-start.1 = (bf16[128,1024]{1,0:T(8,128)(2,1)S(1)}, bf16[128,1024]{1,0:T(8,128)(2,1)S(1)}, u32[]{:S(2)}, u32[]{:S(2)}) collective-permute-start(bf16[128,1024]{1,0:T(8,128)(2,1)S(1)} %bitcast.7), channel_id=1, source_target_pairs={{0,1},{1,0},{2,3},{3,2},{4,5},{5,4},{6,7},{7,6},{8,9},{9,8},{10,11... | collective-permute-start | bytes 786440 | tf_op jit(solution)/shard_map/ppermute | solution.py:40
  10.5 2.2 %collective-permute-done.2.refs_2_ = bf16[128,1024]{1,0:T(8,128)(2,1)S(1)} collective-permute-done((bf16[128,1024]{1,0:T(8,128)(2,1)}, bf16[128,1024]{1,0:T(8,128)(2,1)S(1)}, u32[]{:S(2)}, u32[]{:S(2)}) %collective-permute-start.2) | collective-permute-done | bytes 262176 | tf_op jit(solution)/shard_map/ppermute | solution.py:40
  12.7 0.3 collective-permute-start.6
  13.1 0.0 collective-permute-done.4.refs_4_
  13.1 0.0 copy-start.4
  13.1 2.3 %collective-permute-start.8 = (bf16[64,1024]{1,0:T(8,128)(2,1)S(1)}, bf16[64,1024]{1,0:T(8,128)(2,1)S(1)}, u32[]{:S(2)}, u32[]{:S(2)}) collective-permute-start(bf16[64,1024]{1,0:T(8,128)(2,1)S(1)} %slice.9), channel_id=1, source_target_pairs={{0,2},{1,3},{2,0},{3,1},{4,6},{5,7},{6,4},{7,5},{8,10},{9,11},{10,... | collective-permute-start | bytes 393224 | tf_op jit(solution)/shard_map/ppermute | solution.py:40
  15.4 0.0 collective-permute-start.3
  15.5 0.0 collective-permute-done.1.refs_1_
  15.5 0.5 collective-permute-start.5
  16.0 3.2 %collective-permute-done.6.refs_6_ = bf16[64,1024]{1,0:T(8,128)(2,1)S(1)} collective-permute-done((bf16[64,1024]{1,0:T(8,128)(2,1)S(1)}, bf16[64,1024]{1,0:T(8,128)(2,1)S(1)}, u32[]{:S(2)}, u32[]{:S(2)}) %collective-permute-start.6) | collective-permute-done | bytes 131104 | tf_op jit(solution)/shard_map/ppermute | solution.py:40
  19.2 0.0 collective-permute-start.7
  19.2 0.0 collective-permute-done.8.refs_8_
  19.2 0.5 collective-permute-start.9
  19.7 1.7 %collective-permute-done.fetched = bf16[2,128,1024]{2,1,0:T(8,128)(2,1)S(1)} collective-permute-done((bf16[2,128,1024]{2,1,0:T(8,128)(2,1)S(1)}, bf16[2,128,1024]{2,1,0:T(8,128)(2,1)S(1)}, u32[]{:S(2)}, u32[]{:S(2)}) %collective-permute-start) | collective-permute-done | bytes 524320 | tf_op jit(solution)/shard_map/ppermute | solution.py:89
  21.4 0.0 collective-permute-done.5.refs_5_
  21.4 1.4 %shard_map.69 = (bf16[1024,128]{1,0:T(8,128)(2,1)S(1)}, bf16[128,1024]{1,0:T(8,128)(2,1)S(1)}) custom-call(s32[2]{0:T(128)S(1)} %pad_add_fusion.here, bf16[2,128,1024]{2,1,0:T(8,128)(2,1)S(1)} %shard_map.68.local, bf16[2,128,1024]{2,1,0:T(8,128)(2,1)S(1)} %collective-permute-done.fetched, bf16[128,1024]{1,0:T(8,128)(2,1)S(1)} %bitcast.8, ...), custom_call_target="tpu_custom_call" | custom-call | flops 268435456 | bytes 2097152 | tf_op jit(solution)/shard_map/pallas_call | solution.py:260
  22.8 3.3 %collective-permute-start.10 = (bf16[1024,128]{1,0:T(8,128)(2,1)S(1)}, bf16[1024,128]{1,0:T(8,128)(2,1)S(1)}, u32[]{:S(2)}, u32[]{:S(2)}) collective-permute-start(bf16[1024,128]{1,0:T(8,128)(2,1)S(1)} %get-tuple-element.16.refs_0_.mid), channel_id=1, source_target_pairs={{0,8},{8,0},{16,24},{24,16},{1,9},{9,1},{17,25},{25,17},{2,10},{10... | collective-permute-start | bytes 786440 | tf_op jit(solution)/shard_map/ppermute | solution.py:40
  26.1 0.7 %collective-permute-start.11 = (bf16[1024,128]{1,0:T(8,128)(2,1)S(1)}, bf16[1024,128]{1,0:T(8,128)(2,1)S(1)}, u32[]{:S(2)}, u32[]{:S(2)}) collective-permute-start(bf16[1024,128]{1,0:T(8,128)(2,1)S(1)} %get-tuple-element.16.refs_0_.mid), channel_id=1, source_target_pairs={{8,16},{16,8},{9,17},{17,9},{10,18},{18,10},{11,19},{19,11},{12,20... | collective-permute-start | bytes 786440 | tf_op jit(solution)/shard_map/ppermute | solution.py:227
  26.8 0.1 collective-permute-start.12
  26.9 2.9 %collective-permute-start.13 = (bf16[128,1024]{1,0:T(8,128)(2,1)S(1)}, bf16[128,1024]{1,0:T(8,128)(2,1)S(1)}, u32[]{:S(2)}, u32[]{:S(2)}) collective-permute-start(bf16[128,1024]{1,0:T(8,128)(2,1)S(1)} %get-tuple-element.26.refs_4_), channel_id=1, source_target_pairs={{0,4},{1,5},{2,6},{3,7},{4,0},{5,1},{6,2},{7,3},{8,12},{9,13},{10,... | collective-permute-start | bytes 786440 | tf_op jit(solution)/shard_map/ppermute | solution.py:40
  29.8 2.9 %collective-permute-done.10.refs_1_.near = bf16[1024,128]{1,0:T(8,128)(2,1)S(1)} collective-permute-done((bf16[1024,128]{1,0:T(8,128)(2,1)S(1)}, bf16[1024,128]{1,0:T(8,128)(2,1)S(1)}, u32[]{:S(2)}, u32[]{:S(2)}) %collective-permute-start.10) | collective-permute-done | bytes 262176 | tf_op jit(solution)/shard_map/ppermute | solution.py:40
  32.7 1.0 %shard_map.70.early = bf16[2,9,32,128]{3,2,1,0:T(8,128)(2,1)S(1)} custom-call(bf16[1024,128]{1,0:T(8,128)(2,1)S(1)} %get-tuple-element.16.refs_0_.mid, bf16[1024,128]{1,0:T(8,128)(2,1)S(1)} %collective-permute-done.10.refs_1_.near, bf16[1024,128]{1,0:T(8,128)(2,1)S(1)} %bitcast.10), custom_call_target="tpu_custom_call" | custom-call | flops 603979776 | bytes 786432 | tf_op jit(solution)/shard_map/pallas_call | solution.py:271
  33.7 1.8 %collective-permute-start.14 = (bf16[2,9,32,128]{3,2,1,0:T(8,128)(2,1)S(1)}, bf16[2,9,32,128]{3,2,1,0:T(8,128)(2,1)S(1)}, u32[]{:S(2)}, u32[]{:S(2)}) collective-permute-start(bf16[2,9,32,128]{3,2,1,0:T(8,128)(2,1)S(1)} %shard_map.70.early), channel_id=1, source_target_pairs={{0,8},{8,0},{16,24},{24,16},{1,9},{9,1},{17,25},{25,17},{2,10},{10... | collective-permute-start | bytes 442376 | tf_op jit(solution)/shard_map/ppermute | solution.py:40
  35.5 0.1 shard_map.71.weights
  35.7 0.7 %shard_map.72.late = bf16[1,9,32,128]{3,2,1,0:T(8,128)(2,1)S(1)} custom-call(bf16[1024,128]{1,0:T(8,128)(2,1)S(1)} %collective-permute-done.11.refs_0_.far, bf16[1024,128]{1,0:T(8,128)(2,1)S(1)} %bitcast.11), custom_call_target="tpu_custom_call" | custom-call | flops 301989888 | bytes 786432 | tf_op jit(solution)/shard_map/pallas_call | solution.py:271
  36.3 1.7 %collective-permute-start.15 = (bf16[1,9,32,128]{3,2,1,0:T(8,128)(2,1)S(1)}, bf16[1,9,32,128]{3,2,1,0:T(8,128)(2,1)S(1)}, u32[]{:S(2)}, u32[]{:S(2)}) collective-permute-start(bf16[1,9,32,128]{3,2,1,0:T(8,128)(2,1)S(1)} %shard_map.72.late), channel_id=1, source_target_pairs={{0,8},{8,0},{16,24},{24,16},{1,9},{9,1},{17,25},{25,17},{2,10},{10... | collective-permute-start | bytes 221192 | tf_op jit(solution)/shard_map/ppermute | solution.py:40
  38.0 1.4 %collective-permute-start.19 = (bf16[128,1024]{1,0:T(8,128)(2,1)S(1)}, bf16[128,1024]{1,0:T(8,128)(2,1)S(1)}, u32[]{:S(2)}, u32[]{:S(2)}) collective-permute-start(bf16[128,1024]{1,0:T(8,128)(2,1)S(1)} %get-tuple-element.26.refs_4_), channel_id=1, source_target_pairs={{0,6},{1,7},{2,4},{3,5},{4,2},{5,3},{6,0},{7,1},{8,14},{9,15},{10,... | collective-permute-start | bytes 786440 | tf_op jit(solution)/shard_map/ppermute | solution.py:40
  39.4 2.2 %shard_map.73 = (bf16[256,128]{1,0:T(8,128)(2,1)S(1)}, bf16[256,128]{1,0:T(8,128)(2,1)S(1)}, bf16[256,128]{1,0:T(8,128)(2,1)S(1)}, bf16[256,128]{1,0:T(8,128)(2,1)S(1)}) custom-call(s32[2]{0:T(128)S(1)} %pad_add_fusion.here, bf16[1024,128]{1,0:T(8,128)(2,1)S(1)} %get-tuple-element.16.refs_0_.mid, bf16[1024,128]{1,0:T(8,128)(2,1)S(1)} %collective-permute-done.10.refs_1_.near, ...), custom_call_target="tpu_custom_call" | custom-call | flops 905969664 | bytes 1310720 | tf_op jit(solution)/shard_map/pallas_call | solution.py:285
  41.6 0.0 collective-permute-done.12.refs_5_
  41.7 0.6 %shard_map.74.own = bf16[3,9,32,128]{3,2,1,0:T(8,128)(2,1)S(1)} custom-call(s32[2]{0:T(128)S(1)} %pad_add_fusion.here, bf16[2,9,32,128]{3,2,1,0:T(8,128)(2,1)S(1)} %shard_map.70.early, bf16[1,9,32,128]{3,2,1,0:T(8,128)(2,1)S(1)} %shard_map.72.late, bf16[2,9,32,128]{3,2,1,0:T(8,128)(2,1)S(1)} %collective-permute-done.14.other_early, ...), custom_call_target="tpu_custom_call" | custom-call | bytes 3686400 | tf_op jit(solution)/shard_map/pallas_call | solution.py:293
  42.3 2.6 %collective-permute-start.21 = (bf16[3,9,32,128]{3,2,1,0:T(8,128)(2,1)S(1)}, bf16[3,9,32,128]{3,2,1,0:T(8,128)(2,1)S(1)}, u32[]{:S(2)}, u32[]{:S(2)}) collective-permute-start(bf16[3,9,32,128]{3,2,1,0:T(8,128)(2,1)S(1)} %shard_map.74.own), channel_id=1, source_target_pairs={{0,16},{8,24},{16,0},{24,8},{1,17},{9,25},{17,1},{25,9},{2,18},{10... | collective-permute-start | bytes 663560 | tf_op jit(solution)/shard_map/ppermute | solution.py:40
  44.9 2.0 %collective-permute-start.17 = (bf16[256,128]{1,0:T(8,128)(2,1)S(1)}, bf16[256,128]{1,0:T(8,128)(2,1)S(1)}, u32[]{:S(2)}, u32[]{:S(2)}) collective-permute-start(bf16[256,128]{1,0:T(8,128)(2,1)S(1)} %get-tuple-element.24), channel_id=1, source_target_pairs={{0,4},{1,5},{2,6},{3,7},{4,0},{5,1},{6,2},{7,3},{8,12},{9,13},{10,... | collective-permute-start | bytes 196616 | tf_op jit(solution)/shard_map/ppermute | solution.py:40
  46.9 1.5 %collective-permute-start.18 = (bf16[256,128]{1,0:T(8,128)(2,1)S(1)}, bf16[256,128]{1,0:T(8,128)(2,1)S(1)}, u32[]{:S(2)}, u32[]{:S(2)}) collective-permute-start(bf16[256,128]{1,0:T(8,128)(2,1)S(1)} %get-tuple-element.25), channel_id=1, source_target_pairs={{0,6},{1,7},{2,4},{3,5},{4,2},{5,3},{6,0},{7,1},{8,14},{9,15},{10,... | collective-permute-start | bytes 196616 | tf_op jit(solution)/shard_map/ppermute | solution.py:40
  48.4 0.8 %collective-permute-done.16.refs_1_ = bf16[256,128]{1,0:T(8,128)(2,1)S(1)} collective-permute-done((bf16[256,128]{1,0:T(8,128)(2,1)S(1)}, bf16[256,128]{1,0:T(8,128)(2,1)S(1)}, u32[]{:S(2)}, u32[]{:S(2)}) %collective-permute-start.16) | collective-permute-done | bytes 65568 | tf_op jit(solution)/shard_map/ppermute | solution.py:40
  49.2 0.5 collective-permute-done.17.refs_2_
  49.7 2.4 %collective-permute-done.18.refs_3_ = bf16[256,128]{1,0:T(8,128)(2,1)S(1)} collective-permute-done((bf16[256,128]{1,0:T(8,128)(2,1)S(1)}, bf16[256,128]{1,0:T(8,128)(2,1)S(1)}, u32[]{:S(2)}, u32[]{:S(2)}) %collective-permute-start.18) | collective-permute-done | bytes 65568 | tf_op jit(solution)/shard_map/ppermute | solution.py:40
  52.1 1.3 %shard_map.75 = (f32[128,1024]{1,0:T(8,128)S(1)}, bf16[128,1024]{1,0:T(8,128)(2,1)S(1)}) custom-call(s32[2]{0:T(128)S(1)} %pad_add_fusion.here, bf16[128,1024]{1,0:T(8,128)(2,1)S(1)} %bitcast.9, bf16[256,128]{1,0:T(8,128)(2,1)S(1)} %get-tuple-element.19.refs_0_, bf16[256,128]{1,0:T(8,128)(2,1)S(1)} %collective-permute-done.16.refs_1_, ...), custom_call_target="tpu_custom_call" | custom-call | flops 268435456 | bytes 1048576 | tf_op jit(solution)/shard_map/pallas_call | solution.py:312
  53.4 0.1 collective-permute-start.20
  53.5 0.6 %collective-permute-done.21.other = bf16[3,9,32,128]{3,2,1,0:T(8,128)(2,1)S(1)} collective-permute-done((bf16[3,9,32,128]{3,2,1,0:T(8,128)(2,1)S(1)}, bf16[3,9,32,128]{3,2,1,0:T(8,128)(2,1)S(1)}, u32[]{:S(2)}, u32[]{:S(2)}) %collective-permute-start.21) | collective-permute-done | bytes 221216 | tf_op jit(solution)/shard_map/ppermute | solution.py:40
  54.1 0.8 %shard_map.76 = f32[27,32,128]{2,1,0:T(8,128)} custom-call(bf16[3,9,32,128]{3,2,1,0:T(8,128)(2,1)S(1)} %shard_map.74.own, bf16[3,9,32,128]{3,2,1,0:T(8,128)(2,1)S(1)} %collective-permute-done.21.other), custom_call_target="tpu_custom_call" | custom-call | flops 34359738368 | bytes 884736 | tf_op jit(solution)/shard_map/pallas_call | solution.py:301
  54.9 0.1 collective-permute-done.20
  55.0 0.8 %add_convert_fusion = bf16[128,1024]{1,0:T(8,128)(2,1)} fusion(f32[128,1024]{1,0:T(8,128)S(1)} %get-tuple-element.27, bf16[128,1024]{1,0:T(8,128)(2,1)S(1)} %collective-permute-done.20), kind=kLoop, calls=%fused_computation | loop fusion | flops 393216 | bytes 1048576 | tf_op jit(solution)/shard_map/convert_element_type | solution.py:322
  (20 shorter events, 0.1 us)
Async XLA Ops:
  0.6 4.6 %copy-start = (bf16[256,1024]{1,0:T(8,128)(2,1)S(1)}, bf16[256,1024]{1,0:T(8,128)(2,1)}, u32[]{:S(2)}) copy-start(bf16[256,1024]{1,0:T(8,128)(2,1)} %param.8) | copy-start | bytes 1572868
  0.6 4.6 %copy-start.2 = (bf16[256,1024]{1,0:T(8,128)(2,1)S(1)}, bf16[256,1024]{1,0:T(8,128)(2,1)}, u32[]{:S(2)}) copy-start(bf16[256,1024]{1,0:T(8,128)(2,1)} %w_in.1) | copy-start | bytes 1572868
  0.7 12.1 %collective-permute-start.2 = (bf16[128,1024]{1,0:T(8,128)(2,1)}, bf16[128,1024]{1,0:T(8,128)(2,1)S(1)}, u32[]{:S(2)}, u32[]{:S(2)}) collective-permute-start(bf16[128,1024]{1,0:T(8,128)(2,1)} %bitcast.5), channel_id=1, source_target_pairs={{0,2},{1,3},{2,0},{3,1},{4,6},{5,7},{6,4},{7,5},{8,10},{9,11},{10,... | collective-permute-start | bytes 786440 | tf_op jit(solution)/shard_map/ppermute | solution.py:40
  3.7 9.4 %collective-permute-start.4 = (bf16[128,1024]{1,0:T(8,128)(2,1)}, bf16[128,1024]{1,0:T(8,128)(2,1)S(1)}, u32[]{:S(2)}, u32[]{:S(2)}) collective-permute-start(bf16[128,1024]{1,0:T(8,128)(2,1)} %bitcast.6), channel_id=1, source_target_pairs={{0,4},{1,5},{2,6},{3,7},{4,0},{5,1},{6,2},{7,3},{8,12},{9,13},{10,... | collective-permute-start | bytes 786440 | tf_op jit(solution)/shard_map/ppermute | solution.py:40
  5.3 4.2 %copy-start.1 = (bf16[1,2,64,1024]{3,2,1,0:T(8,128)(2,1)S(1)}, bf16[1,2,64,1024]{3,2,1,0:T(8,128)(2,1)}, u32[]{:S(2)}) copy-start(bf16[1,2,64,1024]{3,2,1,0:T(8,128)(2,1)} %param.5) | copy-start | bytes 786436
  5.9 15.5 %collective-permute-start = (bf16[2,128,1024]{2,1,0:T(8,128)(2,1)S(1)}, bf16[2,128,1024]{2,1,0:T(8,128)(2,1)S(1)}, u32[]{:S(2)}, u32[]{:S(2)}) collective-permute-start(bf16[2,128,1024]{2,1,0:T(8,128)(2,1)S(1)} %shard_map.68.local), channel_id=1, source_target_pairs={{0,8},{2,16},{4,24},{10,2},{14,18},{8,26},{16,4},{20,12},{22,28},{... | collective-permute-start | bytes 1572872 | tf_op jit(solution)/shard_map/ppermute | solution.py:89
  9.5 6.0 %collective-permute-start.1 = (bf16[128,1024]{1,0:T(8,128)(2,1)S(1)}, bf16[128,1024]{1,0:T(8,128)(2,1)S(1)}, u32[]{:S(2)}, u32[]{:S(2)}) collective-permute-start(bf16[128,1024]{1,0:T(8,128)(2,1)S(1)} %bitcast.7), channel_id=1, source_target_pairs={{0,1},{1,0},{2,3},{3,2},{4,5},{5,4},{6,7},{7,6},{8,9},{9,8},{10,11... | collective-permute-start | bytes 786440 | tf_op jit(solution)/shard_map/ppermute | solution.py:40
  12.7 6.4 %collective-permute-start.6 = (bf16[64,1024]{1,0:T(8,128)(2,1)S(1)}, bf16[64,1024]{1,0:T(8,128)(2,1)S(1)}, u32[]{:S(2)}, u32[]{:S(2)}) collective-permute-start(bf16[64,1024]{1,0:T(8,128)(2,1)S(1)} %slice.8), channel_id=1, source_target_pairs={{0,4},{1,5},{2,6},{3,7},{4,0},{5,1},{6,2},{7,3},{8,12},{9,13},{10,... | collective-permute-start | bytes 393224 | tf_op jit(solution)/shard_map/ppermute | solution.py:40
  13.1 19.6 %copy-start.4 = (bf16[1,16,64,128]{3,2,1,0:T(8,128)(2,1)S(1)}, bf16[1,16,64,128]{3,2,1,0:T(8,128)(2,1)}, u32[]{:S(2)}) copy-start(bf16[1,16,64,128]{3,2,1,0:T(8,128)(2,1)} %param.6) | copy-start | bytes 786436
  13.1 6.0 %collective-permute-start.8 = (bf16[64,1024]{1,0:T(8,128)(2,1)S(1)}, bf16[64,1024]{1,0:T(8,128)(2,1)S(1)}, u32[]{:S(2)}, u32[]{:S(2)}) collective-permute-start(bf16[64,1024]{1,0:T(8,128)(2,1)S(1)} %slice.9), channel_id=1, source_target_pairs={{0,2},{1,3},{2,0},{3,1},{4,6},{5,7},{6,4},{7,5},{8,10},{9,11},{10,... | collective-permute-start | bytes 393224 | tf_op jit(solution)/shard_map/ppermute | solution.py:40
  15.4 5.9 %collective-permute-start.3 = (bf16[128,1024]{1,0:T(8,128)(2,1)S(1)}, bf16[128,1024]{1,0:T(8,128)(2,1)S(1)}, u32[]{:S(2)}, u32[]{:S(2)}) collective-permute-start(bf16[128,1024]{1,0:T(8,128)(2,1)S(1)} %collective-permute-done.2.refs_2_), channel_id=1, source_target_pairs={{0,1},{1,0},{2,3},{3,2},{4,5},{5,4},{6,7},{7,6},{8,9},{9,8},{10,11... | collective-permute-start | bytes 786440 | tf_op jit(solution)/shard_map/ppermute | solution.py:40
  15.5 5.9 %collective-permute-start.5 = (bf16[128,1024]{1,0:T(8,128)(2,1)S(1)}, bf16[128,1024]{1,0:T(8,128)(2,1)S(1)}, u32[]{:S(2)}, u32[]{:S(2)}) collective-permute-start(bf16[128,1024]{1,0:T(8,128)(2,1)S(1)} %collective-permute-done.4.refs_4_), channel_id=1, source_target_pairs={{0,1},{1,0},{2,3},{3,2},{4,5},{5,4},{6,7},{7,6},{8,9},{9,8},{10,11... | collective-permute-start | bytes 786440 | tf_op jit(solution)/shard_map/ppermute | solution.py:40
  19.2 2.2 %collective-permute-start.7 = (bf16[64,1024]{1,0:T(8,128)(2,1)S(1)}, bf16[64,1024]{1,0:T(8,128)(2,1)S(1)}, u32[]{:S(2)}, u32[]{:S(2)}) collective-permute-start(bf16[64,1024]{1,0:T(8,128)(2,1)S(1)} %collective-permute-done.6.refs_6_), channel_id=1, source_target_pairs={{0,1},{1,0},{2,3},{3,2},{4,5},{5,4},{6,7},{7,6},{8,9},{9,8},{10,11... | collective-permute-start | bytes 393224 | tf_op jit(solution)/shard_map/ppermute | solution.py:40
  19.2 2.2 %collective-permute-start.9 = (bf16[64,1024]{1,0:T(8,128)(2,1)S(1)}, bf16[64,1024]{1,0:T(8,128)(2,1)S(1)}, u32[]{:S(2)}, u32[]{:S(2)}) collective-permute-start(bf16[64,1024]{1,0:T(8,128)(2,1)S(1)} %collective-permute-done.8.refs_8_), channel_id=1, source_target_pairs={{0,1},{1,0},{2,3},{3,2},{4,5},{5,4},{6,7},{7,6},{8,9},{9,8},{10,11... | collective-permute-start | bytes 393224 | tf_op jit(solution)/shard_map/ppermute | solution.py:40
  22.8 9.9 %collective-permute-start.10 = (bf16[1024,128]{1,0:T(8,128)(2,1)S(1)}, bf16[1024,128]{1,0:T(8,128)(2,1)S(1)}, u32[]{:S(2)}, u32[]{:S(2)}) collective-permute-start(bf16[1024,128]{1,0:T(8,128)(2,1)S(1)} %get-tuple-element.16.refs_0_.mid), channel_id=1, source_target_pairs={{0,8},{8,0},{16,24},{24,16},{1,9},{9,1},{17,25},{25,17},{2,10},{10... | collective-permute-start | bytes 786440 | tf_op jit(solution)/shard_map/ppermute | solution.py:40
  26.1 9.5 %collective-permute-start.11 = (bf16[1024,128]{1,0:T(8,128)(2,1)S(1)}, bf16[1024,128]{1,0:T(8,128)(2,1)S(1)}, u32[]{:S(2)}, u32[]{:S(2)}) collective-permute-start(bf16[1024,128]{1,0:T(8,128)(2,1)S(1)} %get-tuple-element.16.refs_0_.mid), channel_id=1, source_target_pairs={{8,16},{16,8},{9,17},{17,9},{10,18},{18,10},{11,19},{19,11},{12,20... | collective-permute-start | bytes 786440 | tf_op jit(solution)/shard_map/ppermute | solution.py:227
  26.8 14.9 %collective-permute-start.12 = (bf16[128,1024]{1,0:T(8,128)(2,1)S(1)}, bf16[128,1024]{1,0:T(8,128)(2,1)S(1)}, u32[]{:S(2)}, u32[]{:S(2)}) collective-permute-start(bf16[128,1024]{1,0:T(8,128)(2,1)S(1)} %get-tuple-element.26.refs_4_), channel_id=1, source_target_pairs={{0,2},{1,3},{2,0},{3,1},{4,6},{5,7},{6,4},{7,5},{8,10},{9,11},{10,... | collective-permute-start | bytes 786440 | tf_op jit(solution)/shard_map/ppermute | solution.py:40
  26.9 14.8 %collective-permute-start.13 = (bf16[128,1024]{1,0:T(8,128)(2,1)S(1)}, bf16[128,1024]{1,0:T(8,128)(2,1)S(1)}, u32[]{:S(2)}, u32[]{:S(2)}) collective-permute-start(bf16[128,1024]{1,0:T(8,128)(2,1)S(1)} %get-tuple-element.26.refs_4_), channel_id=1, source_target_pairs={{0,4},{1,5},{2,6},{3,7},{4,0},{5,1},{6,2},{7,3},{8,12},{9,13},{10,... | collective-permute-start | bytes 786440 | tf_op jit(solution)/shard_map/ppermute | solution.py:40
  32.7 2.8 %copy-start.3 = (bf16[27,32,128]{2,1,0:T(8,128)(2,1)S(1)}, bf16[27,32,128]{2,1,0:T(8,128)(2,1)}, u32[]{:S(2)}) copy-start(bf16[27,32,128]{2,1,0:T(8,128)(2,1)} %kernel) | copy-start | bytes 663556
  33.7 8.0 %collective-permute-start.14 = (bf16[2,9,32,128]{3,2,1,0:T(8,128)(2,1)S(1)}, bf16[2,9,32,128]{3,2,1,0:T(8,128)(2,1)S(1)}, u32[]{:S(2)}, u32[]{:S(2)}) collective-permute-start(bf16[2,9,32,128]{3,2,1,0:T(8,128)(2,1)S(1)} %shard_map.70.early), channel_id=1, source_target_pairs={{0,8},{8,0},{16,24},{24,16},{1,9},{9,1},{17,25},{25,17},{2,10},{10... | collective-permute-start | bytes 442376 | tf_op jit(solution)/shard_map/ppermute | solution.py:40
  36.3 5.3 %collective-permute-start.15 = (bf16[1,9,32,128]{3,2,1,0:T(8,128)(2,1)S(1)}, bf16[1,9,32,128]{3,2,1,0:T(8,128)(2,1)S(1)}, u32[]{:S(2)}, u32[]{:S(2)}) collective-permute-start(bf16[1,9,32,128]{3,2,1,0:T(8,128)(2,1)S(1)} %shard_map.72.late), channel_id=1, source_target_pairs={{0,8},{8,0},{16,24},{24,16},{1,9},{9,1},{17,25},{25,17},{2,10},{10... | collective-permute-start | bytes 221192 | tf_op jit(solution)/shard_map/ppermute | solution.py:40
  38.0 14.1 %collective-permute-start.19 = (bf16[128,1024]{1,0:T(8,128)(2,1)S(1)}, bf16[128,1024]{1,0:T(8,128)(2,1)S(1)}, u32[]{:S(2)}, u32[]{:S(2)}) collective-permute-start(bf16[128,1024]{1,0:T(8,128)(2,1)S(1)} %get-tuple-element.26.refs_4_), channel_id=1, source_target_pairs={{0,6},{1,7},{2,4},{3,5},{4,2},{5,3},{6,0},{7,1},{8,14},{9,15},{10,... | collective-permute-start | bytes 786440 | tf_op jit(solution)/shard_map/ppermute | solution.py:40
  42.3 11.8 %collective-permute-start.21 = (bf16[3,9,32,128]{3,2,1,0:T(8,128)(2,1)S(1)}, bf16[3,9,32,128]{3,2,1,0:T(8,128)(2,1)S(1)}, u32[]{:S(2)}, u32[]{:S(2)}) collective-permute-start(bf16[3,9,32,128]{3,2,1,0:T(8,128)(2,1)S(1)} %shard_map.74.own), channel_id=1, source_target_pairs={{0,16},{8,24},{16,0},{24,8},{1,17},{9,25},{17,1},{25,9},{2,18},{10... | collective-permute-start | bytes 663560 | tf_op jit(solution)/shard_map/ppermute | solution.py:40
  44.9 4.3 %collective-permute-start.16 = (bf16[256,128]{1,0:T(8,128)(2,1)S(1)}, bf16[256,128]{1,0:T(8,128)(2,1)S(1)}, u32[]{:S(2)}, u32[]{:S(2)}) collective-permute-start(bf16[256,128]{1,0:T(8,128)(2,1)S(1)} %get-tuple-element.23), channel_id=1, source_target_pairs={{0,2},{1,3},{2,0},{3,1},{4,6},{5,7},{6,4},{7,5},{8,10},{9,11},{10,... | collective-permute-start | bytes 196616 | tf_op jit(solution)/shard_map/ppermute | solution.py:40
  44.9 4.8 %collective-permute-start.17 = (bf16[256,128]{1,0:T(8,128)(2,1)S(1)}, bf16[256,128]{1,0:T(8,128)(2,1)S(1)}, u32[]{:S(2)}, u32[]{:S(2)}) collective-permute-start(bf16[256,128]{1,0:T(8,128)(2,1)S(1)} %get-tuple-element.24), channel_id=1, source_target_pairs={{0,4},{1,5},{2,6},{3,7},{4,0},{5,1},{6,2},{7,3},{8,12},{9,13},{10,... | collective-permute-start | bytes 196616 | tf_op jit(solution)/shard_map/ppermute | solution.py:40
  46.9 5.2 %collective-permute-start.18 = (bf16[256,128]{1,0:T(8,128)(2,1)S(1)}, bf16[256,128]{1,0:T(8,128)(2,1)S(1)}, u32[]{:S(2)}, u32[]{:S(2)}) collective-permute-start(bf16[256,128]{1,0:T(8,128)(2,1)S(1)} %get-tuple-element.25), channel_id=1, source_target_pairs={{0,6},{1,7},{2,4},{3,5},{4,2},{5,3},{6,0},{7,1},{8,14},{9,15},{10,... | collective-permute-start | bytes 196616 | tf_op jit(solution)/shard_map/ppermute | solution.py:40
  53.4 1.6 %collective-permute-start.20 = (bf16[128,1024]{1,0:T(8,128)(2,1)S(1)}, bf16[128,1024]{1,0:T(8,128)(2,1)S(1)}, u32[]{:S(2)}, u32[]{:S(2)}) collective-permute-start(bf16[128,1024]{1,0:T(8,128)(2,1)S(1)} %get-tuple-element.28), channel_id=1, source_target_pairs={{0,1},{1,0},{2,3},{3,2},{4,5},{5,4},{6,7},{7,6},{8,9},{9,8},{10,11... | collective-permute-start | bytes 786440 | tf_op jit(solution)/shard_map/ppermute | solution.py:40

commit v6 on v5

--- a/solution.py
+++ b/solution.py
@@ -51,16 +51,16 @@
 
 CARRIERS = (
     {
-        (0, 1): 0, (0, 2): 1, (0, 3): 2,
-        (1, 0): 1, (1, 2): 3, (1, 3): 0,
-        (2, 0): 0, (2, 1): 2, (2, 3): 3,
-        (3, 0): 3, (3, 1): 1, (3, 2): 2,
+        (0, 1): 1, (0, 2): 0, (0, 3): 2,
+        (1, 0): 0, (1, 2): 3, (1, 3): 1,
+        (2, 0): 2, (2, 1): 0, (2, 3): 3,
+        (3, 0): 1, (3, 1): 3, (3, 2): 2,
     },
     {
-        (0, 1): 1, (0, 2): 2, (0, 3): 0,
-        (1, 0): 0, (1, 2): 1, (1, 3): 3,
-        (2, 0): 3, (2, 1): 0, (2, 3): 2,
-        (3, 0): 1, (3, 1): 2, (3, 2): 3,
+        (0, 1): 0, (0, 2): 2, (0, 3): 1,
+        (1, 0): 1, (1, 2): 0, (1, 3): 3,
+        (2, 0): 0, (2, 1): 3, (2, 3): 2,
+        (3, 0): 2, (3, 1): 1, (3, 2): 3,
     },
 )
 
@@ -106,17 +106,24 @@
 
 
 def mid_body(places, rows, here, local, fetched, *refs):
-    blocks, (out, w_in) = refs[:-2], refs[-2:]
+    blocks, out = refs[:-1], refs[-1]
     d, h = here[0], here[1]
-    own = d == h // 2
-    w = jnp.where(own, local[0], fetched[0])
+    w = jnp.where(d == h // 2, local[0], fetched[0])
+    lhs = jnp.concatenate([block[...] for block in blocks], axis=0)
+    mid = lax.dot_general(lhs, w, NT, preferred_element_type=F32).astype(BF16)
+    start = 0
     for (mask, first), block in zip(places, blocks):
         n = block.shape[0]
         at = pl.multiple_of((h ^ mask) * rows + first, 16)
-        out[pl.ds(at, n), :] = lax.dot_general(
-            block[...], w, NT, preferred_element_type=F32
-        ).astype(BF16)
-    w_in[...] = jnp.where(own, local[1], fetched[1])
+        out[pl.ds(at, n), :] = mid[start : start + n]
+        start += n
+
+
+def columns_body(here, local, fetched, out):
+    packed = jnp.where(here[0] == here[1] // 2, local[1], fetched[1])
+    part, width = packed.shape[0], packed.shape[1] // 2
+    out[:part] = packed[:, :width]
+    out[part:] = packed[:, width:]
 
 
 def kgrad_body(wid, group, planes, *refs):
@@ -173,18 +180,22 @@
     for s in range(3):
         pad[s, 0:wid, :] = zero
         pad[s, wid + cells : 2 * wid + cells, :] = zero
-    col = lax.broadcasted_iota(jnp.int32, (rows, 1), 0) % wid
-    for m, out in enumerate(outs):
-        first = pl.multiple_of(((h // 2) ^ m) * rows, wid)
+    col = lax.broadcasted_iota(jnp.int32, (2 * rows, 1), 0) % wid
+    chip = h // 2
+    for m in range(0, len(outs), 2):
+        first = pl.multiple_of(((chip ^ m) // 2) * 2 * rows, wid)
         lhs = jnp.concatenate(
-            [pad[s, pl.ds(first + (2 - t) * wid, rows), :] for s in range(3) for t in range(3)], axis=1
+            [pad[s, pl.ds(first + (2 - t) * wid, 2 * rows), :] for s in range(3) for t in range(3)], axis=1
         )
         y = lax.dot_general(lhs, weights[...], NT, preferred_element_type=F32)
         total = y[:, chans : 2 * chans]
-        total = total + jnp.where(col < wid - 1, pltpu.roll(y[:, :chans], rows - 1, 0), 0.0)
+        total = total + jnp.where(col < wid - 1, pltpu.roll(y[:, :chans], 2 * rows - 1, 0), 0.0)
         total = total + jnp.where(col > 0, pltpu.roll(y[:, 2 * chans :], 1, 0), 0.0)
-        keep = pre[pl.ds(first, rows), :].astype(F32) > 0
-        out[...] = jnp.where(keep, total, 0.0).astype(BF16)
+        keep = pre[pl.ds(first, 2 * rows), :].astype(F32) > 0
+        total = jnp.where(keep, total, 0.0).astype(BF16)
+        even = chip % 2 == 0
+        outs[m][...] = jnp.where(even, total[:rows], total[rows:])
+        outs[m + 1][...] = jnp.where(even, total[rows:], total[:rows])
 
 
 def partial_body(here, skip, *refs):
@@ -195,17 +206,14 @@
     for m, grad in enumerate(grads):
         lhs_ref[chip ^ m] = grad[...]
     lhs = jnp.concatenate([lhs_ref[i] for i in range(chips)], axis=1)
-    part, depth = ws[0].shape[0], lhs.shape[1]
     for m, w in enumerate(ws):
-        for half in range(2):
-            acc = lax.dot_general(
-                lhs, w[:, half * depth : (half + 1) * depth], NT, preferred_element_type=F32
-            )
-            at = pl.ds(pl.multiple_of((chip ^ m) * 2 * part + half * part, part), part)
-            here_part = jnp.where(core == 0, acc[:rows], acc[rows:])
-            there_part = jnp.where(core == 0, acc[rows:], acc[:rows])
-            own[:, at] = here_part + skip[:, at].astype(F32)
-            other[:, at] = there_part.astype(BF16)
+        acc = lax.dot_general(lhs, w[...], NT, preferred_element_type=F32)
+        width = w.shape[0]
+        at = pl.ds(pl.multiple_of((chip ^ m) * width, width), width)
+        here_part = jnp.where(core == 0, acc[:rows], acc[rows:])
+        there_part = jnp.where(core == 0, acc[rows:], acc[:rows])
+        own[:, at] = here_part + skip[:, at].astype(F32)
+        other[:, at] = there_part.astype(BF16)
 
 
 def weights_body(group, kernel, out):
@@ -257,15 +265,18 @@
     )(order(kernel, fetched))
 
     places = [(mask, first) for mask, first, _ in gathered]
-    mid, w_cols = call(
+    mid = call(
         functools.partial(mid_body, places, block),
-        [jax.ShapeDtypeStruct((cells, chans), BF16), jax.ShapeDtypeStruct(mine.shape[1:], BF16)],
+        jax.ShapeDtypeStruct((cells, chans), BF16),
         2 + len(places),
         flops=2 * cells * width * chans,
         nbytes=2 * cells * width,
     )(here, mine, fetched, *[b for _, _, b in gathered])
 
     near, far = z_swaps(mid)
+    w_cols = call(
+        columns_body, jax.ShapeDtypeStruct((w_in.shape[0], width // 2), BF16), 2, nbytes=2 * w_in.size
+    )(here, order(mine, mid), fetched)
     kernel_flops = 2 * 9 * chans * chans * cells
     early, late = (
         call(

time: 55.9 us -> 55.4 us (level)
  starting transfers between devices: 30.8 us -> 30 us
    ppermute x20, starting transfers between devices: 26.7 us -> 24.8 us  [swap(): return lax.ppermute(x, axis, [(i, i ^ mask) for i in range(n)])]
    ppermute x20, waiting for transfers between devices: 12.7 us -> 14.3 us  [swap(): return lax.ppermute(x, axis, [(i, i ^ mask) for i in range(n)])]
    ppermute x1, waiting for transfers between devices: 1.71 us -> 0.41 us  [fetch(): return lax.ppermute(mine, ('depth', 'height'), pairs)]
    ppermute x1, starting transfers between devices: 3.51 us -> 4.53 us  [fetch(): return lax.ppermute(mine, ('depth', 'height'), pairs)]
    pallas_call x1 -> x2, Pallas kernels: 1.44 us -> 1.84 us  [the longest x1 1.26 us: fast(): call(functools.partial(mid_body, places, block), jax.ShapeDtypeStruct((ce...]
  transfers between devices with their start and end apart: 22 -> 22, of which waited for: 9 -> 10; matrix products, arithmetic and copies ran while one was open for 0% -> 0% of each run, Pallas kernels for 13% -> 14%
where the time goes in v6:
time: 55.4 us; the launch traced here: 55.3 us
  starting transfers between devices  30 us (54%)
  waiting for transfers between devices  14.7 us (27%)
  Pallas kernels  8.84 us (16%)
  between operations  0.86 us (2%)
  other arithmetic  0.85 us (2%)
    ppermute x20, starting transfers between devices, swap(): return lax.ppermute(x, axis, [(i, i ^ mask) for i in range(n)])  24.8 us
    ppermute x20, waiting for transfers between devices, swap(): return lax.ppermute(x, axis, [(i, i ^ mask) for i in range(n)])  14.3 us
    ppermute x1, starting transfers between devices, fetch(): return lax.ppermute(mine, ('depth', 'height'), pairs)  4.53 us
    pallas_call x1, Pallas kernels, fast(): call(functools.partial(back_body, wid), [jax.ShapeDtypeStruct((chip_cells...  2.16 us
    pallas_call x2, Pallas kernels, fast(): call(functools.partial(kgrad_body, wid, group, len(planes)), jax.ShapeDty...  1.63 us
    pallas_call x1, Pallas kernels, fast(): call(functools.partial(mid_body, places, block), jax.ShapeDtypeStruct((ce...  1.26 us
  transfers between devices with their start and end apart: 22, of which 10 were waited for; matrix products, arithmetic and copies ran while one was open for 0% of the time, Pallas kernels for 14%

profile of v6, /device:TPU:0, one launch (start us, length us, event | category | flops | bytes accessed | tf_op | source)
XLA Modules:
  0.0 55.3 jit_solution(5043170091061505213)
XLA Ops:
  0.6 0.0 copy-start
  0.7 3.0 %collective-permute-start.2 = (bf16[128,1024]{1,0:T(8,128)(2,1)}, bf16[128,1024]{1,0:T(8,128)(2,1)S(1)}, u32[]{:S(2)}, u32[]{:S(2)}) collective-permute-start(bf16[128,1024]{1,0:T(8,128)(2,1)} %bitcast.5), channel_id=1, source_target_pairs={{0,2},{1,3},{2,0},{3,1},{4,6},{5,7},{6,4},{7,5},{8,10},{9,11},{10,... | collective-permute-start | bytes 786440 | tf_op jit(solution)/shard_map/ppermute | solution.py:40
  3.7 1.5 %collective-permute-start.4 = (bf16[128,1024]{1,0:T(8,128)(2,1)}, bf16[128,1024]{1,0:T(8,128)(2,1)S(1)}, u32[]{:S(2)}, u32[]{:S(2)}) collective-permute-start(bf16[128,1024]{1,0:T(8,128)(2,1)} %bitcast.6), channel_id=1, source_target_pairs={{0,4},{1,5},{2,6},{3,7},{4,0},{5,1},{6,2},{7,3},{8,12},{9,13},{10,... | collective-permute-start | bytes 786440 | tf_op jit(solution)/shard_map/ppermute | solution.py:40
  5.2 0.1 pad_add_fusion.here
  5.3 0.6 %shard_map.68.local = bf16[2,128,1024]{2,1,0:T(8,128)(2,1)S(1)} custom-call(s32[2]{0:T(128)S(1)} %pad_add_fusion.here, bf16[128,1024]{1,0:T(8,128)(2,1)S(1)} %constant_dynamic-slice_fusion.rows, bf16[256,1024]{1,0:T(8,128)(2,1)S(1)} %copy-done.2), custom_call_target="tpu_custom_call" | custom-call | bytes 1572864 | tf_op jit(solution)/shard_map/pallas_call | solution.py:255
  5.9 4.5 %collective-permute-start = (bf16[2,128,1024]{2,1,0:T(8,128)(2,1)S(1)}, bf16[2,128,1024]{2,1,0:T(8,128)(2,1)S(1)}, u32[]{:S(2)}, u32[]{:S(2)}) collective-permute-start(bf16[2,128,1024]{2,1,0:T(8,128)(2,1)S(1)} %shard_map.68.local), channel_id=1, source_target_pairs={{2,8},{0,16},{4,24},{8,2},{14,18},{10,26},{20,4},{16,12},{22,28},{... | collective-permute-start | bytes 1572872 | tf_op jit(solution)/shard_map/ppermute | solution.py:89
  10.5 0.1 collective-permute-start.1
  10.5 0.0 collective-permute-done.2.refs_2_
  10.6 2.5 %collective-permute-start.6 = (bf16[64,1024]{1,0:T(8,128)(2,1)S(1)}, bf16[64,1024]{1,0:T(8,128)(2,1)S(1)}, u32[]{:S(2)}, u32[]{:S(2)}) collective-permute-start(bf16[64,1024]{1,0:T(8,128)(2,1)S(1)} %slice.8), channel_id=1, source_target_pairs={{0,4},{1,5},{2,6},{3,7},{4,0},{5,1},{6,2},{7,3},{8,12},{9,13},{10,... | collective-permute-start | bytes 393224 | tf_op jit(solution)/shard_map/ppermute | solution.py:40
  13.1 0.6 %collective-permute-done.4.refs_4_ = bf16[128,1024]{1,0:T(8,128)(2,1)S(1)} collective-permute-done((bf16[128,1024]{1,0:T(8,128)(2,1)}, bf16[128,1024]{1,0:T(8,128)(2,1)S(1)}, u32[]{:S(2)}, u32[]{:S(2)}) %collective-permute-start.4) | collective-permute-done | bytes 262176 | tf_op jit(solution)/shard_map/ppermute | solution.py:40
  13.7 0.1 collective-permute-start.8
  13.7 0.1 collective-permute-start.3
  13.8 0.5 collective-permute-start.5
  14.3 4.8 %collective-permute-done.6.refs_6_ = bf16[64,1024]{1,0:T(8,128)(2,1)S(1)} collective-permute-done((bf16[64,1024]{1,0:T(8,128)(2,1)S(1)}, bf16[64,1024]{1,0:T(8,128)(2,1)S(1)}, u32[]{:S(2)}, u32[]{:S(2)}) %collective-permute-start.6) | collective-permute-done | bytes 131104 | tf_op jit(solution)/shard_map/ppermute | solution.py:40
  19.1 0.0 collective-permute-done.8.refs_8_
  19.2 0.5 collective-permute-start.9
  19.6 0.4 collective-permute-done.fetched
  20.1 0.4 collective-permute-done.7.refs_7_
  20.5 0.2 collective-permute-done.9.refs_9_
  20.7 0.0 collective-permute-done.3.refs_3_
  20.7 1.3 %shard_map.69.refs_0_.mid = bf16[1024,128]{1,0:T(8,128)(2,1)S(1)} custom-call(s32[2]{0:T(128)S(1)} %pad_add_fusion.here, bf16[2,128,1024]{2,1,0:T(8,128)(2,1)S(1)} %shard_map.68.local, bf16[2,128,1024]{2,1,0:T(8,128)(2,1)S(1)} %collective-permute-done.fetched, bf16[128,1024]{1,0:T(8,128)(2,1)S(1)} %bitcast.8, ...), custom_call_target="tpu_custom_call" | custom-call | flops 268435456 | bytes 2097152 | tf_op jit(solution)/shard_map/pallas_call | solution.py:268
  21.9 0.0 copy-start.4
  22.0 4.2 %collective-permute-start.10 = (bf16[1024,128]{1,0:T(8,128)(2,1)S(1)}, bf16[1024,128]{1,0:T(8,128)(2,1)S(1)}, u32[]{:S(2)}, u32[]{:S(2)}) collective-permute-start(bf16[1024,128]{1,0:T(8,128)(2,1)S(1)} %shard_map.69.refs_0_.mid), channel_id=1, source_target_pairs={{0,8},{8,0},{16,24},{24,16},{1,9},{9,1},{17,25},{25,17},{2,10},{10... | collective-permute-start | bytes 786440 | tf_op jit(solution)/shard_map/ppermute | solution.py:40
  26.1 0.7 %collective-permute-start.11 = (bf16[1024,128]{1,0:T(8,128)(2,1)S(1)}, bf16[1024,128]{1,0:T(8,128)(2,1)S(1)}, u32[]{:S(2)}, u32[]{:S(2)}) collective-permute-start(bf16[1024,128]{1,0:T(8,128)(2,1)S(1)} %shard_map.69.refs_0_.mid), channel_id=1, source_target_pairs={{8,16},{16,8},{9,17},{17,9},{10,18},{18,10},{11,19},{19,11},{12,20... | collective-permute-start | bytes 786440 | tf_op jit(solution)/shard_map/ppermute | solution.py:235
  26.8 0.6 %shard_map.74.refs_4_ = bf16[256,512]{1,0:T(8,128)(2,1)S(1)} custom-call(s32[2]{0:T(128)S(1)} %pad_add_fusion.here, bf16[2,128,1024]{2,1,0:T(8,128)(2,1)S(1)} %shard_map.68.local, bf16[2,128,1024]{2,1,0:T(8,128)(2,1)S(1)} %collective-permute-done.fetched), custom_call_target="tpu_custom_call" | custom-call | bytes 524288 | tf_op jit(solution)/shard_map/pallas_call | solution.py:277
  27.4 0.1 collective-permute-start.12
  27.5 0.8 %collective-permute-start.13 = (bf16[256,512]{1,0:T(8,128)(2,1)S(1)}, bf16[256,512]{1,0:T(8,128)(2,1)S(1)}, u32[]{:S(2)}, u32[]{:S(2)}) collective-permute-start(bf16[256,512]{1,0:T(8,128)(2,1)S(1)} %shard_map.74.refs_4_), channel_id=1, source_target_pairs={{0,4},{1,5},{2,6},{3,7},{4,0},{5,1},{6,2},{7,3},{8,12},{9,13},{10,... | collective-permute-start | bytes 786440 | tf_op jit(solution)/shard_map/ppermute | solution.py:40
  28.3 3.5 %collective-permute-done.10.refs_1_.near = bf16[1024,128]{1,0:T(8,128)(2,1)S(1)} collective-permute-done((bf16[1024,128]{1,0:T(8,128)(2,1)S(1)}, bf16[1024,128]{1,0:T(8,128)(2,1)S(1)}, u32[]{:S(2)}, u32[]{:S(2)}) %collective-permute-start.10) | collective-permute-done | bytes 262176 | tf_op jit(solution)/shard_map/ppermute | solution.py:40
  31.8 1.0 %shard_map.70.early = bf16[2,9,32,128]{3,2,1,0:T(8,128)(2,1)S(1)} custom-call(bf16[1024,128]{1,0:T(8,128)(2,1)S(1)} %shard_map.69.refs_0_.mid, bf16[1024,128]{1,0:T(8,128)(2,1)S(1)} %collective-permute-done.10.refs_1_.near, bf16[1024,128]{1,0:T(8,128)(2,1)S(1)} %bitcast.10), custom_call_target="tpu_custom_call" | custom-call | flops 603979776 | bytes 786432 | tf_op jit(solution)/shard_map/pallas_call | solution.py:282
  32.8 1.8 %collective-permute-start.14 = (bf16[2,9,32,128]{3,2,1,0:T(8,128)(2,1)S(1)}, bf16[2,9,32,128]{3,2,1,0:T(8,128)(2,1)S(1)}, u32[]{:S(2)}, u32[]{:S(2)}) collective-permute-start(bf16[2,9,32,128]{3,2,1,0:T(8,128)(2,1)S(1)} %shard_map.70.early), channel_id=1, source_target_pairs={{0,8},{8,0},{16,24},{24,16},{1,9},{9,1},{17,25},{25,17},{2,10},{10... | collective-permute-start | bytes 442376 | tf_op jit(solution)/shard_map/ppermute | solution.py:40
  34.6 0.1 shard_map.71.weights
  34.7 0.7 %shard_map.72.late = bf16[1,9,32,128]{3,2,1,0:T(8,128)(2,1)S(1)} custom-call(bf16[1024,128]{1,0:T(8,128)(2,1)S(1)} %collective-permute-done.11.refs_0_.far, bf16[1024,128]{1,0:T(8,128)(2,1)S(1)} %bitcast.11), custom_call_target="tpu_custom_call" | custom-call | flops 301989888 | bytes 786432 | tf_op jit(solution)/shard_map/pallas_call | solution.py:282
  35.4 2.7 %collective-permute-start.15 = (bf16[1,9,32,128]{3,2,1,0:T(8,128)(2,1)S(1)}, bf16[1,9,32,128]{3,2,1,0:T(8,128)(2,1)S(1)}, u32[]{:S(2)}, u32[]{:S(2)}) collective-permute-start(bf16[1,9,32,128]{3,2,1,0:T(8,128)(2,1)S(1)} %shard_map.72.late), channel_id=1, source_target_pairs={{0,8},{8,0},{16,24},{24,16},{1,9},{9,1},{17,25},{25,17},{2,10},{10... | collective-permute-start | bytes 221192 | tf_op jit(solution)/shard_map/ppermute | solution.py:40
  38.1 0.8 %collective-permute-start.19 = (bf16[256,512]{1,0:T(8,128)(2,1)S(1)}, bf16[256,512]{1,0:T(8,128)(2,1)S(1)}, u32[]{:S(2)}, u32[]{:S(2)}) collective-permute-start(bf16[256,512]{1,0:T(8,128)(2,1)S(1)} %shard_map.74.refs_4_), channel_id=1, source_target_pairs={{0,6},{1,7},{2,4},{3,5},{4,2},{5,3},{6,0},{7,1},{8,14},{9,15},{10,... | collective-permute-start | bytes 786440 | tf_op jit(solution)/shard_map/ppermute | solution.py:40
  38.9 2.2 %shard_map.73 = (bf16[256,128]{1,0:T(8,128)(2,1)S(1)}, bf16[256,128]{1,0:T(8,128)(2,1)S(1)}, bf16[256,128]{1,0:T(8,128)(2,1)S(1)}, bf16[256,128]{1,0:T(8,128)(2,1)S(1)}) custom-call(s32[2]{0:T(128)S(1)} %pad_add_fusion.here, bf16[1024,128]{1,0:T(8,128)(2,1)S(1)} %shard_map.69.refs_0_.mid, bf16[1024,128]{1,0:T(8,128)(2,1)S(1)} %collective-permute-done.10.refs_1_.near, ...), custom_call_target="tpu_custom_call" | custom-call | flops 905969664 | bytes 1310720 | tf_op jit(solution)/shard_map/pallas_call | solution.py:296
  41.2 0.6 %shard_map.75.own = bf16[3,9,32,128]{3,2,1,0:T(8,128)(2,1)S(1)} custom-call(s32[2]{0:T(128)S(1)} %pad_add_fusion.here, bf16[2,9,32,128]{3,2,1,0:T(8,128)(2,1)S(1)} %shard_map.70.early, bf16[1,9,32,128]{3,2,1,0:T(8,128)(2,1)S(1)} %shard_map.72.late, bf16[2,9,32,128]{3,2,1,0:T(8,128)(2,1)S(1)} %collective-permute-done.14.other_early, ...), custom_call_target="tpu_custom_call" | custom-call | bytes 3686400 | tf_op jit(solution)/shard_map/pallas_call | solution.py:304
  41.8 2.6 %collective-permute-start.21 = (bf16[3,9,32,128]{3,2,1,0:T(8,128)(2,1)S(1)}, bf16[3,9,32,128]{3,2,1,0:T(8,128)(2,1)S(1)}, u32[]{:S(2)}, u32[]{:S(2)}) collective-permute-start(bf16[3,9,32,128]{3,2,1,0:T(8,128)(2,1)S(1)} %shard_map.75.own), channel_id=1, source_target_pairs={{0,16},{8,24},{16,0},{24,8},{1,17},{9,25},{17,1},{25,9},{2,18},{10... | collective-permute-start | bytes 663560 | tf_op jit(solution)/shard_map/ppermute | solution.py:40
  44.3 0.3 collective-permute-start.16
  44.6 1.8 %collective-permute-start.17 = (bf16[256,128]{1,0:T(8,128)(2,1)S(1)}, bf16[256,128]{1,0:T(8,128)(2,1)S(1)}, u32[]{:S(2)}, u32[]{:S(2)}) collective-permute-start(bf16[256,128]{1,0:T(8,128)(2,1)S(1)} %get-tuple-element.22), channel_id=1, source_target_pairs={{0,4},{1,5},{2,6},{3,7},{4,0},{5,1},{6,2},{7,3},{8,12},{9,13},{10,... | collective-permute-start | bytes 196616 | tf_op jit(solution)/shard_map/ppermute | solution.py:40
  46.4 1.4 %collective-permute-start.18 = (bf16[256,128]{1,0:T(8,128)(2,1)S(1)}, bf16[256,128]{1,0:T(8,128)(2,1)S(1)}, u32[]{:S(2)}, u32[]{:S(2)}) collective-permute-start(bf16[256,128]{1,0:T(8,128)(2,1)S(1)} %get-tuple-element.23), channel_id=1, source_target_pairs={{0,6},{1,7},{2,4},{3,5},{4,2},{5,3},{6,0},{7,1},{8,14},{9,15},{10,... | collective-permute-start | bytes 196616 | tf_op jit(solution)/shard_map/ppermute | solution.py:40
  47.8 0.8 %collective-permute-done.16.refs_1_ = bf16[256,128]{1,0:T(8,128)(2,1)S(1)} collective-permute-done((bf16[256,128]{1,0:T(8,128)(2,1)S(1)}, bf16[256,128]{1,0:T(8,128)(2,1)S(1)}, u32[]{:S(2)}, u32[]{:S(2)}) %collective-permute-start.16) | collective-permute-done | bytes 65568 | tf_op jit(solution)/shard_map/ppermute | solution.py:40
  48.6 0.7 %collective-permute-done.17.refs_2_ = bf16[256,128]{1,0:T(8,128)(2,1)S(1)} collective-permute-done((bf16[256,128]{1,0:T(8,128)(2,1)S(1)}, bf16[256,128]{1,0:T(8,128)(2,1)S(1)}, u32[]{:S(2)}, u32[]{:S(2)}) %collective-permute-start.17) | collective-permute-done | bytes 65568 | tf_op jit(solution)/shard_map/ppermute | solution.py:40
  49.3 2.3 %collective-permute-done.18.refs_3_ = bf16[256,128]{1,0:T(8,128)(2,1)S(1)} collective-permute-done((bf16[256,128]{1,0:T(8,128)(2,1)S(1)}, bf16[256,128]{1,0:T(8,128)(2,1)S(1)}, u32[]{:S(2)}, u32[]{:S(2)}) %collective-permute-start.18) | collective-permute-done | bytes 65568 | tf_op jit(solution)/shard_map/ppermute | solution.py:40
  51.6 1.0 %shard_map.76 = (f32[128,1024]{1,0:T(8,128)S(1)}, bf16[128,1024]{1,0:T(8,128)(2,1)S(1)}) custom-call(s32[2]{0:T(128)S(1)} %pad_add_fusion.here, bf16[128,1024]{1,0:T(8,128)(2,1)S(1)} %bitcast.9, bf16[256,128]{1,0:T(8,128)(2,1)S(1)} %get-tuple-element.17.refs_0_, bf16[256,128]{1,0:T(8,128)(2,1)S(1)} %collective-permute-done.16.refs_1_, ...), custom_call_target="tpu_custom_call" | custom-call | flops 268435456 | bytes 1048576 | tf_op jit(solution)/shard_map/pallas_call | solution.py:323
  52.6 0.1 collective-permute-start.20
  52.7 0.9 %collective-permute-done.21.other = bf16[3,9,32,128]{3,2,1,0:T(8,128)(2,1)S(1)} collective-permute-done((bf16[3,9,32,128]{3,2,1,0:T(8,128)(2,1)S(1)}, bf16[3,9,32,128]{3,2,1,0:T(8,128)(2,1)S(1)}, u32[]{:S(2)}, u32[]{:S(2)}) %collective-permute-start.21) | collective-permute-done | bytes 221216 | tf_op jit(solution)/shard_map/ppermute | solution.py:40
  53.7 0.8 %shard_map.77 = f32[27,32,128]{2,1,0:T(8,128)} custom-call(bf16[3,9,32,128]{3,2,1,0:T(8,128)(2,1)S(1)} %shard_map.75.own, bf16[3,9,32,128]{3,2,1,0:T(8,128)(2,1)S(1)} %collective-permute-done.21.other), custom_call_target="tpu_custom_call" | custom-call | flops 34359738368 | bytes 884736 | tf_op jit(solution)/shard_map/pallas_call | solution.py:312
  54.5 0.8 %add_convert_fusion = bf16[128,1024]{1,0:T(8,128)(2,1)} fusion(f32[128,1024]{1,0:T(8,128)S(1)} %get-tuple-element.25, bf16[128,1024]{1,0:T(8,128)(2,1)S(1)} %collective-permute-done.20), kind=kLoop, calls=%fused_computation | loop fusion | flops 393216 | bytes 1048576 | tf_op jit(solution)/shard_map/convert_element_type | solution.py:333
  (21 shorter events, 0.1 us)
Async XLA Ops:
  0.6 4.6 %copy-start = (bf16[256,1024]{1,0:T(8,128)(2,1)S(1)}, bf16[256,1024]{1,0:T(8,128)(2,1)}, u32[]{:S(2)}) copy-start(bf16[256,1024]{1,0:T(8,128)(2,1)} %param.8) | copy-start | bytes 1572868
  0.6 4.6 %copy-start.2 = (bf16[256,1024]{1,0:T(8,128)(2,1)S(1)}, bf16[256,1024]{1,0:T(8,128)(2,1)}, u32[]{:S(2)}) copy-start(bf16[256,1024]{1,0:T(8,128)(2,1)} %w_in.1) | copy-start | bytes 1572868
  0.7 9.9 %collective-permute-start.2 = (bf16[128,1024]{1,0:T(8,128)(2,1)}, bf16[128,1024]{1,0:T(8,128)(2,1)S(1)}, u32[]{:S(2)}, u32[]{:S(2)}) collective-permute-start(bf16[128,1024]{1,0:T(8,128)(2,1)} %bitcast.5), channel_id=1, source_target_pairs={{0,2},{1,3},{2,0},{3,1},{4,6},{5,7},{6,4},{7,5},{8,10},{9,11},{10,... | collective-permute-start | bytes 786440 | tf_op jit(solution)/shard_map/ppermute | solution.py:40
  3.7 10.0 %collective-permute-start.4 = (bf16[128,1024]{1,0:T(8,128)(2,1)}, bf16[128,1024]{1,0:T(8,128)(2,1)S(1)}, u32[]{:S(2)}, u32[]{:S(2)}) collective-permute-start(bf16[128,1024]{1,0:T(8,128)(2,1)} %bitcast.6), channel_id=1, source_target_pairs={{0,4},{1,5},{2,6},{3,7},{4,0},{5,1},{6,2},{7,3},{8,12},{9,13},{10,... | collective-permute-start | bytes 786440 | tf_op jit(solution)/shard_map/ppermute | solution.py:40
  5.3 5.2 %copy-start.1 = (bf16[1,2,64,1024]{3,2,1,0:T(8,128)(2,1)S(1)}, bf16[1,2,64,1024]{3,2,1,0:T(8,128)(2,1)}, u32[]{:S(2)}) copy-start(bf16[1,2,64,1024]{3,2,1,0:T(8,128)(2,1)} %param.5) | copy-start | bytes 786436
  5.9 14.1 %collective-permute-start = (bf16[2,128,1024]{2,1,0:T(8,128)(2,1)S(1)}, bf16[2,128,1024]{2,1,0:T(8,128)(2,1)S(1)}, u32[]{:S(2)}, u32[]{:S(2)}) collective-permute-start(bf16[2,128,1024]{2,1,0:T(8,128)(2,1)S(1)} %shard_map.68.local), channel_id=1, source_target_pairs={{2,8},{0,16},{4,24},{8,2},{14,18},{10,26},{20,4},{16,12},{22,28},{... | collective-permute-start | bytes 1572872 | tf_op jit(solution)/shard_map/ppermute | solution.py:89
  10.5 3.4 %collective-permute-start.1 = (bf16[128,1024]{1,0:T(8,128)(2,1)S(1)}, bf16[128,1024]{1,0:T(8,128)(2,1)S(1)}, u32[]{:S(2)}, u32[]{:S(2)}) collective-permute-start(bf16[128,1024]{1,0:T(8,128)(2,1)S(1)} %bitcast.7), channel_id=1, source_target_pairs={{0,1},{1,0},{2,3},{3,2},{4,5},{5,4},{6,7},{7,6},{8,9},{9,8},{10,11... | collective-permute-start | bytes 786440 | tf_op jit(solution)/shard_map/ppermute | solution.py:40
  10.6 8.6 %collective-permute-start.6 = (bf16[64,1024]{1,0:T(8,128)(2,1)S(1)}, bf16[64,1024]{1,0:T(8,128)(2,1)S(1)}, u32[]{:S(2)}, u32[]{:S(2)}) collective-permute-start(bf16[64,1024]{1,0:T(8,128)(2,1)S(1)} %slice.8), channel_id=1, source_target_pairs={{0,4},{1,5},{2,6},{3,7},{4,0},{5,1},{6,2},{7,3},{8,12},{9,13},{10,... | collective-permute-start | bytes 393224 | tf_op jit(solution)/shard_map/ppermute | solution.py:40
  13.7 5.5 %collective-permute-start.8 = (bf16[64,1024]{1,0:T(8,128)(2,1)S(1)}, bf16[64,1024]{1,0:T(8,128)(2,1)S(1)}, u32[]{:S(2)}, u32[]{:S(2)}) collective-permute-start(bf16[64,1024]{1,0:T(8,128)(2,1)S(1)} %slice.9), channel_id=1, source_target_pairs={{0,2},{1,3},{2,0},{3,1},{4,6},{5,7},{6,4},{7,5},{8,10},{9,11},{10,... | collective-permute-start | bytes 393224 | tf_op jit(solution)/shard_map/ppermute | solution.py:40
  13.7 6.9 %collective-permute-start.3 = (bf16[128,1024]{1,0:T(8,128)(2,1)S(1)}, bf16[128,1024]{1,0:T(8,128)(2,1)S(1)}, u32[]{:S(2)}, u32[]{:S(2)}) collective-permute-start(bf16[128,1024]{1,0:T(8,128)(2,1)S(1)} %collective-permute-done.2.refs_2_), channel_id=1, source_target_pairs={{0,1},{1,0},{2,3},{3,2},{4,5},{5,4},{6,7},{7,6},{8,9},{9,8},{10,11... | collective-permute-start | bytes 786440 | tf_op jit(solution)/shard_map/ppermute | solution.py:40
  13.8 6.8 %collective-permute-start.5 = (bf16[128,1024]{1,0:T(8,128)(2,1)S(1)}, bf16[128,1024]{1,0:T(8,128)(2,1)S(1)}, u32[]{:S(2)}, u32[]{:S(2)}) collective-permute-start(bf16[128,1024]{1,0:T(8,128)(2,1)S(1)} %collective-permute-done.4.refs_4_), channel_id=1, source_target_pairs={{0,1},{1,0},{2,3},{3,2},{4,5},{5,4},{6,7},{7,6},{8,9},{9,8},{10,11... | collective-permute-start | bytes 786440 | tf_op jit(solution)/shard_map/ppermute | solution.py:40
  19.1 1.3 %collective-permute-start.7 = (bf16[64,1024]{1,0:T(8,128)(2,1)S(1)}, bf16[64,1024]{1,0:T(8,128)(2,1)S(1)}, u32[]{:S(2)}, u32[]{:S(2)}) collective-permute-start(bf16[64,1024]{1,0:T(8,128)(2,1)S(1)} %collective-permute-done.6.refs_6_), channel_id=1, source_target_pairs={{0,1},{1,0},{2,3},{3,2},{4,5},{5,4},{6,7},{7,6},{8,9},{9,8},{10,11... | collective-permute-start | bytes 393224 | tf_op jit(solution)/shard_map/ppermute | solution.py:40
  19.2 1.5 %collective-permute-start.9 = (bf16[64,1024]{1,0:T(8,128)(2,1)S(1)}, bf16[64,1024]{1,0:T(8,128)(2,1)S(1)}, u32[]{:S(2)}, u32[]{:S(2)}) collective-permute-start(bf16[64,1024]{1,0:T(8,128)(2,1)S(1)} %collective-permute-done.8.refs_8_), channel_id=1, source_target_pairs={{0,1},{1,0},{2,3},{3,2},{4,5},{5,4},{6,7},{7,6},{8,9},{9,8},{10,11... | collective-permute-start | bytes 393224 | tf_op jit(solution)/shard_map/ppermute | solution.py:40
  21.9 9.8 %copy-start.4 = (bf16[1,16,64,128]{3,2,1,0:T(8,128)(2,1)S(1)}, bf16[1,16,64,128]{3,2,1,0:T(8,128)(2,1)}, u32[]{:S(2)}) copy-start(bf16[1,16,64,128]{3,2,1,0:T(8,128)(2,1)} %param.6) | copy-start | bytes 786436
  22.0 9.8 %collective-permute-start.10 = (bf16[1024,128]{1,0:T(8,128)(2,1)S(1)}, bf16[1024,128]{1,0:T(8,128)(2,1)S(1)}, u32[]{:S(2)}, u32[]{:S(2)}) collective-permute-start(bf16[1024,128]{1,0:T(8,128)(2,1)S(1)} %shard_map.69.refs_0_.mid), channel_id=1, source_target_pairs={{0,8},{8,0},{16,24},{24,16},{1,9},{9,1},{17,25},{25,17},{2,10},{10... | collective-permute-start | bytes 786440 | tf_op jit(solution)/shard_map/ppermute | solution.py:40
  26.1 8.6 %collective-permute-start.11 = (bf16[1024,128]{1,0:T(8,128)(2,1)S(1)}, bf16[1024,128]{1,0:T(8,128)(2,1)S(1)}, u32[]{:S(2)}, u32[]{:S(2)}) collective-permute-start(bf16[1024,128]{1,0:T(8,128)(2,1)S(1)} %shard_map.69.refs_0_.mid), channel_id=1, source_target_pairs={{8,16},{16,8},{9,17},{17,9},{10,18},{18,10},{11,19},{19,11},{12,20... | collective-permute-start | bytes 786440 | tf_op jit(solution)/shard_map/ppermute | solution.py:235
  27.4 13.7 %collective-permute-start.12 = (bf16[256,512]{1,0:T(8,128)(2,1)S(1)}, bf16[256,512]{1,0:T(8,128)(2,1)S(1)}, u32[]{:S(2)}, u32[]{:S(2)}) collective-permute-start(bf16[256,512]{1,0:T(8,128)(2,1)S(1)} %shard_map.74.refs_4_), channel_id=1, source_target_pairs={{0,2},{1,3},{2,0},{3,1},{4,6},{5,7},{6,4},{7,5},{8,10},{9,11},{10,... | collective-permute-start | bytes 786440 | tf_op jit(solution)/shard_map/ppermute | solution.py:40
  27.5 13.6 %collective-permute-start.13 = (bf16[256,512]{1,0:T(8,128)(2,1)S(1)}, bf16[256,512]{1,0:T(8,128)(2,1)S(1)}, u32[]{:S(2)}, u32[]{:S(2)}) collective-permute-start(bf16[256,512]{1,0:T(8,128)(2,1)S(1)} %shard_map.74.refs_4_), channel_id=1, source_target_pairs={{0,4},{1,5},{2,6},{3,7},{4,0},{5,1},{6,2},{7,3},{8,12},{9,13},{10,... | collective-permute-start | bytes 786440 | tf_op jit(solution)/shard_map/ppermute | solution.py:40
  31.8 2.8 %copy-start.3 = (bf16[27,32,128]{2,1,0:T(8,128)(2,1)S(1)}, bf16[27,32,128]{2,1,0:T(8,128)(2,1)}, u32[]{:S(2)}) copy-start(bf16[27,32,128]{2,1,0:T(8,128)(2,1)} %kernel) | copy-start | bytes 663556
  32.8 8.4 %collective-permute-start.14 = (bf16[2,9,32,128]{3,2,1,0:T(8,128)(2,1)S(1)}, bf16[2,9,32,128]{3,2,1,0:T(8,128)(2,1)S(1)}, u32[]{:S(2)}, u32[]{:S(2)}) collective-permute-start(bf16[2,9,32,128]{3,2,1,0:T(8,128)(2,1)S(1)} %shard_map.70.early), channel_id=1, source_target_pairs={{0,8},{8,0},{16,24},{24,16},{1,9},{9,1},{17,25},{25,17},{2,10},{10... | collective-permute-start | bytes 442376 | tf_op jit(solution)/shard_map/ppermute | solution.py:40
  35.4 5.7 %collective-permute-start.15 = (bf16[1,9,32,128]{3,2,1,0:T(8,128)(2,1)S(1)}, bf16[1,9,32,128]{3,2,1,0:T(8,128)(2,1)S(1)}, u32[]{:S(2)}, u32[]{:S(2)}) collective-permute-start(bf16[1,9,32,128]{3,2,1,0:T(8,128)(2,1)S(1)} %shard_map.72.late), channel_id=1, source_target_pairs={{0,8},{8,0},{16,24},{24,16},{1,9},{9,1},{17,25},{25,17},{2,10},{10... | collective-permute-start | bytes 221192 | tf_op jit(solution)/shard_map/ppermute | solution.py:40
  38.1 13.5 %collective-permute-start.19 = (bf16[256,512]{1,0:T(8,128)(2,1)S(1)}, bf16[256,512]{1,0:T(8,128)(2,1)S(1)}, u32[]{:S(2)}, u32[]{:S(2)}) collective-permute-start(bf16[256,512]{1,0:T(8,128)(2,1)S(1)} %shard_map.74.refs_4_), channel_id=1, source_target_pairs={{0,6},{1,7},{2,4},{3,5},{4,2},{5,3},{6,0},{7,1},{8,14},{9,15},{10,... | collective-permute-start | bytes 786440 | tf_op jit(solution)/shard_map/ppermute | solution.py:40
  41.8 11.9 %collective-permute-start.21 = (bf16[3,9,32,128]{3,2,1,0:T(8,128)(2,1)S(1)}, bf16[3,9,32,128]{3,2,1,0:T(8,128)(2,1)S(1)}, u32[]{:S(2)}, u32[]{:S(2)}) collective-permute-start(bf16[3,9,32,128]{3,2,1,0:T(8,128)(2,1)S(1)} %shard_map.75.own), channel_id=1, source_target_pairs={{0,16},{8,24},{16,0},{24,8},{1,17},{9,25},{17,1},{25,9},{2,18},{10... | collective-permute-start | bytes 663560 | tf_op jit(solution)/shard_map/ppermute | solution.py:40
  44.3 4.3 %collective-permute-start.16 = (bf16[256,128]{1,0:T(8,128)(2,1)S(1)}, bf16[256,128]{1,0:T(8,128)(2,1)S(1)}, u32[]{:S(2)}, u32[]{:S(2)}) collective-permute-start(bf16[256,128]{1,0:T(8,128)(2,1)S(1)} %get-tuple-element.21), channel_id=1, source_target_pairs={{0,2},{1,3},{2,0},{3,1},{4,6},{5,7},{6,4},{7,5},{8,10},{9,11},{10,... | collective-permute-start | bytes 196616 | tf_op jit(solution)/shard_map/ppermute | solution.py:40
  44.6 4.7 %collective-permute-start.17 = (bf16[256,128]{1,0:T(8,128)(2,1)S(1)}, bf16[256,128]{1,0:T(8,128)(2,1)S(1)}, u32[]{:S(2)}, u32[]{:S(2)}) collective-permute-start(bf16[256,128]{1,0:T(8,128)(2,1)S(1)} %get-tuple-element.22), channel_id=1, source_target_pairs={{0,4},{1,5},{2,6},{3,7},{4,0},{5,1},{6,2},{7,3},{8,12},{9,13},{10,... | collective-permute-start | bytes 196616 | tf_op jit(solution)/shard_map/ppermute | solution.py:40
  46.4 5.2 %collective-permute-start.18 = (bf16[256,128]{1,0:T(8,128)(2,1)S(1)}, bf16[256,128]{1,0:T(8,128)(2,1)S(1)}, u32[]{:S(2)}, u32[]{:S(2)}) collective-permute-start(bf16[256,128]{1,0:T(8,128)(2,1)S(1)} %get-tuple-element.23), channel_id=1, source_target_pairs={{0,6},{1,7},{2,4},{3,5},{4,2},{5,3},{6,0},{7,1},{8,14},{9,15},{10,... | collective-permute-start | bytes 196616 | tf_op jit(solution)/shard_map/ppermute | solution.py:40
  52.6 1.9 %collective-permute-start.20 = (bf16[128,1024]{1,0:T(8,128)(2,1)S(1)}, bf16[128,1024]{1,0:T(8,128)(2,1)S(1)}, u32[]{:S(2)}, u32[]{:S(2)}) collective-permute-start(bf16[128,1024]{1,0:T(8,128)(2,1)S(1)} %get-tuple-element.26), channel_id=1, source_target_pairs={{0,1},{1,0},{2,3},{3,2},{4,5},{5,4},{6,7},{7,6},{8,9},{9,8},{10,11... | collective-permute-start | bytes 786440 | tf_op jit(solution)/shard_map/ppermute | solution.py:40

commit v7 on v6

--- a/solution.py
+++ b/solution.py
@@ -276,7 +276,7 @@
     near, far = z_swaps(mid)
     w_cols = call(
         columns_body, jax.ShapeDtypeStruct((w_in.shape[0], width // 2), BF16), 2, nbytes=2 * w_in.size
-    )(here, order(mine, mid), fetched)
+    )(here, mine, fetched)
     kernel_flops = 2 * 9 * chans * chans * cells
     early, late = (
         call(
@@ -291,7 +291,7 @@
         for planes in ((mid, near), (far,))
     )
     w_blocks = [w_cols] + [swap(w_cols, "height", 2 * m) for m in (1, 2)]
-    w_blocks.append(swap(order(w_cols, late), "height", 6))
+    w_blocks.append(swap(w_blocks[1], "height", 4))
     chip_cells = 2 * block
     back = call(
         functools.partial(back_body, wid),

time: 55.4 us -> 55.4 us (level)
  transfers between devices with their start and end apart: 22 -> 22, of which waited for: 10 -> 11; matrix products, arithmetic and copies ran while one was open for 0% -> 0% of each run, Pallas kernels for 14% -> 14%
where the time goes in v7:
time: 55.4 us; the launch traced here: 55.3 us
  starting transfers between devices  29.9 us (54%)
  waiting for transfers between devices  14.8 us (27%)
  Pallas kernels  8.84 us (16%)
  other arithmetic  0.85 us (2%)
  between operations  0.84 us (2%)
    ppermute x20, starting transfers between devices, swap(): return lax.ppermute(x, axis, [(i, i ^ mask) for i in range(n)])  24.7 us
    ppermute x20, waiting for transfers between devices, swap(): return lax.ppermute(x, axis, [(i, i ^ mask) for i in range(n)])  14.4 us
    ppermute x1, starting transfers between devices, fetch(): return lax.ppermute(mine, ('depth', 'height'), pairs)  4.53 us
    pallas_call x1, Pallas kernels, fast(): call(functools.partial(back_body, wid), [jax.ShapeDtypeStruct((chip_cells...  2.16 us
    pallas_call x2, Pallas kernels, fast(): call(functools.partial(kgrad_body, wid, group, len(planes)), jax.ShapeDty...  1.63 us
    pallas_call x1, Pallas kernels, fast(): call(functools.partial(mid_body, places, block), jax.ShapeDtypeStruct((ce...  1.26 us
  transfers between devices with their start and end apart: 22, of which 11 were waited for; matrix products, arithmetic and copies ran while one was open for 0% of the time, Pallas kernels for 14%

profile of v7, /device:TPU:0, one launch (start us, length us, event | category | flops | bytes accessed | tf_op | source)
XLA Modules:
  0.0 55.3 jit_solution(3693807341441187200)
XLA Ops:
  0.6 0.0 copy-start
  0.7 3.0 %collective-permute-start.2 = (bf16[128,1024]{1,0:T(8,128)(2,1)}, bf16[128,1024]{1,0:T(8,128)(2,1)S(1)}, u32[]{:S(2)}, u32[]{:S(2)}) collective-permute-start(bf16[128,1024]{1,0:T(8,128)(2,1)} %bitcast.5), channel_id=1, source_target_pairs={{0,2},{1,3},{2,0},{3,1},{4,6},{5,7},{6,4},{7,5},{8,10},{9,11},{10,... | collective-permute-start | bytes 786440 | tf_op jit(solution)/shard_map/ppermute | solution.py:40
  3.7 1.5 %collective-permute-start.4 = (bf16[128,1024]{1,0:T(8,128)(2,1)}, bf16[128,1024]{1,0:T(8,128)(2,1)S(1)}, u32[]{:S(2)}, u32[]{:S(2)}) collective-permute-start(bf16[128,1024]{1,0:T(8,128)(2,1)} %bitcast.6), channel_id=1, source_target_pairs={{0,4},{1,5},{2,6},{3,7},{4,0},{5,1},{6,2},{7,3},{8,12},{9,13},{10,... | collective-permute-start | bytes 786440 | tf_op jit(solution)/shard_map/ppermute | solution.py:40
  5.2 0.1 pad_add_fusion.here
  5.3 0.6 %shard_map.68.local = bf16[2,128,1024]{2,1,0:T(8,128)(2,1)S(1)} custom-call(s32[2]{0:T(128)S(1)} %pad_add_fusion.here, bf16[128,1024]{1,0:T(8,128)(2,1)S(1)} %constant_dynamic-slice_fusion.rows, bf16[256,1024]{1,0:T(8,128)(2,1)S(1)} %copy-done.2), custom_call_target="tpu_custom_call" | custom-call | bytes 1572864 | tf_op jit(solution)/shard_map/pallas_call | solution.py:255
  5.9 4.5 %collective-permute-start = (bf16[2,128,1024]{2,1,0:T(8,128)(2,1)S(1)}, bf16[2,128,1024]{2,1,0:T(8,128)(2,1)S(1)}, u32[]{:S(2)}, u32[]{:S(2)}) collective-permute-start(bf16[2,128,1024]{2,1,0:T(8,128)(2,1)S(1)} %shard_map.68.local), channel_id=1, source_target_pairs={{2,8},{0,16},{4,24},{8,2},{14,18},{10,26},{20,4},{16,12},{22,28},{... | collective-permute-start | bytes 1572872 | tf_op jit(solution)/shard_map/ppermute | solution.py:89
  10.5 0.1 collective-permute-start.1
  10.5 0.0 collective-permute-done.2.refs_2_
  10.6 2.5 %collective-permute-start.6 = (bf16[64,1024]{1,0:T(8,128)(2,1)S(1)}, bf16[64,1024]{1,0:T(8,128)(2,1)S(1)}, u32[]{:S(2)}, u32[]{:S(2)}) collective-permute-start(bf16[64,1024]{1,0:T(8,128)(2,1)S(1)} %slice.8), channel_id=1, source_target_pairs={{0,4},{1,5},{2,6},{3,7},{4,0},{5,1},{6,2},{7,3},{8,12},{9,13},{10,... | collective-permute-start | bytes 393224 | tf_op jit(solution)/shard_map/ppermute | solution.py:40
  13.1 0.6 %collective-permute-done.4.refs_4_ = bf16[128,1024]{1,0:T(8,128)(2,1)S(1)} collective-permute-done((bf16[128,1024]{1,0:T(8,128)(2,1)}, bf16[128,1024]{1,0:T(8,128)(2,1)S(1)}, u32[]{:S(2)}, u32[]{:S(2)}) %collective-permute-start.4) | collective-permute-done | bytes 262176 | tf_op jit(solution)/shard_map/ppermute | solution.py:40
  13.7 0.1 collective-permute-start.8
  13.7 0.1 collective-permute-start.3
  13.8 0.5 collective-permute-start.5
  14.3 4.8 %collective-permute-done.6.refs_6_ = bf16[64,1024]{1,0:T(8,128)(2,1)S(1)} collective-permute-done((bf16[64,1024]{1,0:T(8,128)(2,1)S(1)}, bf16[64,1024]{1,0:T(8,128)(2,1)S(1)}, u32[]{:S(2)}, u32[]{:S(2)}) %collective-permute-start.6) | collective-permute-done | bytes 131104 | tf_op jit(solution)/shard_map/ppermute | solution.py:40
  19.1 0.0 collective-permute-done.8.refs_8_
  19.2 0.5 collective-permute-start.9
  19.6 0.4 collective-permute-done.fetched
  20.1 0.4 collective-permute-done.7.refs_7_
  20.5 0.2 collective-permute-done.9.refs_9_
  20.7 0.0 collective-permute-done.3.refs_3_
  20.7 1.3 %shard_map.69.refs_0_.mid = bf16[1024,128]{1,0:T(8,128)(2,1)S(1)} custom-call(s32[2]{0:T(128)S(1)} %pad_add_fusion.here, bf16[2,128,1024]{2,1,0:T(8,128)(2,1)S(1)} %shard_map.68.local, bf16[2,128,1024]{2,1,0:T(8,128)(2,1)S(1)} %collective-permute-done.fetched, bf16[128,1024]{1,0:T(8,128)(2,1)S(1)} %bitcast.8, ...), custom_call_target="tpu_custom_call" | custom-call | flops 268435456 | bytes 2097152 | tf_op jit(solution)/shard_map/pallas_call | solution.py:268
  21.9 0.0 copy-start.4
  22.0 4.2 %collective-permute-start.10 = (bf16[1024,128]{1,0:T(8,128)(2,1)S(1)}, bf16[1024,128]{1,0:T(8,128)(2,1)S(1)}, u32[]{:S(2)}, u32[]{:S(2)}) collective-permute-start(bf16[1024,128]{1,0:T(8,128)(2,1)S(1)} %shard_map.69.refs_0_.mid), channel_id=1, source_target_pairs={{0,8},{8,0},{16,24},{24,16},{1,9},{9,1},{17,25},{25,17},{2,10},{10... | collective-permute-start | bytes 786440 | tf_op jit(solution)/shard_map/ppermute | solution.py:40
  26.1 0.7 %collective-permute-start.11 = (bf16[1024,128]{1,0:T(8,128)(2,1)S(1)}, bf16[1024,128]{1,0:T(8,128)(2,1)S(1)}, u32[]{:S(2)}, u32[]{:S(2)}) collective-permute-start(bf16[1024,128]{1,0:T(8,128)(2,1)S(1)} %shard_map.69.refs_0_.mid), channel_id=1, source_target_pairs={{8,16},{16,8},{9,17},{17,9},{10,18},{18,10},{11,19},{19,11},{12,20... | collective-permute-start | bytes 786440 | tf_op jit(solution)/shard_map/ppermute | solution.py:235
  26.8 0.6 %shard_map.74.refs_4_ = bf16[256,512]{1,0:T(8,128)(2,1)S(1)} custom-call(s32[2]{0:T(128)S(1)} %pad_add_fusion.here, bf16[2,128,1024]{2,1,0:T(8,128)(2,1)S(1)} %shard_map.68.local, bf16[2,128,1024]{2,1,0:T(8,128)(2,1)S(1)} %collective-permute-done.fetched), custom_call_target="tpu_custom_call" | custom-call | bytes 524288 | tf_op jit(solution)/shard_map/pallas_call | solution.py:277
  27.4 0.1 collective-permute-start.12
  27.5 0.8 %collective-permute-start.13 = (bf16[256,512]{1,0:T(8,128)(2,1)S(1)}, bf16[256,512]{1,0:T(8,128)(2,1)S(1)}, u32[]{:S(2)}, u32[]{:S(2)}) collective-permute-start(bf16[256,512]{1,0:T(8,128)(2,1)S(1)} %shard_map.74.refs_4_), channel_id=1, source_target_pairs={{0,4},{1,5},{2,6},{3,7},{4,0},{5,1},{6,2},{7,3},{8,12},{9,13},{10,... | collective-permute-start | bytes 786440 | tf_op jit(solution)/shard_map/ppermute | solution.py:40
  28.3 3.5 %collective-permute-done.10.refs_1_.near = bf16[1024,128]{1,0:T(8,128)(2,1)S(1)} collective-permute-done((bf16[1024,128]{1,0:T(8,128)(2,1)S(1)}, bf16[1024,128]{1,0:T(8,128)(2,1)S(1)}, u32[]{:S(2)}, u32[]{:S(2)}) %collective-permute-start.10) | collective-permute-done | bytes 262176 | tf_op jit(solution)/shard_map/ppermute | solution.py:40
  31.8 1.0 %shard_map.70.early = bf16[2,9,32,128]{3,2,1,0:T(8,128)(2,1)S(1)} custom-call(bf16[1024,128]{1,0:T(8,128)(2,1)S(1)} %shard_map.69.refs_0_.mid, bf16[1024,128]{1,0:T(8,128)(2,1)S(1)} %collective-permute-done.10.refs_1_.near, bf16[1024,128]{1,0:T(8,128)(2,1)S(1)} %bitcast.10), custom_call_target="tpu_custom_call" | custom-call | flops 603979776 | bytes 786432 | tf_op jit(solution)/shard_map/pallas_call | solution.py:282
  32.8 1.8 %collective-permute-start.14 = (bf16[2,9,32,128]{3,2,1,0:T(8,128)(2,1)S(1)}, bf16[2,9,32,128]{3,2,1,0:T(8,128)(2,1)S(1)}, u32[]{:S(2)}, u32[]{:S(2)}) collective-permute-start(bf16[2,9,32,128]{3,2,1,0:T(8,128)(2,1)S(1)} %shard_map.70.early), channel_id=1, source_target_pairs={{0,8},{8,0},{16,24},{24,16},{1,9},{9,1},{17,25},{25,17},{2,10},{10... | collective-permute-start | bytes 442376 | tf_op jit(solution)/shard_map/ppermute | solution.py:40
  34.6 0.1 shard_map.71.weights
  34.7 0.7 %shard_map.72.late = bf16[1,9,32,128]{3,2,1,0:T(8,128)(2,1)S(1)} custom-call(bf16[1024,128]{1,0:T(8,128)(2,1)S(1)} %collective-permute-done.11.refs_0_.far, bf16[1024,128]{1,0:T(8,128)(2,1)S(1)} %bitcast.11), custom_call_target="tpu_custom_call" | custom-call | flops 301989888 | bytes 786432 | tf_op jit(solution)/shard_map/pallas_call | solution.py:282
  35.4 2.7 %collective-permute-start.15 = (bf16[1,9,32,128]{3,2,1,0:T(8,128)(2,1)S(1)}, bf16[1,9,32,128]{3,2,1,0:T(8,128)(2,1)S(1)}, u32[]{:S(2)}, u32[]{:S(2)}) collective-permute-start(bf16[1,9,32,128]{3,2,1,0:T(8,128)(2,1)S(1)} %shard_map.72.late), channel_id=1, source_target_pairs={{0,8},{8,0},{16,24},{24,16},{1,9},{9,1},{17,25},{25,17},{2,10},{10... | collective-permute-start | bytes 221192 | tf_op jit(solution)/shard_map/ppermute | solution.py:40
  38.1 2.2 %shard_map.73 = (bf16[256,128]{1,0:T(8,128)(2,1)S(1)}, bf16[256,128]{1,0:T(8,128)(2,1)S(1)}, bf16[256,128]{1,0:T(8,128)(2,1)S(1)}, bf16[256,128]{1,0:T(8,128)(2,1)S(1)}) custom-call(s32[2]{0:T(128)S(1)} %pad_add_fusion.here, bf16[1024,128]{1,0:T(8,128)(2,1)S(1)} %shard_map.69.refs_0_.mid, bf16[1024,128]{1,0:T(8,128)(2,1)S(1)} %collective-permute-done.10.refs_1_.near, ...), custom_call_target="tpu_custom_call" | custom-call | flops 905969664 | bytes 1310720 | tf_op jit(solution)/shard_map/pallas_call | solution.py:296
  40.3 0.1 collective-permute-done.15.other_late
  40.5 0.6 %shard_map.75.own = bf16[3,9,32,128]{3,2,1,0:T(8,128)(2,1)S(1)} custom-call(s32[2]{0:T(128)S(1)} %pad_add_fusion.here, bf16[2,9,32,128]{3,2,1,0:T(8,128)(2,1)S(1)} %shard_map.70.early, bf16[1,9,32,128]{3,2,1,0:T(8,128)(2,1)S(1)} %shard_map.72.late, bf16[2,9,32,128]{3,2,1,0:T(8,128)(2,1)S(1)} %collective-permute-done.14.other_early, ...), custom_call_target="tpu_custom_call" | custom-call | bytes 3686400 | tf_op jit(solution)/shard_map/pallas_call | solution.py:304
  41.1 3.3 %collective-permute-start.21 = (bf16[3,9,32,128]{3,2,1,0:T(8,128)(2,1)S(1)}, bf16[3,9,32,128]{3,2,1,0:T(8,128)(2,1)S(1)}, u32[]{:S(2)}, u32[]{:S(2)}) collective-permute-start(bf16[3,9,32,128]{3,2,1,0:T(8,128)(2,1)S(1)} %shard_map.75.own), channel_id=1, source_target_pairs={{0,16},{8,24},{16,0},{24,8},{1,17},{9,25},{17,1},{25,9},{2,18},{10... | collective-permute-start | bytes 663560 | tf_op jit(solution)/shard_map/ppermute | solution.py:40
  44.3 0.6 %collective-permute-start.16 = (bf16[256,128]{1,0:T(8,128)(2,1)S(1)}, bf16[256,128]{1,0:T(8,128)(2,1)S(1)}, u32[]{:S(2)}, u32[]{:S(2)}) collective-permute-start(bf16[256,128]{1,0:T(8,128)(2,1)S(1)} %get-tuple-element.18), channel_id=1, source_target_pairs={{0,2},{1,3},{2,0},{3,1},{4,6},{5,7},{6,4},{7,5},{8,10},{9,11},{10,... | collective-permute-start | bytes 196616 | tf_op jit(solution)/shard_map/ppermute | solution.py:40
  44.9 1.6 %collective-permute-start.17 = (bf16[256,128]{1,0:T(8,128)(2,1)S(1)}, bf16[256,128]{1,0:T(8,128)(2,1)S(1)}, u32[]{:S(2)}, u32[]{:S(2)}) collective-permute-start(bf16[256,128]{1,0:T(8,128)(2,1)S(1)} %get-tuple-element.19), channel_id=1, source_target_pairs={{0,4},{1,5},{2,6},{3,7},{4,0},{5,1},{6,2},{7,3},{8,12},{9,13},{10,... | collective-permute-start | bytes 196616 | tf_op jit(solution)/shard_map/ppermute | solution.py:40
  46.4 1.4 %collective-permute-start.18 = (bf16[256,128]{1,0:T(8,128)(2,1)S(1)}, bf16[256,128]{1,0:T(8,128)(2,1)S(1)}, u32[]{:S(2)}, u32[]{:S(2)}) collective-permute-start(bf16[256,128]{1,0:T(8,128)(2,1)S(1)} %get-tuple-element.20), channel_id=1, source_target_pairs={{0,6},{1,7},{2,4},{3,5},{4,2},{5,3},{6,0},{7,1},{8,14},{9,15},{10,... | collective-permute-start | bytes 196616 | tf_op jit(solution)/shard_map/ppermute | solution.py:40
  47.8 0.8 %collective-permute-done.16.refs_1_ = bf16[256,128]{1,0:T(8,128)(2,1)S(1)} collective-permute-done((bf16[256,128]{1,0:T(8,128)(2,1)S(1)}, bf16[256,128]{1,0:T(8,128)(2,1)S(1)}, u32[]{:S(2)}, u32[]{:S(2)}) %collective-permute-start.16) | collective-permute-done | bytes 65568 | tf_op jit(solution)/shard_map/ppermute | solution.py:40
  48.6 0.8 %collective-permute-done.17.refs_2_ = bf16[256,128]{1,0:T(8,128)(2,1)S(1)} collective-permute-done((bf16[256,128]{1,0:T(8,128)(2,1)S(1)}, bf16[256,128]{1,0:T(8,128)(2,1)S(1)}, u32[]{:S(2)}, u32[]{:S(2)}) %collective-permute-start.17) | collective-permute-done | bytes 65568 | tf_op jit(solution)/shard_map/ppermute | solution.py:40
  49.4 2.2 %collective-permute-done.18.refs_3_ = bf16[256,128]{1,0:T(8,128)(2,1)S(1)} collective-permute-done((bf16[256,128]{1,0:T(8,128)(2,1)S(1)}, bf16[256,128]{1,0:T(8,128)(2,1)S(1)}, u32[]{:S(2)}, u32[]{:S(2)}) %collective-permute-start.18) | collective-permute-done | bytes 65568 | tf_op jit(solution)/shard_map/ppermute | solution.py:40
  51.6 1.0 %shard_map.76 = (f32[128,1024]{1,0:T(8,128)S(1)}, bf16[128,1024]{1,0:T(8,128)(2,1)S(1)}) custom-call(s32[2]{0:T(128)S(1)} %pad_add_fusion.here, bf16[128,1024]{1,0:T(8,128)(2,1)S(1)} %bitcast.9, bf16[256,128]{1,0:T(8,128)(2,1)S(1)} %get-tuple-element.15.refs_0_, bf16[256,128]{1,0:T(8,128)(2,1)S(1)} %collective-permute-done.16.refs_1_, ...), custom_call_target="tpu_custom_call" | custom-call | flops 268435456 | bytes 1048576 | tf_op jit(solution)/shard_map/pallas_call | solution.py:323
  52.6 0.1 collective-permute-start.20
  52.7 0.9 %collective-permute-done.21.other = bf16[3,9,32,128]{3,2,1,0:T(8,128)(2,1)S(1)} collective-permute-done((bf16[3,9,32,128]{3,2,1,0:T(8,128)(2,1)S(1)}, bf16[3,9,32,128]{3,2,1,0:T(8,128)(2,1)S(1)}, u32[]{:S(2)}, u32[]{:S(2)}) %collective-permute-start.21) | collective-permute-done | bytes 221216 | tf_op jit(solution)/shard_map/ppermute | solution.py:40
  53.7 0.8 %shard_map.77 = f32[27,32,128]{2,1,0:T(8,128)} custom-call(bf16[3,9,32,128]{3,2,1,0:T(8,128)(2,1)S(1)} %shard_map.75.own, bf16[3,9,32,128]{3,2,1,0:T(8,128)(2,1)S(1)} %collective-permute-done.21.other), custom_call_target="tpu_custom_call" | custom-call | flops 34359738368 | bytes 884736 | tf_op jit(solution)/shard_map/pallas_call | solution.py:312
  54.5 0.8 %add_convert_fusion = bf16[128,1024]{1,0:T(8,128)(2,1)} fusion(f32[128,1024]{1,0:T(8,128)S(1)} %get-tuple-element.21, bf16[128,1024]{1,0:T(8,128)(2,1)S(1)} %collective-permute-done.20), kind=kLoop, calls=%fused_computation | loop fusion | flops 393216 | bytes 1048576 | tf_op jit(solution)/shard_map/convert_element_type | solution.py:333
  (21 shorter events, 0.1 us)
Async XLA Ops:
  0.6 4.6 %copy-start = (bf16[256,1024]{1,0:T(8,128)(2,1)S(1)}, bf16[256,1024]{1,0:T(8,128)(2,1)}, u32[]{:S(2)}) copy-start(bf16[256,1024]{1,0:T(8,128)(2,1)} %param.8) | copy-start | bytes 1572868
  0.6 4.6 %copy-start.2 = (bf16[256,1024]{1,0:T(8,128)(2,1)S(1)}, bf16[256,1024]{1,0:T(8,128)(2,1)}, u32[]{:S(2)}) copy-start(bf16[256,1024]{1,0:T(8,128)(2,1)} %w_in.1) | copy-start | bytes 1572868
  0.7 9.9 %collective-permute-start.2 = (bf16[128,1024]{1,0:T(8,128)(2,1)}, bf16[128,1024]{1,0:T(8,128)(2,1)S(1)}, u32[]{:S(2)}, u32[]{:S(2)}) collective-permute-start(bf16[128,1024]{1,0:T(8,128)(2,1)} %bitcast.5), channel_id=1, source_target_pairs={{0,2},{1,3},{2,0},{3,1},{4,6},{5,7},{6,4},{7,5},{8,10},{9,11},{10,... | collective-permute-start | bytes 786440 | tf_op jit(solution)/shard_map/ppermute | solution.py:40
  3.7 10.0 %collective-permute-start.4 = (bf16[128,1024]{1,0:T(8,128)(2,1)}, bf16[128,1024]{1,0:T(8,128)(2,1)S(1)}, u32[]{:S(2)}, u32[]{:S(2)}) collective-permute-start(bf16[128,1024]{1,0:T(8,128)(2,1)} %bitcast.6), channel_id=1, source_target_pairs={{0,4},{1,5},{2,6},{3,7},{4,0},{5,1},{6,2},{7,3},{8,12},{9,13},{10,... | collective-permute-start | bytes 786440 | tf_op jit(solution)/shard_map/ppermute | solution.py:40
  5.3 5.2 %copy-start.1 = (bf16[1,2,64,1024]{3,2,1,0:T(8,128)(2,1)S(1)}, bf16[1,2,64,1024]{3,2,1,0:T(8,128)(2,1)}, u32[]{:S(2)}) copy-start(bf16[1,2,64,1024]{3,2,1,0:T(8,128)(2,1)} %param.5) | copy-start | bytes 786436
  5.9 14.1 %collective-permute-start = (bf16[2,128,1024]{2,1,0:T(8,128)(2,1)S(1)}, bf16[2,128,1024]{2,1,0:T(8,128)(2,1)S(1)}, u32[]{:S(2)}, u32[]{:S(2)}) collective-permute-start(bf16[2,128,1024]{2,1,0:T(8,128)(2,1)S(1)} %shard_map.68.local), channel_id=1, source_target_pairs={{2,8},{0,16},{4,24},{8,2},{14,18},{10,26},{20,4},{16,12},{22,28},{... | collective-permute-start | bytes 1572872 | tf_op jit(solution)/shard_map/ppermute | solution.py:89
  10.5 3.4 %collective-permute-start.1 = (bf16[128,1024]{1,0:T(8,128)(2,1)S(1)}, bf16[128,1024]{1,0:T(8,128)(2,1)S(1)}, u32[]{:S(2)}, u32[]{:S(2)}) collective-permute-start(bf16[128,1024]{1,0:T(8,128)(2,1)S(1)} %bitcast.7), channel_id=1, source_target_pairs={{0,1},{1,0},{2,3},{3,2},{4,5},{5,4},{6,7},{7,6},{8,9},{9,8},{10,11... | collective-permute-start | bytes 786440 | tf_op jit(solution)/shard_map/ppermute | solution.py:40
  10.6 8.6 %collective-permute-start.6 = (bf16[64,1024]{1,0:T(8,128)(2,1)S(1)}, bf16[64,1024]{1,0:T(8,128)(2,1)S(1)}, u32[]{:S(2)}, u32[]{:S(2)}) collective-permute-start(bf16[64,1024]{1,0:T(8,128)(2,1)S(1)} %slice.8), channel_id=1, source_target_pairs={{0,4},{1,5},{2,6},{3,7},{4,0},{5,1},{6,2},{7,3},{8,12},{9,13},{10,... | collective-permute-start | bytes 393224 | tf_op jit(solution)/shard_map/ppermute | solution.py:40
  13.7 5.5 %collective-permute-start.8 = (bf16[64,1024]{1,0:T(8,128)(2,1)S(1)}, bf16[64,1024]{1,0:T(8,128)(2,1)S(1)}, u32[]{:S(2)}, u32[]{:S(2)}) collective-permute-start(bf16[64,1024]{1,0:T(8,128)(2,1)S(1)} %slice.9), channel_id=1, source_target_pairs={{0,2},{1,3},{2,0},{3,1},{4,6},{5,7},{6,4},{7,5},{8,10},{9,11},{10,... | collective-permute-start | bytes 393224 | tf_op jit(solution)/shard_map/ppermute | solution.py:40
  13.7 6.9 %collective-permute-start.3 = (bf16[128,1024]{1,0:T(8,128)(2,1)S(1)}, bf16[128,1024]{1,0:T(8,128)(2,1)S(1)}, u32[]{:S(2)}, u32[]{:S(2)}) collective-permute-start(bf16[128,1024]{1,0:T(8,128)(2,1)S(1)} %collective-permute-done.2.refs_2_), channel_id=1, source_target_pairs={{0,1},{1,0},{2,3},{3,2},{4,5},{5,4},{6,7},{7,6},{8,9},{9,8},{10,11... | collective-permute-start | bytes 786440 | tf_op jit(solution)/shard_map/ppermute | solution.py:40
  13.8 6.8 %collective-permute-start.5 = (bf16[128,1024]{1,0:T(8,128)(2,1)S(1)}, bf16[128,1024]{1,0:T(8,128)(2,1)S(1)}, u32[]{:S(2)}, u32[]{:S(2)}) collective-permute-start(bf16[128,1024]{1,0:T(8,128)(2,1)S(1)} %collective-permute-done.4.refs_4_), channel_id=1, source_target_pairs={{0,1},{1,0},{2,3},{3,2},{4,5},{5,4},{6,7},{7,6},{8,9},{9,8},{10,11... | collective-permute-start | bytes 786440 | tf_op jit(solution)/shard_map/ppermute | solution.py:40
  19.1 1.3 %collective-permute-start.7 = (bf16[64,1024]{1,0:T(8,128)(2,1)S(1)}, bf16[64,1024]{1,0:T(8,128)(2,1)S(1)}, u32[]{:S(2)}, u32[]{:S(2)}) collective-permute-start(bf16[64,1024]{1,0:T(8,128)(2,1)S(1)} %collective-permute-done.6.refs_6_), channel_id=1, source_target_pairs={{0,1},{1,0},{2,3},{3,2},{4,5},{5,4},{6,7},{7,6},{8,9},{9,8},{10,11... | collective-permute-start | bytes 393224 | tf_op jit(solution)/shard_map/ppermute | solution.py:40
  19.2 1.5 %collective-permute-start.9 = (bf16[64,1024]{1,0:T(8,128)(2,1)S(1)}, bf16[64,1024]{1,0:T(8,128)(2,1)S(1)}, u32[]{:S(2)}, u32[]{:S(2)}) collective-permute-start(bf16[64,1024]{1,0:T(8,128)(2,1)S(1)} %collective-permute-done.8.refs_8_), channel_id=1, source_target_pairs={{0,1},{1,0},{2,3},{3,2},{4,5},{5,4},{6,7},{7,6},{8,9},{9,8},{10,11... | collective-permute-start | bytes 393224 | tf_op jit(solution)/shard_map/ppermute | solution.py:40
  21.9 9.8 %copy-start.4 = (bf16[1,16,64,128]{3,2,1,0:T(8,128)(2,1)S(1)}, bf16[1,16,64,128]{3,2,1,0:T(8,128)(2,1)}, u32[]{:S(2)}) copy-start(bf16[1,16,64,128]{3,2,1,0:T(8,128)(2,1)} %param.6) | copy-start | bytes 786436
  22.0 9.8 %collective-permute-start.10 = (bf16[1024,128]{1,0:T(8,128)(2,1)S(1)}, bf16[1024,128]{1,0:T(8,128)(2,1)S(1)}, u32[]{:S(2)}, u32[]{:S(2)}) collective-permute-start(bf16[1024,128]{1,0:T(8,128)(2,1)S(1)} %shard_map.69.refs_0_.mid), channel_id=1, source_target_pairs={{0,8},{8,0},{16,24},{24,16},{1,9},{9,1},{17,25},{25,17},{2,10},{10... | collective-permute-start | bytes 786440 | tf_op jit(solution)/shard_map/ppermute | solution.py:40
  26.1 8.6 %collective-permute-start.11 = (bf16[1024,128]{1,0:T(8,128)(2,1)S(1)}, bf16[1024,128]{1,0:T(8,128)(2,1)S(1)}, u32[]{:S(2)}, u32[]{:S(2)}) collective-permute-start(bf16[1024,128]{1,0:T(8,128)(2,1)S(1)} %shard_map.69.refs_0_.mid), channel_id=1, source_target_pairs={{8,16},{16,8},{9,17},{17,9},{10,18},{18,10},{11,19},{19,11},{12,20... | collective-permute-start | bytes 786440 | tf_op jit(solution)/shard_map/ppermute | solution.py:235
  27.4 10.7 %collective-permute-start.12 = (bf16[256,512]{1,0:T(8,128)(2,1)S(1)}, bf16[256,512]{1,0:T(8,128)(2,1)S(1)}, u32[]{:S(2)}, u32[]{:S(2)}) collective-permute-start(bf16[256,512]{1,0:T(8,128)(2,1)S(1)} %shard_map.74.refs_4_), channel_id=1, source_target_pairs={{0,2},{1,3},{2,0},{3,1},{4,6},{5,7},{6,4},{7,5},{8,10},{9,11},{10,... | collective-permute-start | bytes 786440 | tf_op jit(solution)/shard_map/ppermute | solution.py:40
  27.5 12.8 %collective-permute-start.13 = (bf16[256,512]{1,0:T(8,128)(2,1)S(1)}, bf16[256,512]{1,0:T(8,128)(2,1)S(1)}, u32[]{:S(2)}, u32[]{:S(2)}) collective-permute-start(bf16[256,512]{1,0:T(8,128)(2,1)S(1)} %shard_map.74.refs_4_), channel_id=1, source_target_pairs={{0,4},{1,5},{2,6},{3,7},{4,0},{5,1},{6,2},{7,3},{8,12},{9,13},{10,... | collective-permute-start | bytes 786440 | tf_op jit(solution)/shard_map/ppermute | solution.py:40
  31.8 2.8 %copy-start.3 = (bf16[27,32,128]{2,1,0:T(8,128)(2,1)S(1)}, bf16[27,32,128]{2,1,0:T(8,128)(2,1)}, u32[]{:S(2)}) copy-start(bf16[27,32,128]{2,1,0:T(8,128)(2,1)} %kernel) | copy-start | bytes 663556
  32.8 7.7 %collective-permute-start.14 = (bf16[2,9,32,128]{3,2,1,0:T(8,128)(2,1)S(1)}, bf16[2,9,32,128]{3,2,1,0:T(8,128)(2,1)S(1)}, u32[]{:S(2)}, u32[]{:S(2)}) collective-permute-start(bf16[2,9,32,128]{3,2,1,0:T(8,128)(2,1)S(1)} %shard_map.70.early), channel_id=1, source_target_pairs={{0,8},{8,0},{16,24},{24,16},{1,9},{9,1},{17,25},{25,17},{2,10},{10... | collective-permute-start | bytes 442376 | tf_op jit(solution)/shard_map/ppermute | solution.py:40
  35.4 5.0 %collective-permute-start.15 = (bf16[1,9,32,128]{3,2,1,0:T(8,128)(2,1)S(1)}, bf16[1,9,32,128]{3,2,1,0:T(8,128)(2,1)S(1)}, u32[]{:S(2)}, u32[]{:S(2)}) collective-permute-start(bf16[1,9,32,128]{3,2,1,0:T(8,128)(2,1)S(1)} %shard_map.72.late), channel_id=1, source_target_pairs={{0,8},{8,0},{16,24},{24,16},{1,9},{9,1},{17,25},{25,17},{2,10},{10... | collective-permute-start | bytes 221192 | tf_op jit(solution)/shard_map/ppermute | solution.py:40
  38.1 13.5 %collective-permute-start.19 = (bf16[256,512]{1,0:T(8,128)(2,1)S(1)}, bf16[256,512]{1,0:T(8,128)(2,1)S(1)}, u32[]{:S(2)}, u32[]{:S(2)}) collective-permute-start(bf16[256,512]{1,0:T(8,128)(2,1)S(1)} %collective-permute-done.12.refs_5_), channel_id=1, source_target_pairs={{0,4},{1,5},{2,6},{3,7},{4,0},{5,1},{6,2},{7,3},{8,12},{9,13},{10,... | collective-permute-start | bytes 786440 | tf_op jit(solution)/shard_map/ppermute | solution.py:40
  41.1 12.6 %collective-permute-start.21 = (bf16[3,9,32,128]{3,2,1,0:T(8,128)(2,1)S(1)}, bf16[3,9,32,128]{3,2,1,0:T(8,128)(2,1)S(1)}, u32[]{:S(2)}, u32[]{:S(2)}) collective-permute-start(bf16[3,9,32,128]{3,2,1,0:T(8,128)(2,1)S(1)} %shard_map.75.own), channel_id=1, source_target_pairs={{0,16},{8,24},{16,0},{24,8},{1,17},{9,25},{17,1},{25,9},{2,18},{10... | collective-permute-start | bytes 663560 | tf_op jit(solution)/shard_map/ppermute | solution.py:40
  44.3 4.3 %collective-permute-start.16 = (bf16[256,128]{1,0:T(8,128)(2,1)S(1)}, bf16[256,128]{1,0:T(8,128)(2,1)S(1)}, u32[]{:S(2)}, u32[]{:S(2)}) collective-permute-start(bf16[256,128]{1,0:T(8,128)(2,1)S(1)} %get-tuple-element.18), channel_id=1, source_target_pairs={{0,2},{1,3},{2,0},{3,1},{4,6},{5,7},{6,4},{7,5},{8,10},{9,11},{10,... | collective-permute-start | bytes 196616 | tf_op jit(solution)/shard_map/ppermute | solution.py:40
  44.9 4.5 %collective-permute-start.17 = (bf16[256,128]{1,0:T(8,128)(2,1)S(1)}, bf16[256,128]{1,0:T(8,128)(2,1)S(1)}, u32[]{:S(2)}, u32[]{:S(2)}) collective-permute-start(bf16[256,128]{1,0:T(8,128)(2,1)S(1)} %get-tuple-element.19), channel_id=1, source_target_pairs={{0,4},{1,5},{2,6},{3,7},{4,0},{5,1},{6,2},{7,3},{8,12},{9,13},{10,... | collective-permute-start | bytes 196616 | tf_op jit(solution)/shard_map/ppermute | solution.py:40
  46.4 5.2 %collective-permute-start.18 = (bf16[256,128]{1,0:T(8,128)(2,1)S(1)}, bf16[256,128]{1,0:T(8,128)(2,1)S(1)}, u32[]{:S(2)}, u32[]{:S(2)}) collective-permute-start(bf16[256,128]{1,0:T(8,128)(2,1)S(1)} %get-tuple-element.20), channel_id=1, source_target_pairs={{0,6},{1,7},{2,4},{3,5},{4,2},{5,3},{6,0},{7,1},{8,14},{9,15},{10,... | collective-permute-start | bytes 196616 | tf_op jit(solution)/shard_map/ppermute | solution.py:40
  52.6 1.9 %collective-permute-start.20 = (bf16[128,1024]{1,0:T(8,128)(2,1)S(1)}, bf16[128,1024]{1,0:T(8,128)(2,1)S(1)}, u32[]{:S(2)}, u32[]{:S(2)}) collective-permute-start(bf16[128,1024]{1,0:T(8,128)(2,1)S(1)} %get-tuple-element.22), channel_id=1, source_target_pairs={{0,1},{1,0},{2,3},{3,2},{4,5},{5,4},{6,7},{7,6},{8,9},{9,8},{10,11... | collective-permute-start | bytes 786440 | tf_op jit(solution)/shard_map/ppermute | solution.py:40
